TPU v7x, 256 devices: a whole 4x4x8 slice. The times are simulated.
256 devices in a mesh: rows: 8 (over z), chan: 32 (over y, x, core).
Axes of the slice: x: 4, y: 4, z: 8, core: 2. Of those that a mesh axis runs over, the one named last changes fastest.
Arguments:
- features: float32 [256, 96, 256], P('chan', 'rows'), may hold values from -6 to 6
- weight_in: float32 [256, 3, 3, 256], P('chan'), may hold values from -0.125 to 0.125
- weight_out: float32 [256, 3, 3, 128], replicated, may hold values from -0.125 to 0.125
- cotangent: float32 [192, 512, 128], P('rows', 'chan'), may hold values from -6 to 6
Outputs:
- grad_features: float32 [256, 96, 256], P('chan', 'rows')
- grad_weight_in: float32 [256, 3, 3, 256], P('chan')
- grad_weight_out: float32 [256, 3, 3, 128], P('chan')
All inputs are finite; a program needn't handle non-finite values.
Results may differ from a plain program's by a relative error of at most 0.00023.
Values sent between devices are 32-bit elements; how exact they have to be, the bound alone decides.
No kernel may reach another device: no remote copies, remote signals or barrier semaphores. Data moves between devices by JAX's collectives and lax.ppermute only.
A program may use at most 64 MiB of HBM per device.

v0:
```python
import jax
import jax.numpy as jnp
from jax import lax
from jax.experimental import pallas as pl
from jax.experimental.pallas import tpu as pltpu
from jax.sharding import PartitionSpec as P

BLOCK = 16
STEP = BLOCK + 2
ROWS = 24
FLAT = 512
PACK = 72
BACK = 88
F32, BF16 = jnp.float32, jnp.bfloat16
ANYWHERE = pltpu.CompilerParams(vmem_limit_bytes=40 * 1024 * 1024)
FULL = pl.BlockSpec(memory_space=pltpu.VMEM)
SCALAR = pl.BlockSpec(memory_space=pltpu.SMEM)


def halves(x):
    high = x.astype(BF16)
    return high, (x - high.astype(F32)).astype(BF16)


def product(a, b, dims):
    def one(x, y):
        return lax.dot_general(x, y, (dims, ((), ())), preferred_element_type=F32)

    return one(a[0], b[0]) + (one(a[0], b[1]) + one(a[1], b[0]))


NN, NT, TN = ((1,), (0,)), ((1,), (1,)), ((0,), (0,))


def pack_kernel(where, own, other, near, far, kernels, out, image, line):
    parity = where[0]
    image[...] = jnp.zeros_like(image)
    line[...] = jnp.zeros_like(line)
    inner = slice(128, 384)
    half = ROWS // 2
    for i in range(half):
        image[1 + half * parity + i, :, inner] = own[i]
        image[1 + half * (1 - parity) + i, :, inner] = other[i]
    image[(ROWS + 1) * parity, :, inner] = near[...]
    image[(ROWS + 1) * (1 - parity), :, inner] = far[...]
    for block in range(16):
        start = 127 + BLOCK * block
        for r in range(ROWS + 2):
            line[:, r * STEP : (r + 1) * STEP] = image[r, :, start : start + STEP]
        for q in range(4):
            tile = line[:, q * 128 : (q + 1) * 128]
            out[2 * block, q * 8 : q * 8 + 8, :] = tile
            out[2 * block + 1, q * 8 : q * 8 + 8, :] = tile
    for core in range(2):
        part = kernels[core]
        for block in range(16):
            out[2 * block + core, 32:PACK, :] = part


def window_kernel(where, own, other, near, far, weight, s_high, s_low, grad, image, sums):
    core = where[1]
    image[:, pl.ds(pl.multiple_of(8 + 16 * core, 8), 16), :] = own[...]
    image[:, pl.ds(pl.multiple_of(24 - 16 * core, 8), 16), :] = other[...]
    left = jnp.where(core == 0, near[...], far[...])
    right = jnp.where(core == 0, far[...], near[...])
    for r in range(2 * ROWS + 2):
        image[r, 7:8, :] = left[r : r + 1]
        image[r, 40:41, :] = right[r : r + 1]
    sums[...] = jnp.zeros_like(sums)

    def cells(r, start, count):
        return image[r, pl.ds(start, count, stride=2), :]

    def pairs(r, start, count):
        return cells(r, start, count) + cells(r, start + 1, count)

    even = [pairs(r, 7, 17) for r in range(2 * ROWS + 2)]
    odd = [pairs(r, 8, 16) for r in range(2 * ROWS + 2)]
    for r in range(ROWS + 1):
        at = r * STEP
        sums[at : at + 17, 0:128] = even[2 * r] + even[2 * r + 1]
        sums[at : at + 16, 128:256] = odd[2 * r] + odd[2 * r + 1]
        if r < ROWS:
            sums[at : at + 17, 256:384] = even[2 * r + 1] + even[2 * r + 2]
            sums[at : at + 16, 384:512] = odd[2 * r + 1] + odd[2 * r + 2]
    high, low = halves(sums[...])
    s_high[...] = high
    s_low[...] = low
    total = None
    for kind in range(4):
        lanes = slice(kind * 128, (kind + 1) * 128)
        taps = [t for t in range(9) if kind_of(t) == kind]
        left_side = jnp.concatenate([weight[t * 64 : (t + 1) * 64, :] for t in taps], axis=0)
        each = product(halves(left_side), (high[:, lanes], low[:, lanes]), NT)
        for i, t in enumerate(taps):
            term = each[i * 64 : (i + 1) * 64]
            if shift_of(t):
                term = pltpu.roll(term, FLAT - shift_of(t), 1)
            total = term if total is None else total + term
    grad[...] = total


def kind_of(t):
    return 2 * (t // 3 == 1) + (t % 3 == 1)


def shift_of(t):
    return STEP * (t // 3 == 0) + (t % 3 == 0)


def main_kernel(recv, s_high, s_low, grad, keep, out, x_high, x_low, w_high, w_low, g_high, g_low):
    for pair in range(16):
        for q in range(4):
            tile = jnp.concatenate(
                [recv[pl.ds((2 * pair + i) * PACK + q * 8, 8), :] for i in range(2)], axis=0
            )
            high, low = halves(tile)
            x_high[pair * 16 : pair * 16 + 16, q * 128 : q * 128 + 128] = high
            x_low[pair * 16 : pair * 16 + 16, q * 128 : q * 128 + 128] = low
    for t in range(9):
        for h in range(2):
            tile = jnp.concatenate(
                [recv[pl.ds(32 + j * 18 + t * 2 + h, 32, stride=PACK), :] for j in range(2)], axis=0
            )
            high, low = halves(tile)
            w_high[t * 64 : t * 64 + 64, h * 128 : h * 128 + 128] = high
            w_low[t * 64 : t * 64 + 64, h * 128 : h * 128 + 128] = low
    weights = (w_high[...], w_low[...])
    image = (x_high[...], x_low[...])
    each = product(weights, image, NN)
    hidden = each[0:64]
    for t in range(1, 9):
        hidden = hidden + pltpu.roll(each[t * 64 : t * 64 + 64], FLAT - ((t // 3) * STEP + t % 3), 1)
    inside = keep[...] > 0.0
    sigma = 1.0 / (1.0 + jnp.exp(-hidden))
    active = jnp.where(inside, hidden * sigma, 0.0)
    slope = sigma * (1.0 + hidden * (1.0 - sigma))
    gradient = jnp.where(inside, grad[...] * slope, 0.0)
    for t in range(9):
        shift = (t // 3) * STEP + t % 3
        moved = pltpu.roll(gradient, shift, 1) if shift else gradient
        high, low = halves(moved)
        g_high[t * 64 : t * 64 + 64, :] = high
        g_low[t * 64 : t * 64 + 64, :] = low
    moved = (g_high[...], g_low[...])
    into = product(moved, image, NT)
    for t in range(9):
        for h in range(2):
            for j in range(2):
                out[pl.ds(32 + j * 18 + t * 2 + h, 32, stride=BACK), :] = into[
                    t * 64 + j * 32 : t * 64 + j * 32 + 32, h * 128 : h * 128 + 128
                ]
    shifts = [0, 1, STEP, STEP + 1]
    spread = jnp.concatenate([pltpu.roll(active, s, 1) if s else active for s in shifts], axis=0)
    onto = product(halves(spread), (s_high[...], s_low[...]), NN)
    for t in range(9):
        at, kind = shifts.index(shift_of(t)) * 64, kind_of(t)
        for j in range(2):
            out[pl.ds(68 + j * 9 + t, 32, stride=BACK), :] = onto[
                at + j * 32 : at + j * 32 + 32, kind * 128 : kind * 128 + 128
            ]
    back = product(weights, moved, TN)
    for d in range(32):
        for q in range(4):
            out[pl.ds(d * BACK + q * 8, 8), :] = back[d * 8 : d * 8 + 8, q * 128 : q * 128 + 128]
    blank = jnp.zeros((2, 128), F32)
    for d in range(32):
        out[pl.ds(d * BACK + 86, 2), :] = blank


def gather_kernel(scale, where, recv, weights, mine, theirs, image, line):
    parity = where[0]
    for core in range(2):
        total = recv[core, 32:BACK, :]
        for block in range(1, 16):
            total = total + recv[2 * block + core, 32:BACK, :]
        total = total * scale
        for z in range(8):
            weights[z, core * 56 : core * 56 + 56, :] = total
    image[...] = jnp.zeros_like(image)
    for block in range(16):
        start = 127 + BLOCK * block
        for q in range(4):
            at = slice(q * 8, q * 8 + 8)
            line[:, q * 128 : q * 128 + 128] = recv[2 * block, at, :] + recv[2 * block + 1, at, :]
        for r in range(ROWS + 2):
            image[r, :, start : start + STEP] += line[:, r * STEP : (r + 1) * STEP]
    half = ROWS // 2 + 1
    for i in range(half):
        mine[i] = image[half * parity + i, :, 128:384]
        theirs[i] = image[half * (1 - parity) + i, :, 128:384]


def shape(*dims, dtype=F32):
    return jax.ShapeDtypeStruct(dims, dtype)


def call(kernel, outs, scalars, args, scratch, flops, moved):
    return pl.pallas_call(
        kernel,
        out_shape=outs,
        in_specs=[SCALAR] * scalars + [FULL] * (args - scalars),
        out_specs=jax.tree.map(lambda _: FULL, outs),
        scratch_shapes=scratch,
        compiler_params=ANYWHERE,
        cost_estimate=pl.CostEstimate(flops=flops, bytes_accessed=moved, transcendentals=0),
    )


def local(features, weight_in, weight_out, cotangent):
    z, d = lax.axis_index("rows"), lax.axis_index("chan")
    parity, core = z % 2, d % 2
    where = jnp.stack([parity, core]).astype(jnp.int32)
    scale = (4.0 * features.shape[1] * lax.axis_size("rows") * features.shape[2]) ** (-0.5)

    def partner(n):
        return [(i, i ^ 1) for i in range(n)]

    def beside(n):
        return [(i, i + 1) for i in range(1, n - 1, 2)] + [(i, i - 1) for i in range(2, n, 2)]

    def beyond(n):
        return [(i, i + 2) for i in range(1, n - 2, 2)] + [(i, i - 2) for i in range(2, n, 2)]

    lines = jnp.transpose(features, (1, 0, 2))
    edge_f = lax.dynamic_index_in_dim(lines, 11 * parity, 0, False)
    edge_c = lax.dynamic_index_in_dim(cotangent, 23 * parity, 0, False)
    edge = jnp.concatenate([edge_f[:, :128], edge_f[:, 128:], edge_c], axis=0)
    near = lax.ppermute(edge, "rows", beside(8))
    far = lax.ppermute(edge, "rows", beyond(8))
    other = lax.ppermute(lines, "rows", partner(8))
    near_f = jnp.concatenate([near[:8], near[8:16]], axis=1)
    far_f = jnp.concatenate([far[:8], far[8:16]], axis=1)
    mine = lax.dynamic_slice_in_dim(weight_in, 4 * parity, 4, 0).reshape(2, 36, 128)
    mine = jnp.pad(mine, ((0, 0), (0, PACK - 68), (0, 0)))
    packed = call(
        pack_kernel, shape(32, PACK, 128), 1, 6,
        [pltpu.VMEM((ROWS + 2, 8, 512), F32), pltpu.VMEM((8, FLAT), F32)], 10**6, 10**6,
    )(where, lines, other, near_f, far_f, mine)
    recv = lax.all_to_all(packed, "chan", 0, 0, tiled=True)

    other_c = lax.ppermute(cotangent, "rows", partner(8))
    flip = parity == 1
    tall = jnp.concatenate(
        [
            jnp.where(flip, far[16:], near[16:])[None],
            jnp.where(flip, other_c, cotangent),
            jnp.where(flip, cotangent, other_c),
            jnp.where(flip, near[16:], far[16:])[None],
        ],
        axis=0,
    )
    side = lax.ppermute(lax.dynamic_index_in_dim(tall, 15 * core, 1, False), "chan", beside(32))
    other_tall = lax.ppermute(tall, "chan", partner(32))
    other_side = lax.ppermute(side, "chan", partner(32))
    group = lax.dynamic_index_in_dim(weight_out.reshape(32, 4, 2, 9, 128), 2 * parity + core, 1, False)
    group = jnp.transpose(group, (2, 1, 0, 3)).reshape(576, 128)
    s_high, s_low, grad = call(
        window_kernel,
        (shape(FLAT, 512, dtype=BF16), shape(FLAT, 512, dtype=BF16), shape(64, FLAT)), 1, 6,
        [pltpu.VMEM((2 * ROWS + 2, 48, 128), F32), pltpu.VMEM((FLAT, 512), F32)],
        3 * 10**8, 3 * 10**6,
    )(where, tall, other_tall, side, other_side, group)

    at = lax.broadcasted_iota(jnp.int32, (64, FLAT), 1)
    keep = jnp.where((at % STEP < BLOCK) & (at < ROWS * STEP), 1.0, 0.0).astype(F32)
    sent = call(
        main_kernel, shape(32 * BACK, 128), 0, 5,
        [
            pltpu.VMEM((256, FLAT), BF16), pltpu.VMEM((256, FLAT), BF16),
            pltpu.VMEM((576, 256), BF16), pltpu.VMEM((576, 256), BF16),
            pltpu.VMEM((576, FLAT), BF16), pltpu.VMEM((576, FLAT), BF16),
        ],
        10**9, 5 * 10**6,
    )(recv.reshape(32 * PACK, 128), s_high, s_low, grad, keep)
    back = lax.all_to_all(sent.reshape(32, BACK, 128), "chan", 0, 0, tiled=True)

    sums, own, given = call(
        lambda *refs: gather_kernel(scale, *refs),
        (shape(8, 112, 128), shape(13, 8, 256), shape(13, 8, 256)), 1, 2,
        [pltpu.VMEM((ROWS + 2, 8, 512), F32), pltpu.VMEM((8, FLAT), F32)], 10**6, 2 * 10**6,
    )(where, back)
    own = own + lax.ppermute(given, "rows", partner(8))
    outer = lax.ppermute(
        lax.dynamic_index_in_dim(own, 12 * parity, 0, False), "rows", beside(8)
    )
    rows = lax.dynamic_slice_in_dim(own, 1 - parity, 12, 0)
    place = (jnp.arange(12) == 11 * parity)[:, None, None]
    rows = rows + jnp.where(place, outer[None], 0.0)
    grad_image = jnp.transpose(rows, (1, 0, 2))
    sums = lax.all_to_all(sums, "rows", 0, 0, tiled=True)
    sums = sums.reshape(4, 2, 2, 56, 128).sum(axis=0)
    grad_in = sums[:, :, :36].reshape(8, 3, 3, 256)
    grad_out = sums[:, :, 36:54].reshape(8, 3, 3, 128)
    return (grad_image, grad_in, grad_out)


def solution(mesh):
    return jax.shard_map(
        local,
        mesh=mesh,
        in_specs=(
            P("chan", "rows", None),
            P("chan", None, None, None),
            P(),
            P("rows", "chan", None),
        ),
        out_specs=(
            P("chan", "rows", None),
            P("chan", None, None, None),
            P("chan", None, None, None),
        ),
        check_vma=False,
    )
```

profile of v0, /device:TPU:96, one launch (start us, length us, event | category | flops | bytes accessed | tf_op | source)
XLA Modules:
  0.0 112.9 jit_solution(3354661978197005710)
XLA Ops:
  0.7 0.8 dynamic-slice_bitcast_fusion.2
  1.5 0.7 dynamic-slice_bitcast_fusion.1
  2.2 5.0 %collective-permute-start.1 = (f32[32,128]{1,0:T(8,128)S(1)}, f32[32,128]{1,0:T(8,128)S(1)}, u32[]{:S(2)}, u32[]{:S(2)}) collective-permute-start(f32[32,128]{1,0:T(8,128)S(1)} %pad_maximum_fusion.1), channel_id=1, source_target_pairs={{32,64},{96,128},{160,192},{64,32},{128,96},{192,160},{33,65},{97,... | collective-permute-start | bytes 49160 | tf_op jit(solution)/shard_map/ppermute | solution.py:229
  7.2 3.4 %collective-permute-start.2 = (f32[32,128]{1,0:T(8,128)S(1)}, f32[32,128]{1,0:T(8,128)S(1)}, u32[]{:S(2)}, u32[]{:S(2)}) collective-permute-start(f32[32,128]{1,0:T(8,128)S(1)} %pad_maximum_fusion.1), channel_id=1, source_target_pairs={{32,96},{96,160},{160,224},{64,0},{128,64},{192,128},{33,97},{97,1... | collective-permute-start | bytes 49160 | tf_op jit(solution)/shard_map/ppermute | solution.py:230
  10.7 2.0 %collective-permute-start = (f32[12,8,256]{2,1,0:T(8,128)}, f32[12,8,256]{2,1,0:T(8,128)S(1)}, u32[]{:S(2)}, u32[]{:S(2)}) collective-permute-start(f32[12,8,256]{2,1,0:T(8,128)} %bitcast.31), channel_id=1, source_target_pairs={{0,32},{32,0},{64,96},{96,64},{128,160},{160,128},{192,224},{224,1... | collective-permute-start | bytes 294920 | tf_op jit(solution)/shard_map/ppermute | solution.py:231
  12.7 0.9 constant_dynamic-slice_fusion.2
  13.9 5.4 %collective-permute-done.other = f32[12,8,256]{2,1,0:T(8,128)S(1)} collective-permute-done((f32[12,8,256]{2,1,0:T(8,128)}, f32[12,8,256]{2,1,0:T(8,128)S(1)}, u32[]{:S(2)}, u32[]{:S(2)}) %collective-permute-start) | collective-permute-done | bytes 98336 | tf_op jit(solution)/shard_map/ppermute | solution.py:231
  19.3 0.9 copy-done.5
  20.1 2.3 %shard_map.67 = f32[32,72,128]{2,1,0:T(8,128)} custom-call(s32[2]{0:T(128)S(1)} %pad_add_fusion.where.refs_0_, f32[12,8,256]{2,1,0:T(8,128)S(1)} %bitcast.32, f32[12,8,256]{2,1,0:T(8,128)S(1)} %collective-permute-done.other, f32[8,256]{1,0:T(8,128)S(1)} %get-tuple-element.28.near, f32[8,256]{1,0:T(8,128)S(1)} %get-tuple-element.29.far, ...), custom_call_target="tpu_custom_call" | custom-call | flops 1000000 | bytes 1000000 | tf_op jit(solution)/shard_map/pallas_call | solution.py:236
  22.5 7.5 %all-to-all-start = ((f32[32,72,128]{2,1,0:T(8,128)}), f32[32,72,128]{2,1,0:T(8,128)S(1)}, u32[]{:S(2)}, u32[]{:S(2)}) async-start(f32[32,72,128]{2,1,0:T(8,128)} %shard_map.67), calls=%async_computation | async-start | bytes 2359296 | tf_op jit(solution)/shard_map/all_to_all | solution.py:240
  30.1 0.4 collective-permute-start.4
  30.4 0.7 collective-permute-start.5
  31.2 14.7 %collective-permute-start.6 = (f32[50,128]{1,0:T(8,128)S(1)}, f32[50,128]{1,0:T(8,128)S(1)}, u32[]{:S(2)}, u32[]{:S(2)}) collective-permute-start(f32[50,128]{1,0:T(8,128)S(1)} %collective-permute-done.5.near), channel_id=1, source_target_pairs={{0,1},{1,0},{2,3},{3,2},{4,5},{5,4},{6,7},{7,6},{8,9},{9,8},{10,11... | collective-permute-start | bytes 76808 | tf_op jit(solution)/shard_map/ppermute | solution.py:255
  46.0 0.7 collective-permute-done.6.far
  46.7 0.8 copy-done.3
  47.5 1.0 copy-done.4
  48.5 0.7 copy-done.7
  49.2 0.7 copy-done.9
  49.9 1.5 %shard_map.68 = (bf16[512,512]{1,0:T(8,128)(2,1)S(1)}, bf16[512,512]{1,0:T(8,128)(2,1)S(1)}, f32[64,512]{1,0:T(8,128)S(1)}) custom-call(s32[2]{0:T(128)S(1)} %copy-done.9, f32[50,16,128]{2,1,0:T(8,128)S(1)} %pad_maximum_fusion.own, f32[50,16,128]{2,1,0:T(8,128)S(1)} %copy-done.4, f32[50,128]{1,0:T(8,128)S(1)} %copy-done.7, ...), custom_call_target="tpu_custom_call" | custom-call | flops 300000000 | bytes 3000000 | tf_op jit(solution)/shard_map/pallas_call | solution.py:258
  51.4 0.8 copy-done.1
  52.2 1.0 copy-done.2
  53.2 2.7 %shard_map.69 = f32[2816,128]{1,0:T(8,128)S(1)} custom-call(f32[2304,128]{1,0:T(8,128)S(1)} %bitcast.29, bf16[512,512]{1,0:T(8,128)(2,1)S(1)} %get-tuple-element.9.s_high, bf16[512,512]{1,0:T(8,128)(2,1)S(1)} %copy-done.2, f32[64,512]{1,0:T(8,128)S(1)} %get-tuple-element.11.grad, f32[64,512]{1,0:T(8,128)S(1)} %fusion.1.keep), custom_call_target="tpu_custom_call" | custom-call | flops 1000000000 | bytes 5000000 | tf_op jit(solution)/shard_map/pallas_call | solution.py:267
  56.0 27.8 %all_to_all.15.refs_1_ = f32[32,88,128]{2,1,0:T(8,128)S(1)} all-to-all(f32[32,88,128]{2,1,0:T(8,128)S(1)} %bitcast.28), channel_id=1, replica_groups=mesh['rows'=8,'chan'=32] {'chan'}, dimensions={0} | all-to-all | bytes 2883584 | tf_op jit(solution)/shard_map/all_to_all | solution.py:276
  83.8 1.9 %shard_map.70 = (f32[8,112,128]{2,1,0:T(8,128)}, f32[13,8,256]{2,1,0:T(8,128)S(1)}, f32[13,8,256]{2,1,0:T(8,128)S(1)}) custom-call(s32[2]{0:T(128)S(1)} %copy-done.10, f32[32,88,128]{2,1,0:T(8,128)S(1)} %all_to_all.15.refs_1_), custom_call_target="tpu_custom_call" | custom-call | flops 1000000 | bytes 2000000 | tf_op jit(solution)/shard_map/pallas_call | solution.py:278
  85.8 5.1 %all-to-all-start.2 = ((f32[8,112,128]{2,1,0:T(8,128)}), f32[8,112,128]{2,1,0:T(8,128)S(1)}, u32[]{:S(2)}, u32[]{:S(2)}) async-start(f32[8,112,128]{2,1,0:T(8,128)} %get-tuple-element.14), calls=%async_computation.2 | async-start | bytes 917504 | tf_op jit(solution)/shard_map/all_to_all | solution.py:291
  90.9 0.6 collective-permute-start.7
  91.4 12.5 %collective-permute-done.7 = f32[13,8,256]{2,1,0:T(8,128)S(1)} collective-permute-done((f32[13,8,256]{2,1,0:T(8,128)S(1)}, f32[13,8,256]{2,1,0:T(8,128)S(1)}, u32[]{:S(2)}, u32[]{:S(2)}) %collective-permute-start.7) | collective-permute-done | bytes 106528 | tf_op jit(solution)/shard_map/ppermute | solution.py:283
  104.0 4.9 %collective-permute-start.8 = (f32[8,256]{1,0:T(8,128)S(1)}, f32[8,256]{1,0:T(8,128)S(1)}, u32[]{:S(2)}, u32[]{:S(2)}) collective-permute-start(f32[8,256]{1,0:T(8,128)S(1)} %dynamic-slice_bitcast_fusion), channel_id=1, source_target_pairs={{32,64},{96,128},{160,192},{64,32},{128,96},{192,160},{33,65},{97,... | collective-permute-start | bytes 24584 | tf_op jit(solution)/shard_map/ppermute | solution.py:284
  108.9 1.9 %collective-permute-done.8 = f32[8,256]{1,0:T(8,128)S(1)} collective-permute-done((f32[8,256]{1,0:T(8,128)S(1)}, f32[8,256]{1,0:T(8,128)S(1)}, u32[]{:S(2)}, u32[]{:S(2)}) %collective-permute-start.8) | collective-permute-done | bytes 8224 | tf_op jit(solution)/shard_map/ppermute | solution.py:284
  110.7 0.7 add_bitcast_fusion
  111.6 0.6 copy.11
  112.2 0.6 copy.12
  (52 shorter events, 0.8 us)
Async XLA Ops:
  0.6 45.2 %copy-start = (f32[256,3,3,128]{3,0,2,1:T(8,128)S(1)}, f32[256,3,3,128]{3,0,2,1:T(8,128)}, u32[]{:S(2)}) copy-start(f32[256,3,3,128]{3,0,2,1:T(8,128)} %param.6) | copy-start | bytes 3538948
  2.2 11.7 %collective-permute-start.1 = (f32[32,128]{1,0:T(8,128)S(1)}, f32[32,128]{1,0:T(8,128)S(1)}, u32[]{:S(2)}, u32[]{:S(2)}) collective-permute-start(f32[32,128]{1,0:T(8,128)S(1)} %pad_maximum_fusion.1), channel_id=1, source_target_pairs={{32,64},{96,128},{160,192},{64,32},{128,96},{192,160},{33,65},{97,... | collective-permute-start | bytes 49160 | tf_op jit(solution)/shard_map/ppermute | solution.py:229
  7.2 6.6 %collective-permute-start.2 = (f32[32,128]{1,0:T(8,128)S(1)}, f32[32,128]{1,0:T(8,128)S(1)}, u32[]{:S(2)}, u32[]{:S(2)}) collective-permute-start(f32[32,128]{1,0:T(8,128)S(1)} %pad_maximum_fusion.1), channel_id=1, source_target_pairs={{32,96},{96,160},{160,224},{64,0},{128,64},{192,128},{33,97},{97,1... | collective-permute-start | bytes 49160 | tf_op jit(solution)/shard_map/ppermute | solution.py:230
  10.6 19.4 %collective-permute-start.3 = (f32[24,16,128]{2,1,0:T(8,128)}, f32[24,16,128]{2,1,0:T(8,128)S(1)}, u32[]{:S(2)}, u32[]{:S(2)}) collective-permute-start(f32[24,16,128]{2,1,0:T(8,128)} %param.7), channel_id=1, source_target_pairs={{0,32},{32,0},{64,96},{96,64},{128,160},{160,128},{192,224},{224,1... | collective-permute-start | bytes 589832 | tf_op jit(solution)/shard_map/ppermute | solution.py:242
  10.7 8.6 %collective-permute-start = (f32[12,8,256]{2,1,0:T(8,128)}, f32[12,8,256]{2,1,0:T(8,128)S(1)}, u32[]{:S(2)}, u32[]{:S(2)}) collective-permute-start(f32[12,8,256]{2,1,0:T(8,128)} %bitcast.31), channel_id=1, source_target_pairs={{0,32},{32,0},{64,96},{96,64},{128,160},{160,128},{192,224},{224,1... | collective-permute-start | bytes 294920 | tf_op jit(solution)/shard_map/ppermute | solution.py:231
  13.7 8.8 %copy-start.8 = (s32[2]{0:T(128)}, s32[2]{0:T(128)S(1)}, u32[]{:S(2)}) copy-start(s32[2]{0:T(128)S(1)} %pad_add_fusion.where.refs_0_) | copy-start | bytes 28
  19.2 0.9 copy-start.5
  22.5 7.5 %copy-start.11 = (f32[24,16,128]{2,1,0:T(8,128)S(1)}, f32[24,16,128]{2,1,0:T(8,128)}, u32[]{:S(2)}) copy-start(f32[24,16,128]{2,1,0:T(8,128)} %param.7) | copy-start | bytes 589828
  22.5 29.7 %all-to-all-start = ((f32[32,72,128]{2,1,0:T(8,128)}), f32[32,72,128]{2,1,0:T(8,128)S(1)}, u32[]{:S(2)}, u32[]{:S(2)}) async-start(f32[32,72,128]{2,1,0:T(8,128)} %shard_map.67), calls=%async_computation | async-start | bytes 2359296 | tf_op jit(solution)/shard_map/all_to_all | solution.py:240
  30.1 16.7 %collective-permute-start.4 = (f32[50,16,128]{2,1,0:T(8,128)S(1)}, f32[50,16,128]{2,1,0:T(8,128)S(1)}, u32[]{:S(2)}, u32[]{:S(2)}) collective-permute-start(f32[50,16,128]{2,1,0:T(8,128)S(1)} %pad_maximum_fusion.own), channel_id=1, source_target_pairs={{0,1},{1,0},{2,3},{3,2},{4,5},{5,4},{6,7},{7,6},{8,9},{9,8},{10,11... | collective-permute-start | bytes 1228808 | tf_op jit(solution)/shard_map/ppermute | solution.py:254
  30.4 0.7 collective-permute-start.5
  31.2 15.6 %copy-start.6 = (f32[50,128]{1,0:T(8,128)}, f32[50,128]{1,0:T(8,128)S(1)}, u32[]{:S(2)}) copy-start(f32[50,128]{1,0:T(8,128)S(1)} %collective-permute-done.5.near) | copy-start | bytes 76804
  31.2 15.5 %collective-permute-start.6 = (f32[50,128]{1,0:T(8,128)S(1)}, f32[50,128]{1,0:T(8,128)S(1)}, u32[]{:S(2)}, u32[]{:S(2)}) collective-permute-start(f32[50,128]{1,0:T(8,128)S(1)} %collective-permute-done.5.near), channel_id=1, source_target_pairs={{0,1},{1,0},{2,3},{3,2},{4,5},{5,4},{6,7},{7,6},{8,9},{9,8},{10,11... | collective-permute-start | bytes 76808 | tf_op jit(solution)/shard_map/ppermute | solution.py:255
  46.7 0.8 copy-start.3
  47.5 1.0 copy-start.4
  48.5 0.7 copy-start.7
  49.2 0.7 copy-start.9
  51.4 0.8 copy-start.1
  52.2 1.0 copy-start.2
  56.0 27.8 %copy-start.10 = (s32[2]{0:T(128)S(1)}, s32[2]{0:T(128)}, u32[]{:S(2)}) copy-start(s32[2]{0:T(128)} %copy-done.8) | copy-start | bytes 28
  85.8 25.7 %all-to-all-start.2 = ((f32[8,112,128]{2,1,0:T(8,128)}), f32[8,112,128]{2,1,0:T(8,128)S(1)}, u32[]{:S(2)}, u32[]{:S(2)}) async-start(f32[8,112,128]{2,1,0:T(8,128)} %get-tuple-element.14), calls=%async_computation.2 | async-start | bytes 917504 | tf_op jit(solution)/shard_map/all_to_all | solution.py:291
  90.9 13.1 %collective-permute-start.7 = (f32[13,8,256]{2,1,0:T(8,128)S(1)}, f32[13,8,256]{2,1,0:T(8,128)S(1)}, u32[]{:S(2)}, u32[]{:S(2)}) collective-permute-start(f32[13,8,256]{2,1,0:T(8,128)S(1)} %get-tuple-element.13), channel_id=1, source_target_pairs={{0,32},{32,0},{64,96},{96,64},{128,160},{160,128},{192,224},{224,1... | collective-permute-start | bytes 319496 | tf_op jit(solution)/shard_map/ppermute | solution.py:283
  104.0 6.8 %collective-permute-start.8 = (f32[8,256]{1,0:T(8,128)S(1)}, f32[8,256]{1,0:T(8,128)S(1)}, u32[]{:S(2)}, u32[]{:S(2)}) collective-permute-start(f32[8,256]{1,0:T(8,128)S(1)} %dynamic-slice_bitcast_fusion), channel_id=1, source_target_pairs={{32,64},{96,128},{160,192},{64,32},{128,96},{192,160},{33,65},{97,... | collective-permute-start | bytes 24584 | tf_op jit(solution)/shard_map/ppermute | solution.py:284
where the time goes:
time: 114 us; the launch traced here: 113 us
  starting transfers between devices  44.2 us (39%)
  blocking collectives  27.8 us (24%)
  waiting for transfers between devices  20.6 us (18%)
  local copies, waits for them, and re-layouts  9.85 us (9%)
  Pallas kernels  8.48 us (7%)
    all_to_all x1, blocking collectives, local(): back = lax.all_to_all(sent.reshape(32, BACK, 128), 'chan', 0, 0, tiled=True)  27.8 us
    ppermute x1, starting transfers between devices, local(): other_side = lax.ppermute(side, 'chan', partner(32))  14.7 us
    ppermute x1, waiting for transfers between devices, local(): own = own + lax.ppermute(given, 'rows', partner(8))  12.5 us
    all_to_all x1, starting transfers between devices, local(): recv = lax.all_to_all(packed, 'chan', 0, 0, tiled=True)  7.45 us
    unnamed x27, local copies, waits for them, and re-layouts  7.19 us
    ppermute x1, waiting for transfers between devices, local(): other = lax.ppermute(lines, 'rows', partner(8))  5.39 us
    all_to_all x1, starting transfers between devices, local(): sums = lax.all_to_all(sums, 'rows', 0, 0, tiled=True)  5.1 us
    ppermute x1, starting transfers between devices, local(): near = lax.ppermute(edge, 'rows', beside(8))  5.02 us
  transfers between devices with their start and end apart: 11, of which 5 were waited for; matrix products, arithmetic and copies ran while one was open for 2% of the time, Pallas kernels for 3%

commit v1 on v0

v1 whole, which is shorter than its diff:
```python
import jax
import jax.numpy as jnp
from jax import lax
from jax.experimental import pallas as pl
from jax.experimental.pallas import tpu as pltpu
from jax.sharding import PartitionSpec as P

BLOCK = 16
STEP = BLOCK + 2
ROWS = 24
FLAT = 512
PACK = 40
BACK = 88
F32, BF16 = jnp.float32, jnp.bfloat16
GRANT = pltpu.CompilerParams(vmem_limit_bytes=20 * 1024 * 1024)
FULL = pl.BlockSpec(memory_space=pltpu.VMEM)


def halves(x):
    high = x.astype(BF16)
    return high, (x - high.astype(F32)).astype(BF16)


def product(a, b, dims):
    def one(x, y):
        return lax.dot_general(x, y, (dims, ((), ())), preferred_element_type=F32)

    return one(a[0], b[0]) + (one(a[0], b[1]) + one(a[1], b[0]))


NN, NT, TN = ((1,), (0,)), ((1,), (1,)), ((0,), (0,))


def prepare_kernel(features, cotangent, weight, edge, packed, part):
    parity = lax.axis_index("rows") % 2
    row = features[(ROWS // 2 - 1) * parity]
    edge[0:8, :] = row[:, :128]
    edge[8:16, :] = row[:, 128:]
    edge[16:32, :] = cotangent[(ROWS - 1) * parity]
    part[...] = jnp.zeros_like(part)
    for t in range(9):
        rows = jnp.where(parity == 0, weight[t, 0:4, :], weight[t, 4:8, :])
        for core in range(2):
            for h in range(2):
                at = (t * 2 + h) * 2
                part[core, at : at + 2, :] = rows[
                    2 * core : 2 * core + 2, h * 128 : h * 128 + 128
                ]
    for core in range(2):
        tile = part[core]
        for block in range(16):
            packed[2 * block + core] = tile


def pack_kernel(own, other, near, far, out, image, line):
    parity = lax.axis_index("rows") % 2
    image[...] = jnp.zeros_like(image)
    line[...] = jnp.zeros_like(line)
    inner = slice(128, 384)
    half = ROWS // 2
    for i in range(half):
        image[1 + half * parity + i, :, inner] = own[i]
        image[1 + half * (1 - parity) + i, :, inner] = other[i]
    for edge, at in ((near, parity), (far, 1 - parity)):
        image[(ROWS + 1) * at, :, 128:256] = edge[0:8]
        image[(ROWS + 1) * at, :, 256:384] = edge[8:16]
    for block in range(16):
        start = 127 + BLOCK * block
        for r in range(ROWS + 2):
            line[:, r * STEP : (r + 1) * STEP] = image[r, :, start : start + STEP]
        for q in range(4):
            tile = line[:, q * 128 : (q + 1) * 128]
            out[2 * block, q * 8 : q * 8 + 8, :] = tile
            out[2 * block + 1, q * 8 : q * 8 + 8, :] = tile


def column_kernel(own, other, near, far, tall, side):
    parity = lax.axis_index("rows") % 2
    core = lax.axis_index("chan") % 2
    tall[pl.ds(1 + ROWS * parity, ROWS)] = own[...]
    tall[pl.ds(1 + ROWS * (1 - parity), ROWS)] = other[...]
    tall[(2 * ROWS + 1) * parity] = near[16:32]
    tall[(2 * ROWS + 1) * (1 - parity)] = far[16:32]
    for r in range(2 * ROWS + 2):
        line = tall[r]
        side[r : r + 1, :] = jnp.where(core == 0, line[0:1], line[15:16])


def window_kernel(own, other, near, far, weight, s_high, s_low, grad, image, sums):
    core = lax.axis_index("chan") % 2
    group = 2 * (lax.axis_index("rows") % 2) + core
    image[:, pl.ds(pl.multiple_of(8 + 16 * core, 8), 16), :] = own[...]
    image[:, pl.ds(pl.multiple_of(24 - 16 * core, 8), 16), :] = other[...]
    left = jnp.where(core == 0, near[...], far[...])
    right = jnp.where(core == 0, far[...], near[...])
    for r in range(2 * ROWS + 2):
        image[r, 7:8, :] = left[r : r + 1]
        image[r, 40:41, :] = right[r : r + 1]
    sums[...] = jnp.zeros_like(sums)

    def cells(r, start, count):
        return image[r, pl.ds(start, count, stride=2), :]

    def pairs(r, start, count):
        return cells(r, start, count) + cells(r, start + 1, count)

    even = [pairs(r, 7, 17) for r in range(2 * ROWS + 2)]
    odd = [pairs(r, 8, 16) for r in range(2 * ROWS + 2)]
    for r in range(ROWS + 1):
        at = r * STEP
        sums[at : at + 17, 0:128] = even[2 * r] + even[2 * r + 1]
        sums[at : at + 16, 128:256] = odd[2 * r] + odd[2 * r + 1]
        if r < ROWS:
            sums[at : at + 17, 256:384] = even[2 * r + 1] + even[2 * r + 2]
            sums[at : at + 16, 384:512] = odd[2 * r + 1] + odd[2 * r + 2]
    high, low = halves(sums[...])
    s_high[...] = high
    s_low[...] = low
    total = None
    for kind in range(4):
        lanes = slice(kind * 128, (kind + 1) * 128)
        taps = [t for t in range(9) if kind_of(t) == kind]
        left_side = jnp.concatenate(
            [
                weight[pl.ds(t * 256 + 2 * group + j, 32, stride=8), :]
                for t in taps
                for j in range(2)
            ],
            axis=0,
        )
        each = product(halves(left_side), (high[:, lanes], low[:, lanes]), NT)
        for i, t in enumerate(taps):
            term = each[i * 64 : (i + 1) * 64]
            if shift_of(t):
                term = pltpu.roll(term, FLAT - shift_of(t), 1)
            total = term if total is None else total + term
    grad[...] = total


def kind_of(t):
    return 2 * (t // 3 == 1) + (t % 3 == 1)


def shift_of(t):
    return STEP * (t // 3 == 0) + (t % 3 == 0)


def main_kernel(recv, kernels, s_high, s_low, grad, out, x_high, x_low, w_high, w_low, g_high, g_low):
    for pair in range(16):
        for q in range(4):
            tile = jnp.concatenate(
                [recv[pl.ds((2 * pair + i) * 32 + q * 8, 8), :] for i in range(2)], axis=0
            )
            high, low = halves(tile)
            x_high[pair * 16 : pair * 16 + 16, q * 128 : q * 128 + 128] = high
            x_low[pair * 16 : pair * 16 + 16, q * 128 : q * 128 + 128] = low
    for t in range(9):
        for h in range(2):
            tile = jnp.concatenate(
                [kernels[pl.ds((t * 2 + h) * 2 + j, 32, stride=PACK), :] for j in range(2)], axis=0
            )
            high, low = halves(tile)
            w_high[t * 64 : t * 64 + 64, h * 128 : h * 128 + 128] = high
            w_low[t * 64 : t * 64 + 64, h * 128 : h * 128 + 128] = low
    weights = (w_high[...], w_low[...])
    image = (x_high[...], x_low[...])
    each = product(weights, image, NN)
    hidden = each[0:64]
    for t in range(1, 9):
        hidden = hidden + pltpu.roll(each[t * 64 : t * 64 + 64], FLAT - ((t // 3) * STEP + t % 3), 1)
    at = lax.broadcasted_iota(jnp.int32, (64, FLAT), 1)
    inside = (at % STEP < BLOCK) & (at < ROWS * STEP)
    sigma = 1.0 / (1.0 + jnp.exp(-hidden))
    active = jnp.where(inside, hidden * sigma, 0.0)
    slope = sigma * (1.0 + hidden * (1.0 - sigma))
    gradient = jnp.where(inside, grad[...] * slope, 0.0)
    for t in range(9):
        shift = (t // 3) * STEP + t % 3
        moved = pltpu.roll(gradient, shift, 1) if shift else gradient
        high, low = halves(moved)
        g_high[t * 64 : t * 64 + 64, :] = high
        g_low[t * 64 : t * 64 + 64, :] = low
    moved = (g_high[...], g_low[...])
    into = product(moved, image, NT)
    for t in range(9):
        for h in range(2):
            for j in range(2):
                out[pl.ds(32 + (t * 2 + h) * 2 + j, 32, stride=BACK), :] = into[
                    t * 64 + j * 32 : t * 64 + j * 32 + 32, h * 128 : h * 128 + 128
                ]
    shifts = [0, 1, STEP, STEP + 1]
    spread = jnp.concatenate([pltpu.roll(active, s, 1) if s else active for s in shifts], axis=0)
    onto = product(halves(spread), (s_high[...], s_low[...]), NN)
    for t in range(9):
        at, kind = shifts.index(shift_of(t)) * 64, kind_of(t)
        for j in range(2):
            out[pl.ds(68 + t * 2 + j, 32, stride=BACK), :] = onto[
                at + j * 32 : at + j * 32 + 32, kind * 128 : kind * 128 + 128
            ]
    back = product(weights, moved, TN)
    for d in range(32):
        for q in range(4):
            out[pl.ds(d * BACK + q * 8, 8), :] = back[d * 8 : d * 8 + 8, q * 128 : q * 128 + 128]
    blank = jnp.zeros((2, 128), F32)
    for d in range(32):
        out[pl.ds(d * BACK + 86, 2), :] = blank


def gather_kernel(scale, recv, weights, mine, theirs, beside, beyond, image, line, total, mixed):
    parity = lax.axis_index("rows") % 2
    mixed[...] = jnp.zeros_like(mixed)
    for core in range(2):
        each = recv[core, 32:BACK, :]
        for block in range(1, 16):
            each = each + recv[2 * block + core, 32:BACK, :]
        total[...] = each * scale
        for j in range(2):
            mixed[pl.ds(2 * core + j, 27, stride=4), :] = total[pl.ds(j, 27, stride=2), :]
    tile = mixed[...]
    for z in range(8):
        weights[z] = tile
    image[...] = jnp.zeros_like(image)
    for block in range(16):
        start = 127 + BLOCK * block
        for q in range(4):
            at = slice(q * 8, q * 8 + 8)
            line[:, q * 128 : q * 128 + 128] = recv[2 * block, at, :] + recv[2 * block + 1, at, :]
        for r in range(ROWS + 2):
            image[r, :, start : start + STEP] += line[:, r * STEP : (r + 1) * STEP]
    half = ROWS // 2
    for i in range(half):
        mine[i] = image[1 + half * parity + i, :, 128:384]
        theirs[i] = image[1 + half * (1 - parity) + i, :, 128:384]
    beside[...] = image[(ROWS + 1) * parity, :, 128:384]
    beyond[...] = image[(ROWS + 1) * (1 - parity), :, 128:384]


def final_kernel(recv, into, onto):
    sums = []
    for parity in range(2):
        sums.append((recv[parity] + recv[2 + parity]) + (recv[4 + parity] + recv[6 + parity]))
    for k in range(27):
        tile = jnp.concatenate([x[4 * k : 4 * k + 4] for x in sums], axis=0)
        if k < 18:
            into[k // 2, :, (k % 2) * 128 : (k % 2) * 128 + 128] = tile
        else:
            onto[k - 18] = tile


def shape(*dims, dtype=F32):
    return jax.ShapeDtypeStruct(dims, dtype)


def call(kernel, outs, args, scratch=(), flops=10**6, moved=10**6):
    return pl.pallas_call(
        kernel,
        out_shape=outs,
        in_specs=[FULL] * args,
        out_specs=jax.tree.map(lambda _: FULL, outs),
        scratch_shapes=list(scratch),
        compiler_params=GRANT,
        cost_estimate=pl.CostEstimate(flops=flops, bytes_accessed=moved, transcendentals=0),
    )


def partner(n):
    return [(i, i ^ 1) for i in range(n)]


def beside(n):
    return [(i, i + 1) for i in range(1, n - 1, 2)] + [(i, i - 1) for i in range(2, n, 2)]


def inward(n):
    return [(i, i + 2) for i in range(1, n - 2, 2)] + [(i, i - 2) for i in range(2, n, 2)]


def outward(n):
    return [(i, i + 2) for i in range(0, n - 2, 2)] + [(i, i - 2) for i in range(3, n, 2)]


def local(features, weight_in, weight_out, cotangent):
    parity = lax.axis_index("rows") % 2
    scale = (4.0 * features.shape[1] * lax.axis_size("rows") * features.shape[2]) ** (-0.5)
    wide = pltpu.VMEM((ROWS + 2, 8, 512), F32)
    flat = pltpu.VMEM((8, FLAT), F32)

    lines = jnp.transpose(features, (1, 0, 2))
    taps = jnp.transpose(weight_in, (1, 2, 0, 3)).reshape(9, 8, 256)
    edge, packed = call(
        prepare_kernel, (shape(32, 128), shape(32, PACK, 128)), 3, [pltpu.VMEM((2, PACK, 128), F32)]
    )(lines, cotangent, taps)
    kernels = lax.all_to_all(packed, "chan", 0, 0, tiled=True)
    near = lax.ppermute(edge, "rows", beside(8))
    far = lax.ppermute(edge, "rows", inward(8))
    other = lax.ppermute(lines, "rows", partner(8))
    other_c = lax.ppermute(cotangent, "rows", partner(8))
    packed = call(pack_kernel, shape(32, 32, 128), 4, [wide, flat])(lines, other, near, far)
    recv = lax.all_to_all(packed, "chan", 0, 0, tiled=True)

    tall, side = call(column_kernel, (shape(50, 16, 128), shape(50, 128)), 4)(
        cotangent, other_c, near, far
    )
    side = lax.ppermute(side, "chan", beside(32))
    other_tall = lax.ppermute(tall, "chan", partner(32))
    other_side = lax.ppermute(side, "chan", partner(32))
    s_high, s_low, grad = call(
        window_kernel,
        (shape(FLAT, 512, dtype=BF16), shape(FLAT, 512, dtype=BF16), shape(64, FLAT)), 5,
        [pltpu.VMEM((2 * ROWS + 2, 48, 128), F32), pltpu.VMEM((FLAT, 512), F32)],
        3 * 10**8, 3 * 10**6,
    )(tall, other_tall, side, other_side, jnp.transpose(weight_out, (1, 2, 0, 3)).reshape(2304, 128))

    sent = call(
        main_kernel, shape(32 * BACK, 128), 5,
        [
            pltpu.VMEM((256, FLAT), BF16), pltpu.VMEM((256, FLAT), BF16),
            pltpu.VMEM((576, 256), BF16), pltpu.VMEM((576, 256), BF16),
            pltpu.VMEM((576, FLAT), BF16), pltpu.VMEM((576, FLAT), BF16),
        ],
        10**9, 5 * 10**6,
    )(recv.reshape(1024, 128), kernels.reshape(32 * PACK, 128), s_high, s_low, grad)
    back = lax.all_to_all(sent.reshape(32, BACK, 128), "chan", 0, 0, tiled=True)

    sums, own, given, close, away = call(
        lambda *refs: gather_kernel(scale, *refs),
        (shape(8, 112, 128), shape(12, 8, 256), shape(12, 8, 256), shape(8, 256), shape(8, 256)), 1,
        [wide, flat, pltpu.VMEM((56, 128), F32), pltpu.VMEM((112, 128), F32)],
    )(back)
    given = lax.ppermute(given, "rows", partner(8))
    close = lax.ppermute(close, "rows", beside(8))
    away = lax.ppermute(away, "rows", outward(8))
    sums = lax.all_to_all(sums, "rows", 0, 0, tiled=True)
    place = (jnp.arange(12) == 11 * parity)[:, None, None]
    grad_image = jnp.transpose((own + given) + jnp.where(place, (close + away)[None], 0.0), (1, 0, 2))
    into, onto = call(final_kernel, (shape(9, 8, 256), shape(9, 8, 128)), 1)(sums)
    grad_in = jnp.transpose(into.reshape(3, 3, 8, 256), (2, 0, 1, 3))
    grad_out = jnp.transpose(onto.reshape(3, 3, 8, 128), (2, 0, 1, 3))
    return (grad_image, grad_in, grad_out)


def solution(mesh):
    return jax.shard_map(
        local,
        mesh=mesh,
        in_specs=(
            P("chan", "rows", None),
            P("chan", None, None, None),
            P(),
            P("rows", "chan", None),
        ),
        out_specs=(
            P("chan", "rows", None),
            P("chan", None, None, None),
            P("chan", None, None, None),
        ),
        check_vma=False,
    )
```

time: 114 us -> 116 us (1.018)
  the two profiles are of different devices: /device:TPU:96 before, /device:TPU:1 now
where the time goes in v1:
time: 116 us; the launch traced here: 115 us
  blocking collectives  50.8 us (44%)
  starting transfers between devices  29.6 us (26%)
  waiting for transfers between devices  23.2 us (20%)
  Pallas kernels  7.59 us (7%)
  local copies, waits for them, and re-layouts  2.71 us (2%)
    all_to_all x1, blocking collectives, local(): back = lax.all_to_all(sent.reshape(32, BACK, 128), 'chan', 0, 0, tiled=True)  30.4 us
    all_to_all x1, blocking collectives, local(): recv = lax.all_to_all(packed, 'chan', 0, 0, tiled=True)  20.4 us
    all_to_all x1, starting transfers between devices, local(): sums = lax.all_to_all(sums, 'rows', 0, 0, tiled=True)  6.59 us
    ppermute x1, waiting for transfers between devices, local(): given = lax.ppermute(given, 'rows', partner(8))  6.11 us
    ppermute x1, waiting for transfers between devices, local(): far = lax.ppermute(edge, 'rows', inward(8))  5.97 us
    ppermute x1, starting transfers between devices, local(): away = lax.ppermute(away, 'rows', outward(8))  5.79 us
    ppermute x1, waiting for transfers between devices, local(): other_c = lax.ppermute(cotangent, 'rows', partner(8))  5 us
    all_to_all x1, starting transfers between devices, local(): kernels = lax.all_to_all(packed, 'chan', 0, 0, tiled=True)  4 us
  transfers between devices with their start and end apart: 12, of which 7 were waited for; matrix products, arithmetic and copies ran while one was open for 1% of the time, Pallas kernels for 2%

profile of v1, /device:TPU:1, one launch (start us, length us, event | category | flops | bytes accessed | tf_op | source)
XLA Modules:
  0.0 115.3 jit_solution(8560947204509021608)
XLA Ops:
  0.6 2.6 %collective-permute-start = (f32[12,8,256]{2,1,0:T(8,128)}, f32[12,8,256]{2,1,0:T(8,128)S(1)}, u32[]{:S(2)}, u32[]{:S(2)}) collective-permute-start(f32[12,8,256]{2,1,0:T(8,128)} %bitcast.22), channel_id=1, source_target_pairs={{0,32},{32,0},{64,96},{96,64},{128,160},{160,128},{192,224},{224,1... | collective-permute-start | bytes 294920 | tf_op jit(solution)/shard_map/ppermute | solution.py:296
  3.2 0.9 copy-done.1
  4.1 0.9 copy-done.3
  5.0 0.9 copy-done.4
  5.9 0.9 shard_map.67
  6.8 0.8 collective-permute-start.1
  7.6 1.3 %collective-permute-start.2 = (f32[32,128]{1,0:T(8,128)S(1)}, f32[32,128]{1,0:T(8,128)S(1)}, u32[]{:S(2)}, u32[]{:S(2)}) collective-permute-start(f32[32,128]{1,0:T(8,128)S(1)} %get-tuple-element.17), channel_id=1, source_target_pairs={{32,96},{96,160},{160,224},{64,0},{128,64},{192,128},{33,97},{97,1... | collective-permute-start | bytes 49160 | tf_op jit(solution)/shard_map/ppermute | solution.py:295
  8.9 6.0 %collective-permute-done.2.far = f32[32,128]{1,0:T(8,128)S(1)} collective-permute-done((f32[32,128]{1,0:T(8,128)S(1)}, f32[32,128]{1,0:T(8,128)S(1)}, u32[]{:S(2)}, u32[]{:S(2)}) %collective-permute-start.2) | collective-permute-done | bytes 16416 | tf_op jit(solution)/shard_map/ppermute | solution.py:295
  14.9 0.8 shard_map.68
  15.7 0.0 copy-start
  15.7 20.4 %all_to_all.20 = f32[32,32,128]{2,1,0:T(8,128)S(1)} all-to-all(f32[32,32,128]{2,1,0:T(8,128)S(1)} %shard_map.68), channel_id=1, replica_groups=mesh['rows'=8,'chan'=32] {'chan'}, dimensions={0} | all-to-all | bytes 1048576 | tf_op jit(solution)/shard_map/all_to_all | solution.py:299
  36.1 4.0 %all-to-all-start.1 = ((f32[32,40,128]{2,1,0:T(8,128)}), f32[32,40,128]{2,1,0:T(8,128)S(1)}, u32[]{:S(2)}, u32[]{:S(2)}) async-start(f32[32,40,128]{2,1,0:T(8,128)} %get-tuple-element.18), calls=%async_computation.1 | async-start | bytes 1310720 | tf_op jit(solution)/shard_map/all_to_all | solution.py:293
  40.1 3.7 %collective-permute-start.3 = (f32[24,16,128]{2,1,0:T(8,128)S(1)}, f32[24,16,128]{2,1,0:T(8,128)S(1)}, u32[]{:S(2)}, u32[]{:S(2)}) collective-permute-start(f32[24,16,128]{2,1,0:T(8,128)S(1)} %copy-done.2), channel_id=1, source_target_pairs={{0,32},{32,0},{64,96},{96,64},{128,160},{160,128},{192,224},{224,1... | collective-permute-start | bytes 589832 | tf_op jit(solution)/shard_map/ppermute | solution.py:297
  43.7 5.0 %collective-permute-done.3.other = f32[24,16,128]{2,1,0:T(8,128)S(1)} collective-permute-done((f32[24,16,128]{2,1,0:T(8,128)S(1)}, f32[24,16,128]{2,1,0:T(8,128)S(1)}, u32[]{:S(2)}, u32[]{:S(2)}) %collective-permute-start.3) | collective-permute-done | bytes 196640 | tf_op jit(solution)/shard_map/ppermute | solution.py:297
  48.7 0.1 shard_map.69
  48.8 0.9 collective-permute-start.4
  49.8 3.2 %collective-permute-start.5 = (f32[50,128]{1,0:T(8,128)S(1)}, f32[50,128]{1,0:T(8,128)S(1)}, u32[]{:S(2)}, u32[]{:S(2)}) collective-permute-start(f32[50,128]{1,0:T(8,128)S(1)} %get-tuple-element.20), channel_id=1, source_target_pairs={{1,2},{3,4},{5,6},{7,8},{9,10},{11,12},{13,14},{15,16},{17,18},{19... | collective-permute-start | bytes 76808 | tf_op jit(solution)/shard_map/ppermute | solution.py:304
  53.0 2.0 %collective-permute-done.5.near = f32[50,128]{1,0:T(8,128)S(1)} collective-permute-done((f32[50,128]{1,0:T(8,128)S(1)}, f32[50,128]{1,0:T(8,128)S(1)}, u32[]{:S(2)}, u32[]{:S(2)}) %collective-permute-start.5) | collective-permute-done | bytes 25632 | tf_op jit(solution)/shard_map/ppermute | solution.py:304
  54.9 1.2 %collective-permute-done.6.far = f32[50,128]{1,0:T(8,128)S(1)} collective-permute-done((f32[50,128]{1,0:T(8,128)S(1)}, f32[50,128]{1,0:T(8,128)S(1)}, u32[]{:S(2)}, u32[]{:S(2)}) %collective-permute-start.6) | collective-permute-done | bytes 25632 | tf_op jit(solution)/shard_map/ppermute | solution.py:306
  56.1 1.0 shard_map.70
  57.1 2.7 %shard_map.71 = f32[2816,128]{1,0:T(8,128)S(1)} custom-call(f32[1024,128]{1,0:T(8,128)S(1)} %bitcast.20, f32[1280,128]{1,0:T(8,128)S(1)} %bitcast.19, bf16[512,512]{1,0:T(8,128)(2,1)S(1)} %get-tuple-element.21.s_high, bf16[512,512]{1,0:T(8,128)(2,1)S(1)} %get-tuple-element.22.s_low, f32[64,512]{1,0:T(8,128)S(1)} %get-tuple-element.23.grad), custom_call_target="tpu_custom_call" | custom-call | flops 1000000000 | bytes 5000000 | tf_op jit(solution)/shard_map/pallas_call | solution.py:314
  59.9 30.4 %all_to_all.21.refs_0_ = f32[32,88,128]{2,1,0:T(8,128)S(1)} all-to-all(f32[32,88,128]{2,1,0:T(8,128)S(1)} %bitcast.18), channel_id=1, replica_groups=mesh['rows'=8,'chan'=32] {'chan'}, dimensions={0} | all-to-all | bytes 2883584 | tf_op jit(solution)/shard_map/all_to_all | solution.py:323
  90.3 1.4 %shard_map.72 = (f32[8,112,128]{2,1,0:T(8,128)}, f32[12,8,256]{2,1,0:T(8,128)S(1)}, f32[12,8,256]{2,1,0:T(8,128)S(1)}, f32[8,256]{1,0:T(8,128)S(1)}, f32[8,256]{1,0:T(8,128)S(1)}) custom-call(f32[32,88,128]{2,1,0:T(8,128)S(1)} %all_to_all.21.refs_0_), custom_call_target="tpu_custom_call" | custom-call | flops 1000000 | bytes 1000000 | tf_op jit(solution)/shard_map/pallas_call | solution.py:325
  91.7 6.6 %all-to-all-start.3 = ((f32[8,112,128]{2,1,0:T(8,128)}), f32[8,112,128]{2,1,0:T(8,128)S(1)}, u32[]{:S(2)}, u32[]{:S(2)}) async-start(f32[8,112,128]{2,1,0:T(8,128)} %get-tuple-element.28), calls=%async_computation.3 | async-start | bytes 917504 | tf_op jit(solution)/shard_map/all_to_all | solution.py:333
  98.3 0.6 collective-permute-start.8
  99.0 5.8 %collective-permute-start.9 = (f32[8,256]{1,0:T(8,128)S(1)}, f32[8,256]{1,0:T(8,128)S(1)}, u32[]{:S(2)}, u32[]{:S(2)}) collective-permute-start(f32[8,256]{1,0:T(8,128)S(1)} %get-tuple-element.27), channel_id=1, source_target_pairs={{0,64},{64,128},{128,192},{96,32},{160,96},{224,160},{1,65},{65,12... | collective-permute-start | bytes 24584 | tf_op jit(solution)/shard_map/ppermute | solution.py:332
  104.8 0.1 collective-permute-start.7
  104.9 0.8 collective-permute-done.9
  105.7 6.1 %collective-permute-done.7 = f32[12,8,256]{2,1,0:T(8,128)S(1)} collective-permute-done((f32[12,8,256]{2,1,0:T(8,128)S(1)}, f32[12,8,256]{2,1,0:T(8,128)S(1)}, u32[]{:S(2)}, u32[]{:S(2)}) %collective-permute-start.7) | collective-permute-done | bytes 98336 | tf_op jit(solution)/shard_map/ppermute | solution.py:330
  111.8 0.7 add_bitcast_fusion
  112.5 2.1 %all-to-all-done.3.recv = f32[8,112,128]{2,1,0:T(8,128)S(1)} async-done(((f32[8,112,128]{2,1,0:T(8,128)}), f32[8,112,128]{2,1,0:T(8,128)S(1)}, u32[]{:S(2)}, u32[]{:S(2)}) %all-to-all-start.3) | async-done | bytes 458784 | tf_op jit(solution)/shard_map/all_to_all | solution.py:333
  114.6 0.7 shard_map.73
  (14 shorter events, 0.0 us)
Async XLA Ops:
  0.6 14.3 %collective-permute-start = (f32[12,8,256]{2,1,0:T(8,128)}, f32[12,8,256]{2,1,0:T(8,128)S(1)}, u32[]{:S(2)}, u32[]{:S(2)}) collective-permute-start(f32[12,8,256]{2,1,0:T(8,128)} %bitcast.22), channel_id=1, source_target_pairs={{0,32},{32,0},{64,96},{96,64},{128,160},{160,128},{192,224},{224,1... | collective-permute-start | bytes 294920 | tf_op jit(solution)/shard_map/ppermute | solution.py:296
  3.2 0.9 copy-start.1
  4.1 0.9 copy-start.3
  5.0 0.9 copy-start.4
  6.8 33.2 %copy-start.2 = (f32[24,16,128]{2,1,0:T(8,128)S(1)}, f32[24,16,128]{2,1,0:T(8,128)}, u32[]{:S(2)}) copy-start(f32[24,16,128]{2,1,0:T(8,128)} %own.1) | copy-start | bytes 589828
  6.8 2.1 %collective-permute-start.1 = (f32[32,128]{1,0:T(8,128)S(1)}, f32[32,128]{1,0:T(8,128)S(1)}, u32[]{:S(2)}, u32[]{:S(2)}) collective-permute-start(f32[32,128]{1,0:T(8,128)S(1)} %get-tuple-element.17), channel_id=1, source_target_pairs={{32,64},{96,128},{160,192},{64,32},{128,96},{192,160},{33,65},{97,... | collective-permute-start | bytes 49160 | tf_op jit(solution)/shard_map/ppermute | solution.py:294
  7.6 7.3 %collective-permute-start.2 = (f32[32,128]{1,0:T(8,128)S(1)}, f32[32,128]{1,0:T(8,128)S(1)}, u32[]{:S(2)}, u32[]{:S(2)}) collective-permute-start(f32[32,128]{1,0:T(8,128)S(1)} %get-tuple-element.17), channel_id=1, source_target_pairs={{32,96},{96,160},{160,224},{64,0},{128,64},{192,128},{33,97},{97,1... | collective-permute-start | bytes 49160 | tf_op jit(solution)/shard_map/ppermute | solution.py:295
  15.7 40.5 %copy-start = (f32[256,3,3,128]{3,0,2,1:T(8,128)S(1)}, f32[256,3,3,128]{3,0,2,1:T(8,128)}, u32[]{:S(2)}) copy-start(f32[256,3,3,128]{3,0,2,1:T(8,128)} %param.6) | copy-start | bytes 3538948
  36.1 21.1 %all-to-all-start.1 = ((f32[32,40,128]{2,1,0:T(8,128)}), f32[32,40,128]{2,1,0:T(8,128)S(1)}, u32[]{:S(2)}, u32[]{:S(2)}) async-start(f32[32,40,128]{2,1,0:T(8,128)} %get-tuple-element.18), calls=%async_computation.1 | async-start | bytes 1310720 | tf_op jit(solution)/shard_map/all_to_all | solution.py:293
  40.1 8.7 %collective-permute-start.3 = (f32[24,16,128]{2,1,0:T(8,128)S(1)}, f32[24,16,128]{2,1,0:T(8,128)S(1)}, u32[]{:S(2)}, u32[]{:S(2)}) collective-permute-start(f32[24,16,128]{2,1,0:T(8,128)S(1)} %copy-done.2), channel_id=1, source_target_pairs={{0,32},{32,0},{64,96},{96,64},{128,160},{160,128},{192,224},{224,1... | collective-permute-start | bytes 589832 | tf_op jit(solution)/shard_map/ppermute | solution.py:297
  48.8 7.3 %collective-permute-start.4 = (f32[50,16,128]{2,1,0:T(8,128)S(1)}, f32[50,16,128]{2,1,0:T(8,128)S(1)}, u32[]{:S(2)}, u32[]{:S(2)}) collective-permute-start(f32[50,16,128]{2,1,0:T(8,128)S(1)} %get-tuple-element.19.own), channel_id=1, source_target_pairs={{0,1},{1,0},{2,3},{3,2},{4,5},{5,4},{6,7},{7,6},{8,9},{9,8},{10,11... | collective-permute-start | bytes 1228808 | tf_op jit(solution)/shard_map/ppermute | solution.py:305
  49.8 5.2 %collective-permute-start.5 = (f32[50,128]{1,0:T(8,128)S(1)}, f32[50,128]{1,0:T(8,128)S(1)}, u32[]{:S(2)}, u32[]{:S(2)}) collective-permute-start(f32[50,128]{1,0:T(8,128)S(1)} %get-tuple-element.20), channel_id=1, source_target_pairs={{1,2},{3,4},{5,6},{7,8},{9,10},{11,12},{13,14},{15,16},{17,18},{19... | collective-permute-start | bytes 76808 | tf_op jit(solution)/shard_map/ppermute | solution.py:304
  54.9 1.2 %collective-permute-start.6 = (f32[50,128]{1,0:T(8,128)S(1)}, f32[50,128]{1,0:T(8,128)S(1)}, u32[]{:S(2)}, u32[]{:S(2)}) collective-permute-start(f32[50,128]{1,0:T(8,128)S(1)} %collective-permute-done.5.near), channel_id=1, source_target_pairs={{0,1},{1,0},{2,3},{3,2},{4,5},{5,4},{6,7},{7,6},{8,9},{9,8},{10,11... | collective-permute-start | bytes 76808 | tf_op jit(solution)/shard_map/ppermute | solution.py:306
  91.7 22.9 %all-to-all-start.3 = ((f32[8,112,128]{2,1,0:T(8,128)}), f32[8,112,128]{2,1,0:T(8,128)S(1)}, u32[]{:S(2)}, u32[]{:S(2)}) async-start(f32[8,112,128]{2,1,0:T(8,128)} %get-tuple-element.28), calls=%async_computation.3 | async-start | bytes 917504 | tf_op jit(solution)/shard_map/all_to_all | solution.py:333
  98.3 6.6 %collective-permute-start.8 = (f32[8,256]{1,0:T(8,128)S(1)}, f32[8,256]{1,0:T(8,128)S(1)}, u32[]{:S(2)}, u32[]{:S(2)}) collective-permute-start(f32[8,256]{1,0:T(8,128)S(1)} %get-tuple-element.26), channel_id=1, source_target_pairs={{32,64},{96,128},{160,192},{64,32},{128,96},{192,160},{33,65},{97,... | collective-permute-start | bytes 24584 | tf_op jit(solution)/shard_map/ppermute | solution.py:331
  99.0 6.7 %collective-permute-start.9 = (f32[8,256]{1,0:T(8,128)S(1)}, f32[8,256]{1,0:T(8,128)S(1)}, u32[]{:S(2)}, u32[]{:S(2)}) collective-permute-start(f32[8,256]{1,0:T(8,128)S(1)} %get-tuple-element.27), channel_id=1, source_target_pairs={{0,64},{64,128},{128,192},{96,32},{160,96},{224,160},{1,65},{65,12... | collective-permute-start | bytes 24584 | tf_op jit(solution)/shard_map/ppermute | solution.py:332
  104.8 7.0 %collective-permute-start.7 = (f32[12,8,256]{2,1,0:T(8,128)S(1)}, f32[12,8,256]{2,1,0:T(8,128)S(1)}, u32[]{:S(2)}, u32[]{:S(2)}) collective-permute-start(f32[12,8,256]{2,1,0:T(8,128)S(1)} %get-tuple-element.25), channel_id=1, source_target_pairs={{0,32},{32,0},{64,96},{96,64},{128,160},{160,128},{192,224},{224,1... | collective-permute-start | bytes 294920 | tf_op jit(solution)/shard_map/ppermute | solution.py:330

commit v2 on v1

--- a/solution.py
+++ b/solution.py
@@ -8,11 +8,12 @@
 BLOCK = 16
 STEP = BLOCK + 2
 ROWS = 24
+FINE = 2 * ROWS + 6
 FLAT = 512
 PACK = 40
 BACK = 88
 F32, BF16 = jnp.float32, jnp.bfloat16
-GRANT = pltpu.CompilerParams(vmem_limit_bytes=20 * 1024 * 1024)
+GRANT, MOST = 20 * 1024 * 1024, 60 * 1024 * 1024
 FULL = pl.BlockSpec(memory_space=pltpu.VMEM)
 
 
@@ -31,15 +32,27 @@
 NN, NT, TN = ((1,), (0,)), ((1,), (1,)), ((0,), (0,))
 
 
-def prepare_kernel(features, cotangent, weight, edge, packed, part):
+def prepare_kernel(features, cotangent, weight, edge, packed, lines, cells, taps, part, sems):
     parity = lax.axis_index("rows") % 2
-    row = features[(ROWS // 2 - 1) * parity]
-    edge[0:8, :] = row[:, :128]
-    edge[8:16, :] = row[:, 128:]
-    edge[16:32, :] = cotangent[(ROWS - 1) * parity]
+    half = ROWS // 2
+    copies = [
+        pltpu.make_async_copy(weight, taps, sems.at[0]),
+        pltpu.make_async_copy(features.at[pl.ds((half - 2) * parity, 2)], lines, sems.at[1]),
+        pltpu.make_async_copy(cotangent.at[pl.ds((ROWS - 3) * parity, 3)], cells, sems.at[2]),
+    ]
+    for copy in copies:
+        copy.start()
     part[...] = jnp.zeros_like(part)
+    for copy in copies:
+        copy.wait()
+    for k in range(2):
+        for h in range(2):
+            at = (2 * k + h) * 8
+            edge[at : at + 8, :] = lines[k, :, h * 128 : h * 128 + 128]
+    for k in range(3):
+        edge[32 + k * 16 : 48 + k * 16, :] = cells[k]
     for t in range(9):
-        rows = jnp.where(parity == 0, weight[t, 0:4, :], weight[t, 4:8, :])
+        rows = jnp.where(parity == 0, taps[t, 0:4, :], taps[t, 4:8, :])
         for core in range(2):
             for h in range(2):
                 at = (t * 2 + h) * 2
@@ -59,14 +72,16 @@
     inner = slice(128, 384)
     half = ROWS // 2
     for i in range(half):
-        image[1 + half * parity + i, :, inner] = own[i]
-        image[1 + half * (1 - parity) + i, :, inner] = other[i]
+        image[2 + half * parity + i, :, inner] = own[i]
+        image[2 + half * (1 - parity) + i, :, inner] = other[i]
     for edge, at in ((near, parity), (far, 1 - parity)):
-        image[(ROWS + 1) * at, :, 128:256] = edge[0:8]
-        image[(ROWS + 1) * at, :, 256:384] = edge[8:16]
+        for k in range(2):
+            for h in range(2):
+                rows = (2 * k + h) * 8
+                image[(ROWS + 2) * at + k, :, 128 + h * 128 : 256 + h * 128] = edge[rows : rows + 8]
     for block in range(16):
         start = 127 + BLOCK * block
-        for r in range(ROWS + 2):
+        for r in range(ROWS + 4):
             line[:, r * STEP : (r + 1) * STEP] = image[r, :, start : start + STEP]
         for q in range(4):
             tile = line[:, q * 128 : (q + 1) * 128]
@@ -77,13 +92,15 @@
 def column_kernel(own, other, near, far, tall, side):
     parity = lax.axis_index("rows") % 2
     core = lax.axis_index("chan") % 2
-    tall[pl.ds(1 + ROWS * parity, ROWS)] = own[...]
-    tall[pl.ds(1 + ROWS * (1 - parity), ROWS)] = other[...]
-    tall[(2 * ROWS + 1) * parity] = near[16:32]
-    tall[(2 * ROWS + 1) * (1 - parity)] = far[16:32]
-    for r in range(2 * ROWS + 2):
+    tall[pl.ds(3 + ROWS * parity, ROWS)] = own[...]
+    tall[pl.ds(3 + ROWS * (1 - parity), ROWS)] = other[...]
+    for edge, at in ((near, parity), (far, 1 - parity)):
+        for k in range(3):
+            tall[(2 * ROWS + 3) * at + k] = edge[32 + 16 * k : 48 + 16 * k]
+    for r in range(FINE):
         line = tall[r]
         side[r : r + 1, :] = jnp.where(core == 0, line[0:1], line[15:16])
+    side[FINE : FINE + 2, :] = jnp.zeros((2, 128), F32)
 
 
 def window_kernel(own, other, near, far, weight, s_high, s_low, grad, image, sums):
@@ -93,7 +110,7 @@
     image[:, pl.ds(pl.multiple_of(24 - 16 * core, 8), 16), :] = other[...]
     left = jnp.where(core == 0, near[...], far[...])
     right = jnp.where(core == 0, far[...], near[...])
-    for r in range(2 * ROWS + 2):
+    for r in range(FINE):
         image[r, 7:8, :] = left[r : r + 1]
         image[r, 40:41, :] = right[r : r + 1]
     sums[...] = jnp.zeros_like(sums)
@@ -104,13 +121,13 @@
     def pairs(r, start, count):
         return cells(r, start, count) + cells(r, start + 1, count)
 
-    even = [pairs(r, 7, 17) for r in range(2 * ROWS + 2)]
-    odd = [pairs(r, 8, 16) for r in range(2 * ROWS + 2)]
-    for r in range(ROWS + 1):
+    even = [pairs(r, 7, 17) for r in range(FINE)]
+    odd = [pairs(r, 8, 16) for r in range(FINE)]
+    for r in range(ROWS + 3):
         at = r * STEP
         sums[at : at + 17, 0:128] = even[2 * r] + even[2 * r + 1]
         sums[at : at + 16, 128:256] = odd[2 * r] + odd[2 * r + 1]
-        if r < ROWS:
+        if r < ROWS + 2:
             sums[at : at + 17, 256:384] = even[2 * r + 1] + even[2 * r + 2]
             sums[at : at + 16, 384:512] = odd[2 * r + 1] + odd[2 * r + 2]
     high, low = halves(sums[...])
@@ -169,18 +186,26 @@
     for t in range(1, 9):
         hidden = hidden + pltpu.roll(each[t * 64 : t * 64 + 64], FLAT - ((t // 3) * STEP + t % 3), 1)
     at = lax.broadcasted_iota(jnp.int32, (64, FLAT), 1)
-    inside = (at % STEP < BLOCK) & (at < ROWS * STEP)
+    block = lax.axis_index("rows") // 2
+    across = at % STEP < BLOCK
+    inside = across & (at >= STEP) & (at < (ROWS + 1) * STEP)
+    top = jnp.where(block == 0, STEP, 0)
+    bottom = jnp.where(block == 3, (ROWS + 1) * STEP, (ROWS + 2) * STEP)
+    around = across & (at >= top) & (at < bottom)
     sigma = 1.0 / (1.0 + jnp.exp(-hidden))
     active = jnp.where(inside, hidden * sigma, 0.0)
     slope = sigma * (1.0 + hidden * (1.0 - sigma))
-    gradient = jnp.where(inside, grad[...] * slope, 0.0)
-    for t in range(9):
-        shift = (t // 3) * STEP + t % 3
-        moved = pltpu.roll(gradient, shift, 1) if shift else gradient
-        high, low = halves(moved)
-        g_high[t * 64 : t * 64 + 64, :] = high
-        g_low[t * 64 : t * 64 + 64, :] = low
-    moved = (g_high[...], g_low[...])
+    gradient = grad[...] * slope
+
+    def stack(values, offset):
+        for t in range(9):
+            shift = ((t // 3) * STEP + t % 3 + offset) % FLAT
+            high, low = halves(pltpu.roll(values, shift, 1) if shift else values)
+            g_high[t * 64 : t * 64 + 64, :] = high
+            g_low[t * 64 : t * 64 + 64, :] = low
+        return g_high[...], g_low[...]
+
+    moved = stack(jnp.where(inside, gradient, 0.0), 0)
     into = product(moved, image, NT)
     for t in range(9):
         for h in range(2):
@@ -197,7 +222,7 @@
             out[pl.ds(68 + t * 2 + j, 32, stride=BACK), :] = onto[
                 at + j * 32 : at + j * 32 + 32, kind * 128 : kind * 128 + 128
             ]
-    back = product(weights, moved, TN)
+    back = product(weights, stack(jnp.where(around, gradient, 0.0), -2 * STEP), TN)
     for d in range(32):
         for q in range(4):
             out[pl.ds(d * BACK + q * 8, 8), :] = back[d * 8 : d * 8 + 8, q * 128 : q * 128 + 128]
@@ -206,7 +231,7 @@
         out[pl.ds(d * BACK + 86, 2), :] = blank
 
 
-def gather_kernel(scale, recv, weights, mine, theirs, beside, beyond, image, line, total, mixed):
+def gather_kernel(scale, recv, weights, mine, theirs, image, line, total, mixed):
     parity = lax.axis_index("rows") % 2
     mixed[...] = jnp.zeros_like(mixed)
     for core in range(2):
@@ -225,14 +250,12 @@
         for q in range(4):
             at = slice(q * 8, q * 8 + 8)
             line[:, q * 128 : q * 128 + 128] = recv[2 * block, at, :] + recv[2 * block + 1, at, :]
-        for r in range(ROWS + 2):
+        for r in range(ROWS):
             image[r, :, start : start + STEP] += line[:, r * STEP : (r + 1) * STEP]
     half = ROWS // 2
     for i in range(half):
-        mine[i] = image[1 + half * parity + i, :, 128:384]
-        theirs[i] = image[1 + half * (1 - parity) + i, :, 128:384]
-    beside[...] = image[(ROWS + 1) * parity, :, 128:384]
-    beyond[...] = image[(ROWS + 1) * (1 - parity), :, 128:384]
+        mine[i] = image[half * parity + i, :, 128:384]
+        theirs[i] = image[half * (1 - parity) + i, :, 128:384]
 
 
 def final_kernel(recv, into, onto):
@@ -251,14 +274,14 @@
     return jax.ShapeDtypeStruct(dims, dtype)
 
 
-def call(kernel, outs, args, scratch=(), flops=10**6, moved=10**6):
+def call(kernel, outs, args, scratch=(), flops=10**6, moved=10**6, specs=None, grant=GRANT):
     return pl.pallas_call(
         kernel,
         out_shape=outs,
-        in_specs=[FULL] * args,
+        in_specs=specs or [FULL] * args,
         out_specs=jax.tree.map(lambda _: FULL, outs),
         scratch_shapes=list(scratch),
-        compiler_params=GRANT,
+        compiler_params=pltpu.CompilerParams(vmem_limit_bytes=grant),
         cost_estimate=pl.CostEstimate(flops=flops, bytes_accessed=moved, transcendentals=0),
     )
 
@@ -275,41 +298,44 @@
     return [(i, i + 2) for i in range(1, n - 2, 2)] + [(i, i - 2) for i in range(2, n, 2)]
 
 
-def outward(n):
-    return [(i, i + 2) for i in range(0, n - 2, 2)] + [(i, i - 2) for i in range(3, n, 2)]
-
-
 def local(features, weight_in, weight_out, cotangent):
-    parity = lax.axis_index("rows") % 2
     scale = (4.0 * features.shape[1] * lax.axis_size("rows") * features.shape[2]) ** (-0.5)
-    wide = pltpu.VMEM((ROWS + 2, 8, 512), F32)
     flat = pltpu.VMEM((8, FLAT), F32)
 
     lines = jnp.transpose(features, (1, 0, 2))
     taps = jnp.transpose(weight_in, (1, 2, 0, 3)).reshape(9, 8, 256)
     edge, packed = call(
-        prepare_kernel, (shape(32, 128), shape(32, PACK, 128)), 3, [pltpu.VMEM((2, PACK, 128), F32)]
+        prepare_kernel, (shape(80, 128), shape(32, PACK, 128)), 3,
+        [
+            pltpu.VMEM((2, 8, 256), F32), pltpu.VMEM((3, 16, 128), F32),
+            pltpu.VMEM((9, 8, 256), F32), pltpu.VMEM((2, PACK, 128), F32),
+            pltpu.SemaphoreType.DMA((3,)),
+        ],
+        specs=[pl.BlockSpec(memory_space=pltpu.HBM)] * 3, grant=MOST,
     )(lines, cotangent, taps)
-    kernels = lax.all_to_all(packed, "chan", 0, 0, tiled=True)
     near = lax.ppermute(edge, "rows", beside(8))
     far = lax.ppermute(edge, "rows", inward(8))
     other = lax.ppermute(lines, "rows", partner(8))
     other_c = lax.ppermute(cotangent, "rows", partner(8))
-    packed = call(pack_kernel, shape(32, 32, 128), 4, [wide, flat])(lines, other, near, far)
+    kernels = lax.all_to_all(packed, "chan", 0, 0, tiled=True)
+    near, far, other, other_c, kernels = lax.optimization_barrier((near, far, other, other_c, kernels))
+    packed = call(pack_kernel, shape(32, 32, 128), 4, [pltpu.VMEM((ROWS + 4, 8, 512), F32), flat])(
+        lines, other, near, far
+    )
     recv = lax.all_to_all(packed, "chan", 0, 0, tiled=True)
 
-    tall, side = call(column_kernel, (shape(50, 16, 128), shape(50, 128)), 4)(
+    tall, side = call(column_kernel, (shape(FINE, 16, 128), shape(FINE + 2, 128)), 4)(
         cotangent, other_c, near, far
     )
-    side = lax.ppermute(side, "chan", beside(32))
+    near_side = lax.ppermute(side, "chan", beside(32))
+    far_side = lax.ppermute(side, "chan", inward(32))
     other_tall = lax.ppermute(tall, "chan", partner(32))
-    other_side = lax.ppermute(side, "chan", partner(32))
     s_high, s_low, grad = call(
         window_kernel,
         (shape(FLAT, 512, dtype=BF16), shape(FLAT, 512, dtype=BF16), shape(64, FLAT)), 5,
-        [pltpu.VMEM((2 * ROWS + 2, 48, 128), F32), pltpu.VMEM((FLAT, 512), F32)],
+        [pltpu.VMEM((FINE, 48, 128), F32), pltpu.VMEM((FLAT, 512), F32)],
         3 * 10**8, 3 * 10**6,
-    )(tall, other_tall, side, other_side, jnp.transpose(weight_out, (1, 2, 0, 3)).reshape(2304, 128))
+    )(tall, other_tall, near_side, far_side, jnp.transpose(weight_out, (1, 2, 0, 3)).reshape(2304, 128))
 
     sent = call(
         main_kernel, shape(32 * BACK, 128), 5,
@@ -322,17 +348,17 @@
     )(recv.reshape(1024, 128), kernels.reshape(32 * PACK, 128), s_high, s_low, grad)
     back = lax.all_to_all(sent.reshape(32, BACK, 128), "chan", 0, 0, tiled=True)
 
-    sums, own, given, close, away = call(
+    sums, own, given = call(
         lambda *refs: gather_kernel(scale, *refs),
-        (shape(8, 112, 128), shape(12, 8, 256), shape(12, 8, 256), shape(8, 256), shape(8, 256)), 1,
-        [wide, flat, pltpu.VMEM((56, 128), F32), pltpu.VMEM((112, 128), F32)],
+        (shape(8, 112, 128), shape(12, 8, 256), shape(12, 8, 256)), 1,
+        [
+            pltpu.VMEM((ROWS, 8, 512), F32), flat,
+            pltpu.VMEM((56, 128), F32), pltpu.VMEM((112, 128), F32),
+        ],
     )(back)
     given = lax.ppermute(given, "rows", partner(8))
-    close = lax.ppermute(close, "rows", beside(8))
-    away = lax.ppermute(away, "rows", outward(8))
     sums = lax.all_to_all(sums, "rows", 0, 0, tiled=True)
-    place = (jnp.arange(12) == 11 * parity)[:, None, None]
-    grad_image = jnp.transpose((own + given) + jnp.where(place, (close + away)[None], 0.0), (1, 0, 2))
+    grad_image = jnp.transpose(own + given, (1, 0, 2))
     into, onto = call(final_kernel, (shape(9, 8, 256), shape(9, 8, 128)), 1)(sums)
     grad_in = jnp.transpose(into.reshape(3, 3, 8, 256), (2, 0, 1, 3))
     grad_out = jnp.transpose(onto.reshape(3, 3, 8, 128), (2, 0, 1, 3))

time: 116 us -> 102 us (0.88)
  blocking collectives: 50.8 us -> 28.3 us
  starting transfers between devices: 29.6 us -> 34.9 us
  waiting for transfers between devices: 23.2 us -> 27.7 us
  local copies, waits for them, and re-layouts: 2.71 us -> 0.01 us
  Pallas kernels: 7.59 us -> 9.41 us
    all_to_all x1 -> x0, blocking collectives: 20.4 us -> none  [local(): recv = lax.all_to_all(packed, 'chan', 0, 0, tiled=True)]
    ppermute x1, waiting for transfers between devices: 6.11 us -> 11.6 us  [local(): given = lax.ppermute(given, 'rows', partner(8))]
    ppermute x1, waiting for transfers between devices: 5 us -> 0.01 us  [local(): other_c = lax.ppermute(cotangent, 'rows', partner(8))]
    all_to_all x0 -> x1, starting transfers between devices: none -> 4.71 us  [local(): recv = lax.all_to_all(packed, 'chan', 0, 0, tiled=True)]
    all_to_all x1, starting transfers between devices: 4 us -> 8.6 us  [local(): kernels = lax.all_to_all(packed, 'chan', 0, 0, tiled=True)]
    ppermute x4 -> x2, starting transfers between devices: 9.64 us -> 5.71 us  [the longest x1 3.4 us: local(): far_side = lax.ppermute(side, 'chan', inward(32))]
    all_to_all x1, starting transfers between devices: 6.59 us -> 10.3 us  [local(): sums = lax.all_to_all(sums, 'rows', 0, 0, tiled=True)]
    all_to_all x1, waiting for transfers between devices: 0.01 us -> 3.16 us  [local(): kernels = lax.all_to_all(packed, 'chan', 0, 0, tiled=True)]
  transfers between devices with their start and end apart: 12 -> 11, of which waited for: 7 -> 8; matrix products, arithmetic and copies ran while one was open for 1% -> 1% of each run, Pallas kernels for 2% -> 1%
where the time goes in v2:
time: 102 us
  starting transfers between devices  34.9 us (34%)
  blocking collectives  28.3 us (28%)
  waiting for transfers between devices  27.7 us (27%)
  Pallas kernels  9.41 us (9%)
    all_to_all x1, blocking collectives, local(): back = lax.all_to_all(sent.reshape(32, BACK, 128), 'chan', 0, 0, tiled=True)  28.3 us
    ppermute x1, waiting for transfers between devices, local(): given = lax.ppermute(given, 'rows', partner(8))  11.6 us
    all_to_all x1, starting transfers between devices, local(): sums = lax.all_to_all(sums, 'rows', 0, 0, tiled=True)  10.3 us
    all_to_all x1, starting transfers between devices, local(): kernels = lax.all_to_all(packed, 'chan', 0, 0, tiled=True)  8.6 us
    ppermute x1, waiting for transfers between devices, local(): far = lax.ppermute(edge, 'rows', inward(8))  4.82 us
    all_to_all x1, starting transfers between devices, local(): recv = lax.all_to_all(packed, 'chan', 0, 0, tiled=True)  4.71 us
    ppermute x1, starting transfers between devices, local(): far_side = lax.ppermute(side, 'chan', inward(32))  3.4 us
    all_to_all x1, waiting for transfers between devices, local(): kernels = lax.all_to_all(packed, 'chan', 0, 0, tiled=True)  3.16 us
  transfers between devices with their start and end apart: 11, of which 8 were waited for; matrix products, arithmetic and copies ran while one was open for 1% of the time, Pallas kernels for 1%

profile of v2, /device:TPU:1, one launch (start us, length us, event | category | flops | bytes accessed | tf_op | source)
XLA Modules:
  0.0 101.7 jit_solution(8095147367076612270)
XLA Ops:
  0.7 1.9 %shard_map.67 = (f32[80,128]{1,0:T(8,128)}, f32[32,40,128]{2,1,0:T(8,128)}) custom-call(f32[12,8,256]{2,1,0:T(8,128)} %bitcast.22, f32[24,16,128]{2,1,0:T(8,128)} %own.1, f32[9,8,256]{2,1,0:T(8,128)} %bitcast.25), custom_call_target="tpu_custom_call" | custom-call | flops 1000000 | bytes 1000000 | tf_op jit(solution)/shard_map/pallas_call | solution.py:307
  2.5 8.6 %all-to-all-start = ((f32[32,40,128]{2,1,0:T(8,128)}), f32[32,40,128]{2,1,0:T(8,128)S(1)}, u32[]{:S(2)}, u32[]{:S(2)}) async-start(f32[32,40,128]{2,1,0:T(8,128)} %get-tuple-element.21), calls=%async_computation | async-start | bytes 1310720 | tf_op jit(solution)/shard_map/all_to_all | solution.py:320
  11.2 0.0 copy-start
  11.2 1.7 %collective-permute-start.3 = (f32[24,16,128]{2,1,0:T(8,128)S(1)}, f32[24,16,128]{2,1,0:T(8,128)S(1)}, u32[]{:S(2)}, u32[]{:S(2)}) collective-permute-start(f32[24,16,128]{2,1,0:T(8,128)S(1)} %copy-done.1), channel_id=1, source_target_pairs={{0,32},{32,0},{64,96},{96,64},{128,160},{160,128},{192,224},{224,1... | collective-permute-start | bytes 589832 | tf_op jit(solution)/shard_map/ppermute | solution.py:319
  12.9 0.1 collective-permute-start.2
  13.0 1.3 %collective-permute-start.1 = (f32[80,128]{1,0:T(8,128)}, f32[80,128]{1,0:T(8,128)S(1)}, u32[]{:S(2)}, u32[]{:S(2)}) collective-permute-start(f32[80,128]{1,0:T(8,128)} %get-tuple-element.20), channel_id=1, source_target_pairs={{32,96},{96,160},{160,224},{64,0},{128,64},{192,128},{33,97},{97,1... | collective-permute-start | bytes 122888 | tf_op jit(solution)/shard_map/ppermute | solution.py:317
  14.3 0.7 collective-permute-start
  15.0 4.8 %collective-permute-done.1.far = f32[80,128]{1,0:T(8,128)S(1)} collective-permute-done((f32[80,128]{1,0:T(8,128)}, f32[80,128]{1,0:T(8,128)S(1)}, u32[]{:S(2)}, u32[]{:S(2)}) %collective-permute-start.1) | collective-permute-done | bytes 40992 | tf_op jit(solution)/shard_map/ppermute | solution.py:317
  19.8 0.0 collective-permute-done.near
  19.8 1.1 %collective-permute-done.2.other = f32[12,8,256]{2,1,0:T(8,128)S(1)} collective-permute-done((f32[12,8,256]{2,1,0:T(8,128)S(1)}, f32[12,8,256]{2,1,0:T(8,128)S(1)}, u32[]{:S(2)}, u32[]{:S(2)}) %collective-permute-start.2) | collective-permute-done | bytes 98336 | tf_op jit(solution)/shard_map/ppermute | solution.py:318
  20.9 0.0 collective-permute-done.3.other
  20.9 3.2 %all-to-all-done = f32[32,40,128]{2,1,0:T(8,128)S(1)} async-done(((f32[32,40,128]{2,1,0:T(8,128)}), f32[32,40,128]{2,1,0:T(8,128)S(1)}, u32[]{:S(2)}, u32[]{:S(2)}) %all-to-all-start) | async-done | bytes 655392 | tf_op jit(solution)/shard_map/all_to_all | solution.py:320
  24.1 1.6 %shard_map.68 = f32[32,32,128]{2,1,0:T(8,128)} custom-call(f32[12,8,256]{2,1,0:T(8,128)S(1)} %bitcast.24, f32[12,8,256]{2,1,0:T(8,128)S(1)} %collective-permute-done.2.other, f32[80,128]{1,0:T(8,128)S(1)} %collective-permute-done.near, f32[80,128]{1,0:T(8,128)S(1)} %collective-permute-done.1.far), custom_call_target="tpu_custom_call" | custom-call | flops 1000000 | bytes 1000000 | tf_op jit(solution)/shard_map/pallas_call | solution.py:322
  25.7 4.7 %all-to-all-start.1 = ((f32[32,32,128]{2,1,0:T(8,128)}), f32[32,32,128]{2,1,0:T(8,128)S(1)}, u32[]{:S(2)}, u32[]{:S(2)}) async-start(f32[32,32,128]{2,1,0:T(8,128)} %shard_map.68), calls=%async_computation.1 | async-start | bytes 1048576 | tf_op jit(solution)/shard_map/all_to_all | solution.py:325
  30.4 0.1 shard_map.69
  30.5 0.3 collective-permute-start.4
  30.8 3.4 %collective-permute-start.6 = (f32[56,128]{1,0:T(8,128)S(1)}, f32[56,128]{1,0:T(8,128)S(1)}, u32[]{:S(2)}, u32[]{:S(2)}) collective-permute-start(f32[56,128]{1,0:T(8,128)S(1)} %get-tuple-element.28), channel_id=1, source_target_pairs={{1,3},{3,5},{5,7},{7,9},{9,11},{11,13},{13,15},{15,17},{17,19},{19... | collective-permute-start | bytes 86024 | tf_op jit(solution)/shard_map/ppermute | solution.py:331
  34.2 2.3 %collective-permute-start.5 = (f32[56,128]{1,0:T(8,128)S(1)}, f32[56,128]{1,0:T(8,128)S(1)}, u32[]{:S(2)}, u32[]{:S(2)}) collective-permute-start(f32[56,128]{1,0:T(8,128)S(1)} %get-tuple-element.28), channel_id=1, source_target_pairs={{1,2},{3,4},{5,6},{7,8},{9,10},{11,12},{13,14},{15,16},{17,18},{19... | collective-permute-start | bytes 86024 | tf_op jit(solution)/shard_map/ppermute | solution.py:330
  36.5 0.4 collective-permute-done.6.far
  36.9 2.8 %collective-permute-done.5.near = f32[56,128]{1,0:T(8,128)S(1)} collective-permute-done((f32[56,128]{1,0:T(8,128)S(1)}, f32[56,128]{1,0:T(8,128)S(1)}, u32[]{:S(2)}, u32[]{:S(2)}) %collective-permute-start.5) | collective-permute-done | bytes 28704 | tf_op jit(solution)/shard_map/ppermute | solution.py:330
  39.7 0.0 collective-permute-done.4.other
  39.7 1.0 %shard_map.70 = (bf16[512,512]{1,0:T(8,128)(2,1)S(1)}, bf16[512,512]{1,0:T(8,128)(2,1)S(1)}, f32[64,512]{1,0:T(8,128)S(1)}) custom-call(f32[54,16,128]{2,1,0:T(8,128)S(1)} %get-tuple-element.27.own, f32[54,16,128]{2,1,0:T(8,128)S(1)} %collective-permute-done.4.other, f32[56,128]{1,0:T(8,128)S(1)} %collective-permute-done.5.near, ...), custom_call_target="tpu_custom_call" | custom-call | flops 300000000 | bytes 3000000 | tf_op jit(solution)/shard_map/pallas_call | solution.py:333
  40.7 1.2 %all-to-all-done.1 = f32[32,32,128]{2,1,0:T(8,128)S(1)} async-done(((f32[32,32,128]{2,1,0:T(8,128)}), f32[32,32,128]{2,1,0:T(8,128)S(1)}, u32[]{:S(2)}, u32[]{:S(2)}) %all-to-all-start.1) | async-done | bytes 524320 | tf_op jit(solution)/shard_map/all_to_all | solution.py:325
  41.9 2.7 %shard_map.71 = f32[2816,128]{1,0:T(8,128)S(1)} custom-call(f32[1024,128]{1,0:T(8,128)S(1)} %bitcast.20, f32[1280,128]{1,0:T(8,128)S(1)} %bitcast.19, bf16[512,512]{1,0:T(8,128)(2,1)S(1)} %get-tuple-element.29.s_high, bf16[512,512]{1,0:T(8,128)(2,1)S(1)} %get-tuple-element.30.s_low, f32[64,512]{1,0:T(8,128)S(1)} %get-tuple-element.31.grad), custom_call_target="tpu_custom_call" | custom-call | flops 1000000000 | bytes 5000000 | tf_op jit(solution)/shard_map/pallas_call | solution.py:340
  44.7 28.3 %all_to_all.20.refs_0_ = f32[32,88,128]{2,1,0:T(8,128)S(1)} all-to-all(f32[32,88,128]{2,1,0:T(8,128)S(1)} %bitcast.18), channel_id=1, replica_groups=mesh['rows'=8,'chan'=32] {'chan'}, dimensions={0} | all-to-all | bytes 2883584 | tf_op jit(solution)/shard_map/all_to_all | solution.py:349
  73.0 1.4 %shard_map.72 = (f32[8,112,128]{2,1,0:T(8,128)}, f32[12,8,256]{2,1,0:T(8,128)S(1)}, f32[12,8,256]{2,1,0:T(8,128)S(1)}) custom-call(f32[32,88,128]{2,1,0:T(8,128)S(1)} %all_to_all.20.refs_0_), custom_call_target="tpu_custom_call" | custom-call | flops 1000000 | bytes 1000000 | tf_op jit(solution)/shard_map/pallas_call | solution.py:351
  74.3 10.3 %all-to-all-start.3 = ((f32[8,112,128]{2,1,0:T(8,128)}), f32[8,112,128]{2,1,0:T(8,128)S(1)}, u32[]{:S(2)}, u32[]{:S(2)}) async-start(f32[8,112,128]{2,1,0:T(8,128)} %get-tuple-element.34), calls=%async_computation.3 | async-start | bytes 917504 | tf_op jit(solution)/shard_map/all_to_all | solution.py:360
  84.7 1.5 %collective-permute-start.7 = (f32[12,8,256]{2,1,0:T(8,128)S(1)}, f32[12,8,256]{2,1,0:T(8,128)S(1)}, u32[]{:S(2)}, u32[]{:S(2)}) collective-permute-start(f32[12,8,256]{2,1,0:T(8,128)S(1)} %get-tuple-element.33), channel_id=1, source_target_pairs={{0,32},{32,0},{64,96},{96,64},{128,160},{160,128},{192,224},{224,1... | collective-permute-start | bytes 294920 | tf_op jit(solution)/shard_map/ppermute | solution.py:359
  86.2 11.6 %collective-permute-done.7 = f32[12,8,256]{2,1,0:T(8,128)S(1)} collective-permute-done((f32[12,8,256]{2,1,0:T(8,128)S(1)}, f32[12,8,256]{2,1,0:T(8,128)S(1)}, u32[]{:S(2)}, u32[]{:S(2)}) %collective-permute-start.7) | collective-permute-done | bytes 98336 | tf_op jit(solution)/shard_map/ppermute | solution.py:359
  97.8 0.7 add_bitcast_fusion
  98.5 2.6 %all-to-all-done.3.recv = f32[8,112,128]{2,1,0:T(8,128)S(1)} async-done(((f32[8,112,128]{2,1,0:T(8,128)}), f32[8,112,128]{2,1,0:T(8,128)S(1)}, u32[]{:S(2)}, u32[]{:S(2)}) %all-to-all-start.3) | async-done | bytes 458784 | tf_op jit(solution)/shard_map/all_to_all | solution.py:360
  101.0 0.7 shard_map.73
  (5 shorter events, 0.0 us)
Async XLA Ops:
  0.6 10.5 %copy-start.1 = (f32[24,16,128]{2,1,0:T(8,128)S(1)}, f32[24,16,128]{2,1,0:T(8,128)}, u32[]{:S(2)}) copy-start(f32[24,16,128]{2,1,0:T(8,128)} %own.1) | copy-start | bytes 589828
  0.6 12.3 %copy-start.2 = (f32[8,12,256]{2,0,1:T(8,128)S(1)}, f32[8,12,256]{2,0,1:T(8,128)}, u32[]{:S(2)}) copy-start(f32[8,12,256]{2,0,1:T(8,128)} %param.4) | copy-start | bytes 294916
  2.5 21.5 %all-to-all-start = ((f32[32,40,128]{2,1,0:T(8,128)}), f32[32,40,128]{2,1,0:T(8,128)S(1)}, u32[]{:S(2)}, u32[]{:S(2)}) async-start(f32[32,40,128]{2,1,0:T(8,128)} %get-tuple-element.21), calls=%async_computation | async-start | bytes 1310720 | tf_op jit(solution)/shard_map/all_to_all | solution.py:320
  11.2 28.5 %copy-start = (f32[256,3,3,128]{3,0,2,1:T(8,128)S(1)}, f32[256,3,3,128]{3,0,2,1:T(8,128)}, u32[]{:S(2)}) copy-start(f32[256,3,3,128]{3,0,2,1:T(8,128)} %param.6) | copy-start | bytes 3538948
  11.2 9.7 %collective-permute-start.3 = (f32[24,16,128]{2,1,0:T(8,128)S(1)}, f32[24,16,128]{2,1,0:T(8,128)S(1)}, u32[]{:S(2)}, u32[]{:S(2)}) collective-permute-start(f32[24,16,128]{2,1,0:T(8,128)S(1)} %copy-done.1), channel_id=1, source_target_pairs={{0,32},{32,0},{64,96},{96,64},{128,160},{160,128},{192,224},{224,1... | collective-permute-start | bytes 589832 | tf_op jit(solution)/shard_map/ppermute | solution.py:319
  12.9 8.0 %collective-permute-start.2 = (f32[12,8,256]{2,1,0:T(8,128)S(1)}, f32[12,8,256]{2,1,0:T(8,128)S(1)}, u32[]{:S(2)}, u32[]{:S(2)}) collective-permute-start(f32[12,8,256]{2,1,0:T(8,128)S(1)} %bitcast.23), channel_id=1, source_target_pairs={{0,32},{32,0},{64,96},{96,64},{128,160},{160,128},{192,224},{224,1... | collective-permute-start | bytes 294920 | tf_op jit(solution)/shard_map/ppermute | solution.py:318
  13.0 6.8 %collective-permute-start.1 = (f32[80,128]{1,0:T(8,128)}, f32[80,128]{1,0:T(8,128)S(1)}, u32[]{:S(2)}, u32[]{:S(2)}) collective-permute-start(f32[80,128]{1,0:T(8,128)} %get-tuple-element.20), channel_id=1, source_target_pairs={{32,96},{96,160},{160,224},{64,0},{128,64},{192,128},{33,97},{97,1... | collective-permute-start | bytes 122888 | tf_op jit(solution)/shard_map/ppermute | solution.py:317
  14.3 5.5 %collective-permute-start = (f32[80,128]{1,0:T(8,128)}, f32[80,128]{1,0:T(8,128)S(1)}, u32[]{:S(2)}, u32[]{:S(2)}) collective-permute-start(f32[80,128]{1,0:T(8,128)} %get-tuple-element.20), channel_id=1, source_target_pairs={{32,64},{96,128},{160,192},{64,32},{128,96},{192,160},{33,65},{97,... | collective-permute-start | bytes 122888 | tf_op jit(solution)/shard_map/ppermute | solution.py:316
  25.7 16.3 %all-to-all-start.1 = ((f32[32,32,128]{2,1,0:T(8,128)}), f32[32,32,128]{2,1,0:T(8,128)S(1)}, u32[]{:S(2)}, u32[]{:S(2)}) async-start(f32[32,32,128]{2,1,0:T(8,128)} %shard_map.68), calls=%async_computation.1 | async-start | bytes 1048576 | tf_op jit(solution)/shard_map/all_to_all | solution.py:325
  30.5 9.2 %collective-permute-start.4 = (f32[54,16,128]{2,1,0:T(8,128)S(1)}, f32[54,16,128]{2,1,0:T(8,128)S(1)}, u32[]{:S(2)}, u32[]{:S(2)}) collective-permute-start(f32[54,16,128]{2,1,0:T(8,128)S(1)} %get-tuple-element.27.own), channel_id=1, source_target_pairs={{0,1},{1,0},{2,3},{3,2},{4,5},{5,4},{6,7},{7,6},{8,9},{9,8},{10,11... | collective-permute-start | bytes 1327112 | tf_op jit(solution)/shard_map/ppermute | solution.py:332
  30.8 6.1 %collective-permute-start.6 = (f32[56,128]{1,0:T(8,128)S(1)}, f32[56,128]{1,0:T(8,128)S(1)}, u32[]{:S(2)}, u32[]{:S(2)}) collective-permute-start(f32[56,128]{1,0:T(8,128)S(1)} %get-tuple-element.28), channel_id=1, source_target_pairs={{1,3},{3,5},{5,7},{7,9},{9,11},{11,13},{13,15},{15,17},{17,19},{19... | collective-permute-start | bytes 86024 | tf_op jit(solution)/shard_map/ppermute | solution.py:331
  34.2 5.5 %collective-permute-start.5 = (f32[56,128]{1,0:T(8,128)S(1)}, f32[56,128]{1,0:T(8,128)S(1)}, u32[]{:S(2)}, u32[]{:S(2)}) collective-permute-start(f32[56,128]{1,0:T(8,128)S(1)} %get-tuple-element.28), channel_id=1, source_target_pairs={{1,2},{3,4},{5,6},{7,8},{9,10},{11,12},{13,14},{15,16},{17,18},{19... | collective-permute-start | bytes 86024 | tf_op jit(solution)/shard_map/ppermute | solution.py:330
  74.3 26.7 %all-to-all-start.3 = ((f32[8,112,128]{2,1,0:T(8,128)}), f32[8,112,128]{2,1,0:T(8,128)S(1)}, u32[]{:S(2)}, u32[]{:S(2)}) async-start(f32[8,112,128]{2,1,0:T(8,128)} %get-tuple-element.34), calls=%async_computation.3 | async-start | bytes 917504 | tf_op jit(solution)/shard_map/all_to_all | solution.py:360
  84.7 13.1 %collective-permute-start.7 = (f32[12,8,256]{2,1,0:T(8,128)S(1)}, f32[12,8,256]{2,1,0:T(8,128)S(1)}, u32[]{:S(2)}, u32[]{:S(2)}) collective-permute-start(f32[12,8,256]{2,1,0:T(8,128)S(1)} %get-tuple-element.33), channel_id=1, source_target_pairs={{0,32},{32,0},{64,96},{96,64},{128,160},{160,128},{192,224},{224,1... | collective-permute-start | bytes 294920 | tf_op jit(solution)/shard_map/ppermute | solution.py:359

commit v3 on v2

--- a/solution.py
+++ b/solution.py
@@ -11,7 +11,7 @@
 FINE = 2 * ROWS + 6
 FLAT = 512
 PACK = 40
-BACK = 88
+BACK = 56
 F32, BF16 = jnp.float32, jnp.bfloat16
 GRANT, MOST = 20 * 1024 * 1024, 60 * 1024 * 1024
 FULL = pl.BlockSpec(memory_space=pltpu.VMEM)
@@ -162,7 +162,7 @@
     return STEP * (t // 3 == 0) + (t % 3 == 0)
 
 
-def main_kernel(recv, kernels, s_high, s_low, grad, out, x_high, x_low, w_high, w_low, g_high, g_low):
+def main_kernel(recv, kernels, s_high, s_low, grad, out, mine, theirs, x_high, x_low, w_high, w_low, g_high, g_low):
     for pair in range(16):
         for q in range(4):
             tile = jnp.concatenate(
@@ -210,7 +210,7 @@
     for t in range(9):
         for h in range(2):
             for j in range(2):
-                out[pl.ds(32 + (t * 2 + h) * 2 + j, 32, stride=BACK), :] = into[
+                out[pl.ds((t * 2 + h) * 2 + j, 32, stride=BACK), :] = into[
                     t * 64 + j * 32 : t * 64 + j * 32 + 32, h * 128 : h * 128 + 128
                 ]
     shifts = [0, 1, STEP, STEP + 1]
@@ -219,55 +219,61 @@
     for t in range(9):
         at, kind = shifts.index(shift_of(t)) * 64, kind_of(t)
         for j in range(2):
-            out[pl.ds(68 + t * 2 + j, 32, stride=BACK), :] = onto[
+            out[pl.ds(36 + t * 2 + j, 32, stride=BACK), :] = onto[
                 at + j * 32 : at + j * 32 + 32, kind * 128 : kind * 128 + 128
             ]
     back = product(weights, stack(jnp.where(around, gradient, 0.0), -2 * STEP), TN)
-    for d in range(32):
-        for q in range(4):
-            out[pl.ds(d * BACK + q * 8, 8), :] = back[d * 8 : d * 8 + 8, q * 128 : q * 128 + 128]
+    half = ROWS // 2 * STEP
+    first = lax.axis_index("rows") % 2 == 0
+    upper, lower = back[:, 0:256], pltpu.roll(back, FLAT - half, 1)[:, 0:256]
+    for dst, part in (
+        (mine, jnp.where(first, upper, lower)),
+        (theirs, jnp.where(first, lower, upper)),
+    ):
+        for d in range(32):
+            for q in range(2):
+                dst[pl.ds(d * 16 + q * 8, 8), :] = part[d * 8 : d * 8 + 8, q * 128 : q * 128 + 128]
     blank = jnp.zeros((2, 128), F32)
     for d in range(32):
-        out[pl.ds(d * BACK + 86, 2), :] = blank
-
-
-def gather_kernel(scale, recv, weights, mine, theirs, image, line, total, mixed):
-    parity = lax.axis_index("rows") % 2
+        out[pl.ds(d * BACK + 54, 2), :] = blank
+
+
+def weights_kernel(scale, recv, mixed, total):
     mixed[...] = jnp.zeros_like(mixed)
     for core in range(2):
-        each = recv[core, 32:BACK, :]
+        each = recv[core]
         for block in range(1, 16):
-            each = each + recv[2 * block + core, 32:BACK, :]
+            each = each + recv[2 * block + core]
         total[...] = each * scale
         for j in range(2):
             mixed[pl.ds(2 * core + j, 27, stride=4), :] = total[pl.ds(j, 27, stride=2), :]
-    tile = mixed[...]
-    for z in range(8):
-        weights[z] = tile
-    image[...] = jnp.zeros_like(image)
-    for block in range(16):
-        start = 127 + BLOCK * block
-        for q in range(4):
-            at = slice(q * 8, q * 8 + 8)
-            line[:, q * 128 : q * 128 + 128] = recv[2 * block, at, :] + recv[2 * block + 1, at, :]
-        for r in range(ROWS):
-            image[r, :, start : start + STEP] += line[:, r * STEP : (r + 1) * STEP]
-    half = ROWS // 2
-    for i in range(half):
-        mine[i] = image[half * parity + i, :, 128:384]
-        theirs[i] = image[half * (1 - parity) + i, :, 128:384]
-
-
-def final_kernel(recv, into, onto):
-    sums = []
-    for parity in range(2):
-        sums.append((recv[parity] + recv[2 + parity]) + (recv[4 + parity] + recv[6 + parity]))
+
+
+def final_kernel(own, other, into, onto):
+    first = lax.axis_index("rows") % 2 == 0
+    sums = (
+        jnp.where(first, own[...], other[...]),
+        jnp.where(first, other[...], own[...]),
+    )
     for k in range(27):
         tile = jnp.concatenate([x[4 * k : 4 * k + 4] for x in sums], axis=0)
         if k < 18:
             into[k // 2, :, (k % 2) * 128 : (k % 2) * 128 + 128] = tile
         else:
             onto[k - 18] = tile
+
+
+def image_kernel(recv, out, image, line):
+    image[...] = jnp.zeros_like(image)
+    for block in range(16):
+        start = 127 + BLOCK * block
+        for q in range(2):
+            at = slice(q * 8, q * 8 + 8)
+            line[:, q * 128 : q * 128 + 128] = recv[2 * block, at, :] + recv[2 * block + 1, at, :]
+        for r in range(ROWS // 2):
+            image[r, :, start : start + STEP] += line[:, r * STEP : (r + 1) * STEP]
+    for r in range(ROWS // 2):
+        out[r] = image[r, :, 128:384]
 
 
 def shape(*dims, dtype=F32):
@@ -296,6 +302,10 @@
 
 def inward(n):
     return [(i, i + 2) for i in range(1, n - 2, 2)] + [(i, i - 2) for i in range(2, n, 2)]
+
+
+def shifted(n, by):
+    return [(i, (i + by) % n) for i in range(n)]
 
 
 def local(features, weight_in, weight_out, cotangent):
@@ -337,8 +347,8 @@
         3 * 10**8, 3 * 10**6,
     )(tall, other_tall, near_side, far_side, jnp.transpose(weight_out, (1, 2, 0, 3)).reshape(2304, 128))
 
-    sent = call(
-        main_kernel, shape(32 * BACK, 128), 5,
+    sent, own, given = call(
+        main_kernel, (shape(32 * BACK, 128), shape(512, 128), shape(512, 128)), 5,
         [
             pltpu.VMEM((256, FLAT), BF16), pltpu.VMEM((256, FLAT), BF16),
             pltpu.VMEM((576, 256), BF16), pltpu.VMEM((576, 256), BF16),
@@ -346,20 +356,23 @@
         ],
         10**9, 5 * 10**6,
     )(recv.reshape(1024, 128), kernels.reshape(32 * PACK, 128), s_high, s_low, grad)
+    given = lax.ppermute(given, "rows", partner(8))
     back = lax.all_to_all(sent.reshape(32, BACK, 128), "chan", 0, 0, tiled=True)
-
-    sums, own, given = call(
-        lambda *refs: gather_kernel(scale, *refs),
-        (shape(8, 112, 128), shape(12, 8, 256), shape(12, 8, 256)), 1,
-        [
-            pltpu.VMEM((ROWS, 8, 512), F32), flat,
-            pltpu.VMEM((56, 128), F32), pltpu.VMEM((112, 128), F32),
-        ],
-    )(back)
-    given = lax.ppermute(given, "rows", partner(8))
-    sums = lax.all_to_all(sums, "rows", 0, 0, tiled=True)
-    grad_image = jnp.transpose(own + given, (1, 0, 2))
-    into, onto = call(final_kernel, (shape(9, 8, 256), shape(9, 8, 128)), 1)(sums)
+    given, back = lax.optimization_barrier((given, back))
+    mixed = call(lambda *refs: weights_kernel(scale, *refs), shape(112, 128), 1, [pltpu.VMEM((56, 128), F32)])(
+        back
+    )
+    left = lax.ppermute(mixed, "rows", shifted(8, 2))
+    right = lax.ppermute(mixed, "rows", shifted(8, 6))
+    opposite = lax.ppermute(mixed, "rows", shifted(8, 4))
+    image = lax.all_to_all((own + given).reshape(32, 16, 128), "chan", 0, 0, tiled=True)
+    mixed = (mixed + opposite) + (left + right)
+    counter = lax.ppermute(mixed, "rows", partner(8))
+    into, onto = call(final_kernel, (shape(9, 8, 256), shape(9, 8, 128)), 2)(mixed, counter)
+    rows = call(
+        image_kernel, shape(12, 8, 256), 1, [pltpu.VMEM((12, 8, 512), F32), pltpu.VMEM((8, 256), F32)]
+    )(image)
+    grad_image = jnp.transpose(rows, (1, 0, 2))
     grad_in = jnp.transpose(into.reshape(3, 3, 8, 256), (2, 0, 1, 3))
     grad_out = jnp.transpose(onto.reshape(3, 3, 8, 128), (2, 0, 1, 3))
     return (grad_image, grad_in, grad_out)

time: 102 us -> 97.3 us (0.954)
  blocking collectives: 28.3 us -> 0 us
  starting transfers between devices: 34.9 us -> 52.7 us
  waiting for transfers between devices: 27.7 us -> 30.4 us
  local copies, waits for them, and re-layouts: 0.01 us -> 1.86 us
    all_to_all x1 -> x0, blocking collectives: 28.3 us -> none  [local(): back = lax.all_to_all(sent.reshape(32, BACK, 128), 'chan', 0, 0, tiled=True)]
    ppermute x0 -> x4, starting transfers between devices: none -> 12.3 us  [the longest x1 7.27 us: local(): right = lax.ppermute(mixed, 'rows', shifted(8, 6))]
    all_to_all x1 -> x2, waiting for transfers between devices: 2.57 us -> 9.38 us  [the longest x1 4.87 us: local(): lax.all_to_all((own + given).reshape(32, 16, 128), 'chan', 0, 0, tiled=True)]
    ppermute x1, waiting for transfers between devices: 11.6 us -> 6.53 us  [local(): given = lax.ppermute(given, 'rows', partner(8))]
    ppermute x1, starting transfers between devices: 1.46 us -> 4.71 us  [local(): given = lax.ppermute(given, 'rows', partner(8))]
    all_to_all x1 -> x2, starting transfers between devices: 10.3 us -> 12.6 us  [the longest x1 7.81 us: local(): back = lax.all_to_all(sent.reshape(32, BACK, 128), 'chan', 0, 0, tiled=True)]
    ppermute x0 -> x4, waiting for transfers between devices: none -> 1.87 us  [the longest x1 1.86 us: local(): counter = lax.ppermute(mixed, 'rows', partner(8))]
    unnamed x6 -> x12, local copies, waits for them, and re-layouts: 0.01 us -> 1.86 us
  transfers between devices with their start and end apart: 11 -> 16, of which waited for: 8 -> 10; matrix products, arithmetic and copies ran while one was open for 1% -> 1% of each run, Pallas kernels for 1% -> 2%
where the time goes in v3:
time: 97.3 us; the launch traced here: 96.7 us
  starting transfers between devices  52.7 us (54%)
  waiting for transfers between devices  30.4 us (31%)
  Pallas kernels  10.1 us (10%)
  local copies, waits for them, and re-layouts  1.86 us (2%)
    all_to_all x1, starting transfers between devices, local(): kernels = lax.all_to_all(packed, 'chan', 0, 0, tiled=True)  8.6 us
    all_to_all x1, starting transfers between devices, local(): back = lax.all_to_all(sent.reshape(32, BACK, 128), 'chan', 0, 0, tiled=True)  7.81 us
    ppermute x1, starting transfers between devices, local(): right = lax.ppermute(mixed, 'rows', shifted(8, 6))  7.27 us
    ppermute x1, waiting for transfers between devices, local(): given = lax.ppermute(given, 'rows', partner(8))  6.53 us
    all_to_all x1, waiting for transfers between devices, local(): lax.all_to_all((own + given).reshape(32, 16, 128), 'chan', 0, 0, tiled=True)  4.87 us
    all_to_all x1, starting transfers between devices, local(): lax.all_to_all((own + given).reshape(32, 16, 128), 'chan', 0, 0, tiled=True)  4.75 us
    ppermute x1, starting transfers between devices, local(): given = lax.ppermute(given, 'rows', partner(8))  4.71 us
    all_to_all x1, starting transfers between devices, local(): recv = lax.all_to_all(packed, 'chan', 0, 0, tiled=True)  4.71 us
  transfers between devices with their start and end apart: 16, of which 10 were waited for; matrix products, arithmetic and copies ran while one was open for 1% of the time, Pallas kernels for 2%

profile of v3, /device:TPU:1, one launch (start us, length us, event | category | flops | bytes accessed | tf_op | source)
XLA Modules:
  0.0 96.7 jit_solution(13993569156703635112)
XLA Ops:
  0.7 1.9 %shard_map.67 = (f32[80,128]{1,0:T(8,128)}, f32[32,40,128]{2,1,0:T(8,128)}) custom-call(f32[12,8,256]{2,1,0:T(8,128)} %bitcast.21, f32[24,16,128]{2,1,0:T(8,128)} %own.1, f32[9,8,256]{2,1,0:T(8,128)} %bitcast.25), custom_call_target="tpu_custom_call" | custom-call | flops 1000000 | bytes 1000000 | tf_op jit(solution)/shard_map/pallas_call | solution.py:317
  2.5 8.6 %all-to-all-start = ((f32[32,40,128]{2,1,0:T(8,128)}), f32[32,40,128]{2,1,0:T(8,128)S(1)}, u32[]{:S(2)}, u32[]{:S(2)}) async-start(f32[32,40,128]{2,1,0:T(8,128)} %get-tuple-element.23), calls=%async_computation | async-start | bytes 1310720 | tf_op jit(solution)/shard_map/all_to_all | solution.py:330
  11.2 1.7 %collective-permute-start.3 = (f32[24,16,128]{2,1,0:T(8,128)S(1)}, f32[24,16,128]{2,1,0:T(8,128)S(1)}, u32[]{:S(2)}, u32[]{:S(2)}) collective-permute-start(f32[24,16,128]{2,1,0:T(8,128)S(1)} %copy-done.1), channel_id=1, source_target_pairs={{0,32},{32,0},{64,96},{96,64},{128,160},{160,128},{192,224},{224,1... | collective-permute-start | bytes 589832 | tf_op jit(solution)/shard_map/ppermute | solution.py:329
  13.0 1.3 %collective-permute-start.1 = (f32[80,128]{1,0:T(8,128)S(1)}, f32[80,128]{1,0:T(8,128)S(1)}, u32[]{:S(2)}, u32[]{:S(2)}) collective-permute-start(f32[80,128]{1,0:T(8,128)S(1)} %copy-done.5), channel_id=1, source_target_pairs={{32,96},{96,160},{160,224},{64,0},{128,64},{192,128},{33,97},{97,1... | collective-permute-start | bytes 122888 | tf_op jit(solution)/shard_map/ppermute | solution.py:327
  14.3 0.7 collective-permute-start
  15.0 4.6 %collective-permute-done.1.far = f32[80,128]{1,0:T(8,128)S(1)} collective-permute-done((f32[80,128]{1,0:T(8,128)S(1)}, f32[80,128]{1,0:T(8,128)S(1)}, u32[]{:S(2)}, u32[]{:S(2)}) %collective-permute-start.1) | collective-permute-done | bytes 40992 | tf_op jit(solution)/shard_map/ppermute | solution.py:327
  19.6 1.3 %collective-permute-done.2.other = f32[12,8,256]{2,1,0:T(8,128)S(1)} collective-permute-done((f32[12,8,256]{2,1,0:T(8,128)S(1)}, f32[12,8,256]{2,1,0:T(8,128)S(1)}, u32[]{:S(2)}, u32[]{:S(2)}) %collective-permute-start.2) | collective-permute-done | bytes 98336 | tf_op jit(solution)/shard_map/ppermute | solution.py:328
  20.9 3.2 %all-to-all-done = f32[32,40,128]{2,1,0:T(8,128)S(1)} async-done(((f32[32,40,128]{2,1,0:T(8,128)}), f32[32,40,128]{2,1,0:T(8,128)S(1)}, u32[]{:S(2)}, u32[]{:S(2)}) %all-to-all-start) | async-done | bytes 655392 | tf_op jit(solution)/shard_map/all_to_all | solution.py:330
  24.1 1.6 %shard_map.68 = f32[32,32,128]{2,1,0:T(8,128)} custom-call(f32[12,8,256]{2,1,0:T(8,128)S(1)} %bitcast.23, f32[12,8,256]{2,1,0:T(8,128)S(1)} %collective-permute-done.2.other, f32[80,128]{1,0:T(8,128)S(1)} %collective-permute-done.near, f32[80,128]{1,0:T(8,128)S(1)} %collective-permute-done.1.far), custom_call_target="tpu_custom_call" | custom-call | flops 1000000 | bytes 1000000 | tf_op jit(solution)/shard_map/pallas_call | solution.py:332
  25.7 4.7 %all-to-all-start.1 = ((f32[32,32,128]{2,1,0:T(8,128)}), f32[32,32,128]{2,1,0:T(8,128)S(1)}, u32[]{:S(2)}, u32[]{:S(2)}) async-start(f32[32,32,128]{2,1,0:T(8,128)} %shard_map.68), calls=%async_computation.1 | async-start | bytes 1048576 | tf_op jit(solution)/shard_map/all_to_all | solution.py:335
  30.8 3.4 %collective-permute-start.6 = (f32[56,128]{1,0:T(8,128)S(1)}, f32[56,128]{1,0:T(8,128)S(1)}, u32[]{:S(2)}, u32[]{:S(2)}) collective-permute-start(f32[56,128]{1,0:T(8,128)S(1)} %get-tuple-element.30), channel_id=1, source_target_pairs={{1,3},{3,5},{5,7},{7,9},{9,11},{11,13},{13,15},{15,17},{17,19},{19... | collective-permute-start | bytes 86024 | tf_op jit(solution)/shard_map/ppermute | solution.py:341
  34.2 2.3 %collective-permute-start.5 = (f32[56,128]{1,0:T(8,128)S(1)}, f32[56,128]{1,0:T(8,128)S(1)}, u32[]{:S(2)}, u32[]{:S(2)}) collective-permute-start(f32[56,128]{1,0:T(8,128)S(1)} %get-tuple-element.30), channel_id=1, source_target_pairs={{1,2},{3,4},{5,6},{7,8},{9,10},{11,12},{13,14},{15,16},{17,18},{19... | collective-permute-start | bytes 86024 | tf_op jit(solution)/shard_map/ppermute | solution.py:340
  36.5 0.4 collective-permute-done.6.far
  36.9 2.8 %collective-permute-done.5.near = f32[56,128]{1,0:T(8,128)S(1)} collective-permute-done((f32[56,128]{1,0:T(8,128)S(1)}, f32[56,128]{1,0:T(8,128)S(1)}, u32[]{:S(2)}, u32[]{:S(2)}) %collective-permute-start.5) | collective-permute-done | bytes 28704 | tf_op jit(solution)/shard_map/ppermute | solution.py:340
  39.7 1.0 %shard_map.70 = (bf16[512,512]{1,0:T(8,128)(2,1)S(1)}, bf16[512,512]{1,0:T(8,128)(2,1)S(1)}, f32[64,512]{1,0:T(8,128)S(1)}) custom-call(f32[54,16,128]{2,1,0:T(8,128)S(1)} %get-tuple-element.29.own, f32[54,16,128]{2,1,0:T(8,128)S(1)} %collective-permute-done.4.other, f32[56,128]{1,0:T(8,128)S(1)} %collective-permute-done.5.near, ...), custom_call_target="tpu_custom_call" | custom-call | flops 300000000 | bytes 3000000 | tf_op jit(solution)/shard_map/pallas_call | solution.py:343
  40.8 0.8 copy-done.3
  41.6 0.4 all-to-all-done.1
  41.9 1.0 %copy-done.4 = bf16[512,512]{1,0:T(8,128)(2,1)S(1)} copy-done((bf16[512,512]{1,0:T(8,128)(2,1)S(1)}, bf16[512,512]{1,0:T(8,128)(2,1)}, u32[]{:S(2)}) %copy-start.4) | copy-done | bytes 524312
  43.0 3.7 %shard_map.71 = (f32[1792,128]{1,0:T(8,128)}, f32[512,128]{1,0:T(8,128)S(1)}, f32[512,128]{1,0:T(8,128)S(1)}) custom-call(f32[1024,128]{1,0:T(8,128)S(1)} %bitcast.20, f32[1280,128]{1,0:T(8,128)S(1)} %bitcast.19, bf16[512,512]{1,0:T(8,128)(2,1)S(1)} %get-tuple-element.31.s_high, bf16[512,512]{1,0:T(8,128)(2,1)S(1)} %copy-done.4, ...), custom_call_target="tpu_custom_call" | custom-call | flops 1000000000 | bytes 5000000 | tf_op jit(solution)/shard_map/pallas_call | solution.py:350
  46.7 7.8 %all-to-all-start.2 = ((f32[32,56,128]{2,1,0:T(8,128)}), f32[32,56,128]{2,1,0:T(8,128)S(1)}, u32[]{:S(2)}, u32[]{:S(2)}) async-start(f32[32,56,128]{2,1,0:T(8,128)} %bitcast.7), calls=%async_computation.2 | async-start | bytes 1835008 | tf_op jit(solution)/shard_map/all_to_all | solution.py:360
  54.5 4.7 %collective-permute-start.7 = (f32[512,128]{1,0:T(8,128)S(1)}, f32[512,128]{1,0:T(8,128)S(1)}, u32[]{:S(2)}, u32[]{:S(2)}) collective-permute-start(f32[512,128]{1,0:T(8,128)S(1)} %get-tuple-element.35), channel_id=1, source_target_pairs={{0,32},{32,0},{64,96},{96,64},{128,160},{160,128},{192,224},{224,1... | collective-permute-start | bytes 786440 | tf_op jit(solution)/shard_map/ppermute | solution.py:359
  59.3 6.5 %collective-permute-done.7 = f32[512,128]{1,0:T(8,128)S(1)} collective-permute-done((f32[512,128]{1,0:T(8,128)S(1)}, f32[512,128]{1,0:T(8,128)S(1)}, u32[]{:S(2)}, u32[]{:S(2)}) %collective-permute-start.7) | collective-permute-done | bytes 262176 | tf_op jit(solution)/shard_map/ppermute | solution.py:359
  65.8 4.5 %all-to-all-done.2.refs_0_ = f32[32,56,128]{2,1,0:T(8,128)S(1)} async-done(((f32[32,56,128]{2,1,0:T(8,128)}), f32[32,56,128]{2,1,0:T(8,128)S(1)}, u32[]{:S(2)}, u32[]{:S(2)}) %all-to-all-start.2) | async-done | bytes 917536 | tf_op jit(solution)/shard_map/all_to_all | solution.py:360
  70.4 7.3 %collective-permute-start.10 = (f32[112,128]{1,0:T(8,128)S(1)}, f32[112,128]{1,0:T(8,128)S(1)}, u32[]{:S(2)}, u32[]{:S(2)}) collective-permute-start(f32[112,128]{1,0:T(8,128)S(1)} %shard_map.73), channel_id=1, source_target_pairs={{0,192},{32,224},{64,0},{96,32},{128,64},{160,96},{192,128},{224,1... | collective-permute-start | bytes 172040 | tf_op jit(solution)/shard_map/ppermute | solution.py:366
  77.6 3.5 %collective-permute-start.8 = (f32[112,128]{1,0:T(8,128)S(1)}, f32[112,128]{1,0:T(8,128)S(1)}, u32[]{:S(2)}, u32[]{:S(2)}) collective-permute-start(f32[112,128]{1,0:T(8,128)S(1)} %shard_map.73), channel_id=1, source_target_pairs={{0,128},{32,160},{64,192},{96,224},{128,0},{160,32},{192,64},{224,... | collective-permute-start | bytes 172040 | tf_op jit(solution)/shard_map/ppermute | solution.py:367
  81.1 0.7 add.12
  81.9 4.8 %all-to-all-start.3 = ((f32[32,16,128]{2,1,0:T(8,128)}), f32[32,16,128]{2,1,0:T(8,128)S(1)}, u32[]{:S(2)}, u32[]{:S(2)}) async-start(f32[32,16,128]{2,1,0:T(8,128)} %bitcast.8), calls=%async_computation.3 | async-start | bytes 524288 | tf_op jit(solution)/shard_map/all_to_all | solution.py:368
  86.7 1.6 %collective-permute-start.11 = (f32[112,128]{1,0:T(8,128)S(1)}, f32[112,128]{1,0:T(8,128)S(1)}, u32[]{:S(2)}, u32[]{:S(2)}) collective-permute-start(f32[112,128]{1,0:T(8,128)S(1)} %add_add_fusion.own), channel_id=1, source_target_pairs={{0,32},{32,0},{64,96},{96,64},{128,160},{160,128},{192,224},{224,1... | collective-permute-start | bytes 172040 | tf_op jit(solution)/shard_map/ppermute | solution.py:370
  88.2 1.9 %collective-permute-done.11.other = f32[112,128]{1,0:T(8,128)S(1)} collective-permute-done((f32[112,128]{1,0:T(8,128)S(1)}, f32[112,128]{1,0:T(8,128)S(1)}, u32[]{:S(2)}, u32[]{:S(2)}) %collective-permute-start.11) | collective-permute-done | bytes 57376 | tf_op jit(solution)/shard_map/ppermute | solution.py:370
  90.1 0.7 shard_map.74
  90.8 4.9 %all-to-all-done.3.recv = f32[32,16,128]{2,1,0:T(8,128)S(1)} async-done(((f32[32,16,128]{2,1,0:T(8,128)}), f32[32,16,128]{2,1,0:T(8,128)S(1)}, u32[]{:S(2)}, u32[]{:S(2)}) %all-to-all-start.3) | async-done | bytes 262176 | tf_op jit(solution)/shard_map/all_to_all | solution.py:368
  95.6 1.0 %shard_map.72 = f32[12,8,256]{2,1,0:T(8,128)} custom-call(f32[32,16,128]{2,1,0:T(8,128)S(1)} %all-to-all-done.3.recv), custom_call_target="tpu_custom_call" | custom-call | flops 1000000 | bytes 1000000 | tf_op jit(solution)/shard_map/pallas_call | solution.py:372
  (22 shorter events, 0.6 us)
Async XLA Ops:
  0.6 10.5 %copy-start.1 = (f32[24,16,128]{2,1,0:T(8,128)S(1)}, f32[24,16,128]{2,1,0:T(8,128)}, u32[]{:S(2)}) copy-start(f32[24,16,128]{2,1,0:T(8,128)} %own.1) | copy-start | bytes 589828
  0.6 12.3 %copy-start.2 = (f32[8,12,256]{2,0,1:T(8,128)S(1)}, f32[8,12,256]{2,0,1:T(8,128)}, u32[]{:S(2)}) copy-start(f32[8,12,256]{2,0,1:T(8,128)} %param.4) | copy-start | bytes 294916
  2.5 10.5 %copy-start.5 = (f32[80,128]{1,0:T(8,128)S(1)}, f32[80,128]{1,0:T(8,128)}, u32[]{:S(2)}) copy-start(f32[80,128]{1,0:T(8,128)} %get-tuple-element.22) | copy-start | bytes 122884
  2.5 21.5 %all-to-all-start = ((f32[32,40,128]{2,1,0:T(8,128)}), f32[32,40,128]{2,1,0:T(8,128)S(1)}, u32[]{:S(2)}, u32[]{:S(2)}) async-start(f32[32,40,128]{2,1,0:T(8,128)} %get-tuple-element.23), calls=%async_computation | async-start | bytes 1310720 | tf_op jit(solution)/shard_map/all_to_all | solution.py:330
  11.2 28.6 %copy-start = (f32[256,3,3,128]{3,0,2,1:T(8,128)S(1)}, f32[256,3,3,128]{3,0,2,1:T(8,128)}, u32[]{:S(2)}) copy-start(f32[256,3,3,128]{3,0,2,1:T(8,128)} %param.6) | copy-start | bytes 3538948
  11.2 9.7 %collective-permute-start.3 = (f32[24,16,128]{2,1,0:T(8,128)S(1)}, f32[24,16,128]{2,1,0:T(8,128)S(1)}, u32[]{:S(2)}, u32[]{:S(2)}) collective-permute-start(f32[24,16,128]{2,1,0:T(8,128)S(1)} %copy-done.1), channel_id=1, source_target_pairs={{0,32},{32,0},{64,96},{96,64},{128,160},{160,128},{192,224},{224,1... | collective-permute-start | bytes 589832 | tf_op jit(solution)/shard_map/ppermute | solution.py:329
  12.9 8.0 %collective-permute-start.2 = (f32[12,8,256]{2,1,0:T(8,128)S(1)}, f32[12,8,256]{2,1,0:T(8,128)S(1)}, u32[]{:S(2)}, u32[]{:S(2)}) collective-permute-start(f32[12,8,256]{2,1,0:T(8,128)S(1)} %bitcast.22), channel_id=1, source_target_pairs={{0,32},{32,0},{64,96},{96,64},{128,160},{160,128},{192,224},{224,1... | collective-permute-start | bytes 294920 | tf_op jit(solution)/shard_map/ppermute | solution.py:328
  13.0 6.6 %collective-permute-start.1 = (f32[80,128]{1,0:T(8,128)S(1)}, f32[80,128]{1,0:T(8,128)S(1)}, u32[]{:S(2)}, u32[]{:S(2)}) collective-permute-start(f32[80,128]{1,0:T(8,128)S(1)} %copy-done.5), channel_id=1, source_target_pairs={{32,96},{96,160},{160,224},{64,0},{128,64},{192,128},{33,97},{97,1... | collective-permute-start | bytes 122888 | tf_op jit(solution)/shard_map/ppermute | solution.py:327
  14.3 5.3 %collective-permute-start = (f32[80,128]{1,0:T(8,128)S(1)}, f32[80,128]{1,0:T(8,128)S(1)}, u32[]{:S(2)}, u32[]{:S(2)}) collective-permute-start(f32[80,128]{1,0:T(8,128)S(1)} %copy-done.5), channel_id=1, source_target_pairs={{32,64},{96,128},{160,192},{64,32},{128,96},{192,160},{33,65},{97,... | collective-permute-start | bytes 122888 | tf_op jit(solution)/shard_map/ppermute | solution.py:326
  25.7 16.3 %all-to-all-start.1 = ((f32[32,32,128]{2,1,0:T(8,128)}), f32[32,32,128]{2,1,0:T(8,128)S(1)}, u32[]{:S(2)}, u32[]{:S(2)}) async-start(f32[32,32,128]{2,1,0:T(8,128)} %shard_map.68), calls=%async_computation.1 | async-start | bytes 1048576 | tf_op jit(solution)/shard_map/all_to_all | solution.py:335
  30.5 9.2 %collective-permute-start.4 = (f32[54,16,128]{2,1,0:T(8,128)S(1)}, f32[54,16,128]{2,1,0:T(8,128)S(1)}, u32[]{:S(2)}, u32[]{:S(2)}) collective-permute-start(f32[54,16,128]{2,1,0:T(8,128)S(1)} %get-tuple-element.29.own), channel_id=1, source_target_pairs={{0,1},{1,0},{2,3},{3,2},{4,5},{5,4},{6,7},{7,6},{8,9},{9,8},{10,11... | collective-permute-start | bytes 1327112 | tf_op jit(solution)/shard_map/ppermute | solution.py:342
  30.8 6.1 %collective-permute-start.6 = (f32[56,128]{1,0:T(8,128)S(1)}, f32[56,128]{1,0:T(8,128)S(1)}, u32[]{:S(2)}, u32[]{:S(2)}) collective-permute-start(f32[56,128]{1,0:T(8,128)S(1)} %get-tuple-element.30), channel_id=1, source_target_pairs={{1,3},{3,5},{5,7},{7,9},{9,11},{11,13},{13,15},{15,17},{17,19},{19... | collective-permute-start | bytes 86024 | tf_op jit(solution)/shard_map/ppermute | solution.py:341
  34.2 5.5 %collective-permute-start.5 = (f32[56,128]{1,0:T(8,128)S(1)}, f32[56,128]{1,0:T(8,128)S(1)}, u32[]{:S(2)}, u32[]{:S(2)}) collective-permute-start(f32[56,128]{1,0:T(8,128)S(1)} %get-tuple-element.30), channel_id=1, source_target_pairs={{1,2},{3,4},{5,6},{7,8},{9,10},{11,12},{13,14},{15,16},{17,18},{19... | collective-permute-start | bytes 86024 | tf_op jit(solution)/shard_map/ppermute | solution.py:340
  40.8 0.8 copy-start.3
  41.9 1.0 %copy-start.4 = (bf16[512,512]{1,0:T(8,128)(2,1)S(1)}, bf16[512,512]{1,0:T(8,128)(2,1)}, u32[]{:S(2)}) copy-start(bf16[512,512]{1,0:T(8,128)(2,1)} %copy-done.3) | copy-start | bytes 1572868
  46.7 23.6 %all-to-all-start.2 = ((f32[32,56,128]{2,1,0:T(8,128)}), f32[32,56,128]{2,1,0:T(8,128)S(1)}, u32[]{:S(2)}, u32[]{:S(2)}) async-start(f32[32,56,128]{2,1,0:T(8,128)} %bitcast.7), calls=%async_computation.2 | async-start | bytes 1835008 | tf_op jit(solution)/shard_map/all_to_all | solution.py:360
  54.5 11.2 %collective-permute-start.7 = (f32[512,128]{1,0:T(8,128)S(1)}, f32[512,128]{1,0:T(8,128)S(1)}, u32[]{:S(2)}, u32[]{:S(2)}) collective-permute-start(f32[512,128]{1,0:T(8,128)S(1)} %get-tuple-element.35), channel_id=1, source_target_pairs={{0,32},{32,0},{64,96},{96,64},{128,160},{160,128},{192,224},{224,1... | collective-permute-start | bytes 786440 | tf_op jit(solution)/shard_map/ppermute | solution.py:359
  70.4 16.3 %collective-permute-start.10 = (f32[112,128]{1,0:T(8,128)S(1)}, f32[112,128]{1,0:T(8,128)S(1)}, u32[]{:S(2)}, u32[]{:S(2)}) collective-permute-start(f32[112,128]{1,0:T(8,128)S(1)} %shard_map.73), channel_id=1, source_target_pairs={{0,192},{32,224},{64,0},{96,32},{128,64},{160,96},{192,128},{224,1... | collective-permute-start | bytes 172040 | tf_op jit(solution)/shard_map/ppermute | solution.py:366
  77.6 9.0 %collective-permute-start.9 = (f32[112,128]{1,0:T(8,128)S(1)}, f32[112,128]{1,0:T(8,128)S(1)}, u32[]{:S(2)}, u32[]{:S(2)}) collective-permute-start(f32[112,128]{1,0:T(8,128)S(1)} %shard_map.73), channel_id=1, source_target_pairs={{0,64},{32,96},{64,128},{96,160},{128,192},{160,224},{192,0},{224,... | collective-permute-start | bytes 172040 | tf_op jit(solution)/shard_map/ppermute | solution.py:365
  77.6 9.0 %collective-permute-start.8 = (f32[112,128]{1,0:T(8,128)S(1)}, f32[112,128]{1,0:T(8,128)S(1)}, u32[]{:S(2)}, u32[]{:S(2)}) collective-permute-start(f32[112,128]{1,0:T(8,128)S(1)} %shard_map.73), channel_id=1, source_target_pairs={{0,128},{32,160},{64,192},{96,224},{128,0},{160,32},{192,64},{224,... | collective-permute-start | bytes 172040 | tf_op jit(solution)/shard_map/ppermute | solution.py:367
  81.9 13.8 %all-to-all-start.3 = ((f32[32,16,128]{2,1,0:T(8,128)}), f32[32,16,128]{2,1,0:T(8,128)S(1)}, u32[]{:S(2)}, u32[]{:S(2)}) async-start(f32[32,16,128]{2,1,0:T(8,128)} %bitcast.8), calls=%async_computation.3 | async-start | bytes 524288 | tf_op jit(solution)/shard_map/all_to_all | solution.py:368
  86.7 3.4 %collective-permute-start.11 = (f32[112,128]{1,0:T(8,128)S(1)}, f32[112,128]{1,0:T(8,128)S(1)}, u32[]{:S(2)}, u32[]{:S(2)}) collective-permute-start(f32[112,128]{1,0:T(8,128)S(1)} %add_add_fusion.own), channel_id=1, source_target_pairs={{0,32},{32,0},{64,96},{96,64},{128,160},{160,128},{192,224},{224,1... | collective-permute-start | bytes 172040 | tf_op jit(solution)/shard_map/ppermute | solution.py:370

commit v4 on v3

--- a/solution.py
+++ b/solution.py
@@ -103,7 +103,7 @@
     side[FINE : FINE + 2, :] = jnp.zeros((2, 128), F32)
 
 
-def window_kernel(own, other, near, far, weight, s_high, s_low, grad, image, sums):
+def windows(own, other, near, far, weight, sums, image):
     core = lax.axis_index("chan") % 2
     group = 2 * (lax.axis_index("rows") % 2) + core
     image[:, pl.ds(pl.multiple_of(8 + 16 * core, 8), 16), :] = own[...]
@@ -131,8 +131,6 @@
             sums[at : at + 17, 256:384] = even[2 * r + 1] + even[2 * r + 2]
             sums[at : at + 16, 384:512] = odd[2 * r + 1] + odd[2 * r + 2]
     high, low = halves(sums[...])
-    s_high[...] = high
-    s_low[...] = low
     total = None
     for kind in range(4):
         lanes = slice(kind * 128, (kind + 1) * 128)
@@ -151,7 +149,7 @@
             if shift_of(t):
                 term = pltpu.roll(term, FLAT - shift_of(t), 1)
             total = term if total is None else total + term
-    grad[...] = total
+    return (high, low), total
 
 
 def kind_of(t):
@@ -162,7 +160,11 @@
     return STEP * (t // 3 == 0) + (t % 3 == 0)
 
 
-def main_kernel(recv, kernels, s_high, s_low, grad, out, mine, theirs, x_high, x_low, w_high, w_low, g_high, g_low):
+def main_kernel(
+    recv, kernels, own, other, near, far, weight, out, mine, theirs,
+    cells, sums, x_high, x_low, w_high, w_low, g_high, g_low,
+):
+    parts, grad = windows(own, other, near, far, weight, sums, cells)
     for pair in range(16):
         for q in range(4):
             tile = jnp.concatenate(
@@ -195,7 +197,7 @@
     sigma = 1.0 / (1.0 + jnp.exp(-hidden))
     active = jnp.where(inside, hidden * sigma, 0.0)
     slope = sigma * (1.0 + hidden * (1.0 - sigma))
-    gradient = grad[...] * slope
+    gradient = grad * slope
 
     def stack(values, offset):
         for t in range(9):
@@ -215,7 +217,7 @@
                 ]
     shifts = [0, 1, STEP, STEP + 1]
     spread = jnp.concatenate([pltpu.roll(active, s, 1) if s else active for s in shifts], axis=0)
-    onto = product(halves(spread), (s_high[...], s_low[...]), NN)
+    onto = product(halves(spread), parts, NN)
     for t in range(9):
         at, kind = shifts.index(shift_of(t)) * 64, kind_of(t)
         for j in range(2):
@@ -340,37 +342,35 @@
     near_side = lax.ppermute(side, "chan", beside(32))
     far_side = lax.ppermute(side, "chan", inward(32))
     other_tall = lax.ppermute(tall, "chan", partner(32))
-    s_high, s_low, grad = call(
-        window_kernel,
-        (shape(FLAT, 512, dtype=BF16), shape(FLAT, 512, dtype=BF16), shape(64, FLAT)), 5,
-        [pltpu.VMEM((FINE, 48, 128), F32), pltpu.VMEM((FLAT, 512), F32)],
-        3 * 10**8, 3 * 10**6,
-    )(tall, other_tall, near_side, far_side, jnp.transpose(weight_out, (1, 2, 0, 3)).reshape(2304, 128))
-
     sent, own, given = call(
-        main_kernel, (shape(32 * BACK, 128), shape(512, 128), shape(512, 128)), 5,
+        main_kernel, (shape(32 * BACK, 128), shape(512, 128), shape(512, 128)), 7,
         [
+            pltpu.VMEM((FINE, 48, 128), F32), pltpu.VMEM((FLAT, 512), F32),
             pltpu.VMEM((256, FLAT), BF16), pltpu.VMEM((256, FLAT), BF16),
             pltpu.VMEM((576, 256), BF16), pltpu.VMEM((576, 256), BF16),
             pltpu.VMEM((576, FLAT), BF16), pltpu.VMEM((576, FLAT), BF16),
         ],
         10**9, 5 * 10**6,
-    )(recv.reshape(1024, 128), kernels.reshape(32 * PACK, 128), s_high, s_low, grad)
+    )(
+        recv.reshape(1024, 128), kernels.reshape(32 * PACK, 128), tall, other_tall, near_side, far_side,
+        jnp.transpose(weight_out, (1, 2, 0, 3)).reshape(2304, 128),
+    )
     given = lax.ppermute(given, "rows", partner(8))
     back = lax.all_to_all(sent.reshape(32, BACK, 128), "chan", 0, 0, tiled=True)
-    given, back = lax.optimization_barrier((given, back))
+    moved, back = lax.optimization_barrier((own + given, back))
     mixed = call(lambda *refs: weights_kernel(scale, *refs), shape(112, 128), 1, [pltpu.VMEM((56, 128), F32)])(
         back
     )
+    image = lax.all_to_all(moved.reshape(32, 16, 128), "chan", 0, 0, tiled=True)
     left = lax.ppermute(mixed, "rows", shifted(8, 2))
     right = lax.ppermute(mixed, "rows", shifted(8, 6))
     opposite = lax.ppermute(mixed, "rows", shifted(8, 4))
-    image = lax.all_to_all((own + given).reshape(32, 16, 128), "chan", 0, 0, tiled=True)
     mixed = (mixed + opposite) + (left + right)
     counter = lax.ppermute(mixed, "rows", partner(8))
     into, onto = call(final_kernel, (shape(9, 8, 256), shape(9, 8, 128)), 2)(mixed, counter)
     rows = call(
-        image_kernel, shape(12, 8, 256), 1, [pltpu.VMEM((12, 8, 512), F32), pltpu.VMEM((8, 256), F32)]
+        image_kernel, shape(12, 8, 256), 1,
+        [pltpu.VMEM((12, 8, 512), F32), pltpu.VMEM((8, 256), F32)], 10**11, 10**8,
     )(image)
     grad_image = jnp.transpose(rows, (1, 0, 2))
     grad_in = jnp.transpose(into.reshape(3, 3, 8, 256), (2, 0, 1, 3))

time: 97.3 us -> 95.6 us (0.983)
  starting transfers between devices: 52.7 us -> 51.6 us
    all_to_all x1, waiting for transfers between devices: 0.38 us -> 1.46 us  [local(): recv = lax.all_to_all(packed, 'chan', 0, 0, tiled=True)]
    all_to_all x1, starting transfers between devices: 7.81 us -> 6.73 us  [local(): back = lax.all_to_all(sent.reshape(32, BACK, 128), 'chan', 0, 0, tiled=True)]
    pallas_call x1 -> x0, Pallas kernels: 1.05 us -> none  [local(): call(window_kernel, (shape(FLAT, 512, dtype=BF16), shape(FLAT, 512, dtype...]
  transfers between devices with their start and end apart: 16 -> 16, of which waited for: 10 -> 10; matrix products, arithmetic and copies ran while one was open for 1% -> 1% of each run, Pallas kernels for 2% -> 1%
where the time goes in v4:
time: 95.6 us; the launch traced here: 94.9 us
  starting transfers between devices  51.6 us (54%)
  waiting for transfers between devices  30.8 us (32%)
  Pallas kernels  9.15 us (10%)
  local copies, waits for them, and re-layouts  1.81 us (2%)
    all_to_all x1, starting transfers between devices, local(): kernels = lax.all_to_all(packed, 'chan', 0, 0, tiled=True)  8.6 us
    ppermute x1, starting transfers between devices, local(): right = lax.ppermute(mixed, 'rows', shifted(8, 6))  7.27 us
    all_to_all x1, starting transfers between devices, local(): back = lax.all_to_all(sent.reshape(32, BACK, 128), 'chan', 0, 0, tiled=True)  6.73 us
    ppermute x1, waiting for transfers between devices, local(): given = lax.ppermute(given, 'rows', partner(8))  6.53 us
    all_to_all x1, waiting for transfers between devices, local(): image = lax.all_to_all(moved.reshape(32, 16, 128), 'chan', 0, 0, tiled=True)  4.87 us
    all_to_all x1, starting transfers between devices, local(): image = lax.all_to_all(moved.reshape(32, 16, 128), 'chan', 0, 0, tiled=True)  4.76 us
    ppermute x1, starting transfers between devices, local(): given = lax.ppermute(given, 'rows', partner(8))  4.72 us
    all_to_all x1, starting transfers between devices, local(): recv = lax.all_to_all(packed, 'chan', 0, 0, tiled=True)  4.71 us
  transfers between devices with their start and end apart: 16, of which 10 were waited for; matrix products, arithmetic and copies ran while one was open for 1% of the time, Pallas kernels for 1%

profile of v4, /device:TPU:1, one launch (start us, length us, event | category | flops | bytes accessed | tf_op | source)
XLA Modules:
  0.0 94.9 jit_solution(3010518690120642369)
XLA Ops:
  0.7 1.9 %shard_map.67 = (f32[80,128]{1,0:T(8,128)}, f32[32,40,128]{2,1,0:T(8,128)}) custom-call(f32[12,8,256]{2,1,0:T(8,128)} %bitcast.20, f32[24,16,128]{2,1,0:T(8,128)} %own.1, f32[9,8,256]{2,1,0:T(8,128)} %bitcast.24), custom_call_target="tpu_custom_call" | custom-call | flops 1000000 | bytes 1000000 | tf_op jit(solution)/shard_map/pallas_call | solution.py:319
  2.5 8.6 %all-to-all-start = ((f32[32,40,128]{2,1,0:T(8,128)}), f32[32,40,128]{2,1,0:T(8,128)S(1)}, u32[]{:S(2)}, u32[]{:S(2)}) async-start(f32[32,40,128]{2,1,0:T(8,128)} %get-tuple-element.20), calls=%async_computation | async-start | bytes 1310720 | tf_op jit(solution)/shard_map/all_to_all | solution.py:332
  11.2 1.7 %collective-permute-start.3 = (f32[24,16,128]{2,1,0:T(8,128)S(1)}, f32[24,16,128]{2,1,0:T(8,128)S(1)}, u32[]{:S(2)}, u32[]{:S(2)}) collective-permute-start(f32[24,16,128]{2,1,0:T(8,128)S(1)} %copy-done), channel_id=1, source_target_pairs={{0,32},{32,0},{64,96},{96,64},{128,160},{160,128},{192,224},{224,1... | collective-permute-start | bytes 589832 | tf_op jit(solution)/shard_map/ppermute | solution.py:331
  13.0 1.3 %collective-permute-start.1 = (f32[80,128]{1,0:T(8,128)S(1)}, f32[80,128]{1,0:T(8,128)S(1)}, u32[]{:S(2)}, u32[]{:S(2)}) collective-permute-start(f32[80,128]{1,0:T(8,128)S(1)} %copy-done.5), channel_id=1, source_target_pairs={{32,96},{96,160},{160,224},{64,0},{128,64},{192,128},{33,97},{97,1... | collective-permute-start | bytes 122888 | tf_op jit(solution)/shard_map/ppermute | solution.py:329
  14.3 0.7 collective-permute-start
  15.0 4.6 %collective-permute-done.1.far = f32[80,128]{1,0:T(8,128)S(1)} collective-permute-done((f32[80,128]{1,0:T(8,128)S(1)}, f32[80,128]{1,0:T(8,128)S(1)}, u32[]{:S(2)}, u32[]{:S(2)}) %collective-permute-start.1) | collective-permute-done | bytes 40992 | tf_op jit(solution)/shard_map/ppermute | solution.py:329
  19.6 1.3 %collective-permute-done.2.other = f32[12,8,256]{2,1,0:T(8,128)S(1)} collective-permute-done((f32[12,8,256]{2,1,0:T(8,128)S(1)}, f32[12,8,256]{2,1,0:T(8,128)S(1)}, u32[]{:S(2)}, u32[]{:S(2)}) %collective-permute-start.2) | collective-permute-done | bytes 98336 | tf_op jit(solution)/shard_map/ppermute | solution.py:330
  20.9 3.2 %all-to-all-done = f32[32,40,128]{2,1,0:T(8,128)S(1)} async-done(((f32[32,40,128]{2,1,0:T(8,128)}), f32[32,40,128]{2,1,0:T(8,128)S(1)}, u32[]{:S(2)}, u32[]{:S(2)}) %all-to-all-start) | async-done | bytes 655392 | tf_op jit(solution)/shard_map/all_to_all | solution.py:332
  24.0 1.6 %shard_map.68 = f32[32,32,128]{2,1,0:T(8,128)} custom-call(f32[12,8,256]{2,1,0:T(8,128)S(1)} %bitcast.22, f32[12,8,256]{2,1,0:T(8,128)S(1)} %collective-permute-done.2.other, f32[80,128]{1,0:T(8,128)S(1)} %collective-permute-done.near, f32[80,128]{1,0:T(8,128)S(1)} %collective-permute-done.1.far), custom_call_target="tpu_custom_call" | custom-call | flops 1000000 | bytes 1000000 | tf_op jit(solution)/shard_map/pallas_call | solution.py:334
  25.7 4.7 %all-to-all-start.1 = ((f32[32,32,128]{2,1,0:T(8,128)}), f32[32,32,128]{2,1,0:T(8,128)S(1)}, u32[]{:S(2)}, u32[]{:S(2)}) async-start(f32[32,32,128]{2,1,0:T(8,128)} %shard_map.68), calls=%async_computation.1 | async-start | bytes 1048576 | tf_op jit(solution)/shard_map/all_to_all | solution.py:337
  30.5 0.3 collective-permute-start.4
  30.8 3.4 %collective-permute-start.6 = (f32[56,128]{1,0:T(8,128)S(1)}, f32[56,128]{1,0:T(8,128)S(1)}, u32[]{:S(2)}, u32[]{:S(2)}) collective-permute-start(f32[56,128]{1,0:T(8,128)S(1)} %get-tuple-element.27), channel_id=1, source_target_pairs={{1,3},{3,5},{5,7},{7,9},{9,11},{11,13},{13,15},{15,17},{17,19},{19... | collective-permute-start | bytes 86024 | tf_op jit(solution)/shard_map/ppermute | solution.py:343
  34.2 2.3 %collective-permute-start.5 = (f32[56,128]{1,0:T(8,128)S(1)}, f32[56,128]{1,0:T(8,128)S(1)}, u32[]{:S(2)}, u32[]{:S(2)}) collective-permute-start(f32[56,128]{1,0:T(8,128)S(1)} %get-tuple-element.27), channel_id=1, source_target_pairs={{1,2},{3,4},{5,6},{7,8},{9,10},{11,12},{13,14},{15,16},{17,18},{19... | collective-permute-start | bytes 86024 | tf_op jit(solution)/shard_map/ppermute | solution.py:342
  36.5 0.4 collective-permute-done.6.far
  36.9 2.8 %collective-permute-done.5.near = f32[56,128]{1,0:T(8,128)S(1)} collective-permute-done((f32[56,128]{1,0:T(8,128)S(1)}, f32[56,128]{1,0:T(8,128)S(1)}, u32[]{:S(2)}, u32[]{:S(2)}) %collective-permute-start.5) | collective-permute-done | bytes 28704 | tf_op jit(solution)/shard_map/ppermute | solution.py:342
  39.7 0.8 copy-done.3
  40.5 1.5 %all-to-all-done.1 = f32[32,32,128]{2,1,0:T(8,128)S(1)} async-done(((f32[32,32,128]{2,1,0:T(8,128)}), f32[32,32,128]{2,1,0:T(8,128)S(1)}, u32[]{:S(2)}, u32[]{:S(2)}) %all-to-all-start.1) | async-done | bytes 524320 | tf_op jit(solution)/shard_map/all_to_all | solution.py:337
  41.9 1.0 %copy-done.4 = f32[54,16,128]{2,1,0:T(8,128)S(1)} copy-done((f32[54,16,128]{2,1,0:T(8,128)S(1)}, f32[54,16,128]{2,1,0:T(8,128)}, u32[]{:S(2)}) %copy-start.4) | copy-done | bytes 442392
  42.9 3.9 %shard_map.70 = (f32[1792,128]{1,0:T(8,128)}, f32[512,128]{1,0:T(8,128)S(1)}, f32[512,128]{1,0:T(8,128)S(1)}) custom-call(f32[1024,128]{1,0:T(8,128)S(1)} %bitcast.19, f32[1280,128]{1,0:T(8,128)S(1)} %bitcast.18, f32[54,16,128]{2,1,0:T(8,128)S(1)} %get-tuple-element.26.own, f32[54,16,128]{2,1,0:T(8,128)S(1)} %copy-done.4, ...), custom_call_target="tpu_custom_call" | custom-call | flops 1000000000 | bytes 5000000 | tf_op jit(solution)/shard_map/pallas_call | solution.py:345
  46.8 6.7 %all-to-all-start.2 = ((f32[32,56,128]{2,1,0:T(8,128)}), f32[32,56,128]{2,1,0:T(8,128)S(1)}, u32[]{:S(2)}, u32[]{:S(2)}) async-start(f32[32,56,128]{2,1,0:T(8,128)} %bitcast.7), calls=%async_computation.2 | async-start | bytes 1835008 | tf_op jit(solution)/shard_map/all_to_all | solution.py:359
  53.5 4.7 %collective-permute-start.7 = (f32[512,128]{1,0:T(8,128)S(1)}, f32[512,128]{1,0:T(8,128)S(1)}, u32[]{:S(2)}, u32[]{:S(2)}) collective-permute-start(f32[512,128]{1,0:T(8,128)S(1)} %get-tuple-element.29), channel_id=1, source_target_pairs={{0,32},{32,0},{64,96},{96,64},{128,160},{160,128},{192,224},{224,1... | collective-permute-start | bytes 786440 | tf_op jit(solution)/shard_map/ppermute | solution.py:358
  58.2 6.5 %collective-permute-done.7 = f32[512,128]{1,0:T(8,128)S(1)} collective-permute-done((f32[512,128]{1,0:T(8,128)S(1)}, f32[512,128]{1,0:T(8,128)S(1)}, u32[]{:S(2)}, u32[]{:S(2)}) %collective-permute-start.7) | collective-permute-done | bytes 262176 | tf_op jit(solution)/shard_map/ppermute | solution.py:358
  64.8 0.7 add.12
  65.5 3.8 %all-to-all-done.2.refs_0_ = f32[32,56,128]{2,1,0:T(8,128)S(1)} async-done(((f32[32,56,128]{2,1,0:T(8,128)}), f32[32,56,128]{2,1,0:T(8,128)S(1)}, u32[]{:S(2)}, u32[]{:S(2)}) %all-to-all-start.2) | async-done | bytes 917536 | tf_op jit(solution)/shard_map/all_to_all | solution.py:359
  69.4 7.3 %collective-permute-start.10 = (f32[112,128]{1,0:T(8,128)S(1)}, f32[112,128]{1,0:T(8,128)S(1)}, u32[]{:S(2)}, u32[]{:S(2)}) collective-permute-start(f32[112,128]{1,0:T(8,128)S(1)} %shard_map.72), channel_id=1, source_target_pairs={{0,192},{32,224},{64,0},{96,32},{128,64},{160,96},{192,128},{224,1... | collective-permute-start | bytes 172040 | tf_op jit(solution)/shard_map/ppermute | solution.py:366
  76.6 3.5 %collective-permute-start.8 = (f32[112,128]{1,0:T(8,128)S(1)}, f32[112,128]{1,0:T(8,128)S(1)}, u32[]{:S(2)}, u32[]{:S(2)}) collective-permute-start(f32[112,128]{1,0:T(8,128)S(1)} %shard_map.72), channel_id=1, source_target_pairs={{0,128},{32,160},{64,192},{96,224},{128,0},{160,32},{192,64},{224,... | collective-permute-start | bytes 172040 | tf_op jit(solution)/shard_map/ppermute | solution.py:367
  80.1 4.8 %all-to-all-start.3 = ((f32[32,16,128]{2,1,0:T(8,128)}), f32[32,16,128]{2,1,0:T(8,128)S(1)}, u32[]{:S(2)}, u32[]{:S(2)}) async-start(f32[32,16,128]{2,1,0:T(8,128)} %bitcast.8), calls=%async_computation.3 | async-start | bytes 524288 | tf_op jit(solution)/shard_map/all_to_all | solution.py:364
  84.9 1.6 %collective-permute-start.11 = (f32[112,128]{1,0:T(8,128)S(1)}, f32[112,128]{1,0:T(8,128)S(1)}, u32[]{:S(2)}, u32[]{:S(2)}) collective-permute-start(f32[112,128]{1,0:T(8,128)S(1)} %add_add_fusion.own), channel_id=1, source_target_pairs={{0,32},{32,0},{64,96},{96,64},{128,160},{160,128},{192,224},{224,1... | collective-permute-start | bytes 172040 | tf_op jit(solution)/shard_map/ppermute | solution.py:369
  86.5 1.9 %collective-permute-done.11.other = f32[112,128]{1,0:T(8,128)S(1)} collective-permute-done((f32[112,128]{1,0:T(8,128)S(1)}, f32[112,128]{1,0:T(8,128)S(1)}, u32[]{:S(2)}, u32[]{:S(2)}) %collective-permute-start.11) | collective-permute-done | bytes 57376 | tf_op jit(solution)/shard_map/ppermute | solution.py:369
  88.4 0.7 shard_map.73
  89.0 4.9 %all-to-all-done.3.recv = f32[32,16,128]{2,1,0:T(8,128)S(1)} async-done(((f32[32,16,128]{2,1,0:T(8,128)}), f32[32,16,128]{2,1,0:T(8,128)S(1)}, u32[]{:S(2)}, u32[]{:S(2)}) %all-to-all-start.3) | async-done | bytes 262176 | tf_op jit(solution)/shard_map/all_to_all | solution.py:364
  93.9 1.0 %shard_map.71 = f32[12,8,256]{2,1,0:T(8,128)} custom-call(f32[32,16,128]{2,1,0:T(8,128)S(1)} %all-to-all-done.3.recv), custom_call_target="tpu_custom_call" | custom-call | flops 99999997952 | bytes 100000000 | tf_op jit(solution)/shard_map/pallas_call | solution.py:371
  (21 shorter events, 0.3 us)
Async XLA Ops:
  0.6 10.5 %copy-start = (f32[24,16,128]{2,1,0:T(8,128)S(1)}, f32[24,16,128]{2,1,0:T(8,128)}, u32[]{:S(2)}) copy-start(f32[24,16,128]{2,1,0:T(8,128)} %own.1) | copy-start | bytes 589828
  0.6 12.2 %copy-start.1 = (f32[8,12,256]{2,0,1:T(8,128)S(1)}, f32[8,12,256]{2,0,1:T(8,128)}, u32[]{:S(2)}) copy-start(f32[8,12,256]{2,0,1:T(8,128)} %param.4) | copy-start | bytes 294916
  2.5 10.5 %copy-start.5 = (f32[80,128]{1,0:T(8,128)S(1)}, f32[80,128]{1,0:T(8,128)}, u32[]{:S(2)}) copy-start(f32[80,128]{1,0:T(8,128)} %get-tuple-element.19) | copy-start | bytes 122884
  2.5 21.5 %all-to-all-start = ((f32[32,40,128]{2,1,0:T(8,128)}), f32[32,40,128]{2,1,0:T(8,128)S(1)}, u32[]{:S(2)}, u32[]{:S(2)}) async-start(f32[32,40,128]{2,1,0:T(8,128)} %get-tuple-element.20), calls=%async_computation | async-start | bytes 1310720 | tf_op jit(solution)/shard_map/all_to_all | solution.py:332
  11.1 30.8 %copy-start.2 = (f32[256,3,3,128]{3,0,2,1:T(8,128)S(1)}, f32[256,3,3,128]{3,0,2,1:T(8,128)}, u32[]{:S(2)}) copy-start(f32[256,3,3,128]{3,0,2,1:T(8,128)} %param.6) | copy-start | bytes 3538948
  11.2 9.7 %collective-permute-start.3 = (f32[24,16,128]{2,1,0:T(8,128)S(1)}, f32[24,16,128]{2,1,0:T(8,128)S(1)}, u32[]{:S(2)}, u32[]{:S(2)}) collective-permute-start(f32[24,16,128]{2,1,0:T(8,128)S(1)} %copy-done), channel_id=1, source_target_pairs={{0,32},{32,0},{64,96},{96,64},{128,160},{160,128},{192,224},{224,1... | collective-permute-start | bytes 589832 | tf_op jit(solution)/shard_map/ppermute | solution.py:331
  12.9 8.0 %collective-permute-start.2 = (f32[12,8,256]{2,1,0:T(8,128)S(1)}, f32[12,8,256]{2,1,0:T(8,128)S(1)}, u32[]{:S(2)}, u32[]{:S(2)}) collective-permute-start(f32[12,8,256]{2,1,0:T(8,128)S(1)} %bitcast.21), channel_id=1, source_target_pairs={{0,32},{32,0},{64,96},{96,64},{128,160},{160,128},{192,224},{224,1... | collective-permute-start | bytes 294920 | tf_op jit(solution)/shard_map/ppermute | solution.py:330
  13.0 6.6 %collective-permute-start.1 = (f32[80,128]{1,0:T(8,128)S(1)}, f32[80,128]{1,0:T(8,128)S(1)}, u32[]{:S(2)}, u32[]{:S(2)}) collective-permute-start(f32[80,128]{1,0:T(8,128)S(1)} %copy-done.5), channel_id=1, source_target_pairs={{32,96},{96,160},{160,224},{64,0},{128,64},{192,128},{33,97},{97,1... | collective-permute-start | bytes 122888 | tf_op jit(solution)/shard_map/ppermute | solution.py:329
  14.3 5.3 %collective-permute-start = (f32[80,128]{1,0:T(8,128)S(1)}, f32[80,128]{1,0:T(8,128)S(1)}, u32[]{:S(2)}, u32[]{:S(2)}) collective-permute-start(f32[80,128]{1,0:T(8,128)S(1)} %copy-done.5), channel_id=1, source_target_pairs={{32,64},{96,128},{160,192},{64,32},{128,96},{192,160},{33,65},{97,... | collective-permute-start | bytes 122888 | tf_op jit(solution)/shard_map/ppermute | solution.py:328
  25.7 16.3 %all-to-all-start.1 = ((f32[32,32,128]{2,1,0:T(8,128)}), f32[32,32,128]{2,1,0:T(8,128)S(1)}, u32[]{:S(2)}, u32[]{:S(2)}) async-start(f32[32,32,128]{2,1,0:T(8,128)} %shard_map.68), calls=%async_computation.1 | async-start | bytes 1048576 | tf_op jit(solution)/shard_map/all_to_all | solution.py:337
  30.5 9.2 %collective-permute-start.4 = (f32[54,16,128]{2,1,0:T(8,128)S(1)}, f32[54,16,128]{2,1,0:T(8,128)S(1)}, u32[]{:S(2)}, u32[]{:S(2)}) collective-permute-start(f32[54,16,128]{2,1,0:T(8,128)S(1)} %get-tuple-element.26.own), channel_id=1, source_target_pairs={{0,1},{1,0},{2,3},{3,2},{4,5},{5,4},{6,7},{7,6},{8,9},{9,8},{10,11... | collective-permute-start | bytes 1327112 | tf_op jit(solution)/shard_map/ppermute | solution.py:344
  30.8 6.1 %collective-permute-start.6 = (f32[56,128]{1,0:T(8,128)S(1)}, f32[56,128]{1,0:T(8,128)S(1)}, u32[]{:S(2)}, u32[]{:S(2)}) collective-permute-start(f32[56,128]{1,0:T(8,128)S(1)} %get-tuple-element.27), channel_id=1, source_target_pairs={{1,3},{3,5},{5,7},{7,9},{9,11},{11,13},{13,15},{15,17},{17,19},{19... | collective-permute-start | bytes 86024 | tf_op jit(solution)/shard_map/ppermute | solution.py:343
  34.2 5.5 %collective-permute-start.5 = (f32[56,128]{1,0:T(8,128)S(1)}, f32[56,128]{1,0:T(8,128)S(1)}, u32[]{:S(2)}, u32[]{:S(2)}) collective-permute-start(f32[56,128]{1,0:T(8,128)S(1)} %get-tuple-element.27), channel_id=1, source_target_pairs={{1,2},{3,4},{5,6},{7,8},{9,10},{11,12},{13,14},{15,16},{17,18},{19... | collective-permute-start | bytes 86024 | tf_op jit(solution)/shard_map/ppermute | solution.py:342
  39.7 0.8 copy-start.3
  41.9 1.0 %copy-start.4 = (f32[54,16,128]{2,1,0:T(8,128)S(1)}, f32[54,16,128]{2,1,0:T(8,128)}, u32[]{:S(2)}) copy-start(f32[54,16,128]{2,1,0:T(8,128)} %copy-done.3) | copy-start | bytes 1327108
  46.8 22.5 %all-to-all-start.2 = ((f32[32,56,128]{2,1,0:T(8,128)}), f32[32,56,128]{2,1,0:T(8,128)S(1)}, u32[]{:S(2)}, u32[]{:S(2)}) async-start(f32[32,56,128]{2,1,0:T(8,128)} %bitcast.7), calls=%async_computation.2 | async-start | bytes 1835008 | tf_op jit(solution)/shard_map/all_to_all | solution.py:359
  53.5 11.2 %collective-permute-start.7 = (f32[512,128]{1,0:T(8,128)S(1)}, f32[512,128]{1,0:T(8,128)S(1)}, u32[]{:S(2)}, u32[]{:S(2)}) collective-permute-start(f32[512,128]{1,0:T(8,128)S(1)} %get-tuple-element.29), channel_id=1, source_target_pairs={{0,32},{32,0},{64,96},{96,64},{128,160},{160,128},{192,224},{224,1... | collective-permute-start | bytes 786440 | tf_op jit(solution)/shard_map/ppermute | solution.py:358
  69.4 15.5 %collective-permute-start.10 = (f32[112,128]{1,0:T(8,128)S(1)}, f32[112,128]{1,0:T(8,128)S(1)}, u32[]{:S(2)}, u32[]{:S(2)}) collective-permute-start(f32[112,128]{1,0:T(8,128)S(1)} %shard_map.72), channel_id=1, source_target_pairs={{0,192},{32,224},{64,0},{96,32},{128,64},{160,96},{192,128},{224,1... | collective-permute-start | bytes 172040 | tf_op jit(solution)/shard_map/ppermute | solution.py:366
  76.6 8.3 %collective-permute-start.9 = (f32[112,128]{1,0:T(8,128)S(1)}, f32[112,128]{1,0:T(8,128)S(1)}, u32[]{:S(2)}, u32[]{:S(2)}) collective-permute-start(f32[112,128]{1,0:T(8,128)S(1)} %shard_map.72), channel_id=1, source_target_pairs={{0,64},{32,96},{64,128},{96,160},{128,192},{160,224},{192,0},{224,... | collective-permute-start | bytes 172040 | tf_op jit(solution)/shard_map/ppermute | solution.py:365
  76.6 8.3 %collective-permute-start.8 = (f32[112,128]{1,0:T(8,128)S(1)}, f32[112,128]{1,0:T(8,128)S(1)}, u32[]{:S(2)}, u32[]{:S(2)}) collective-permute-start(f32[112,128]{1,0:T(8,128)S(1)} %shard_map.72), channel_id=1, source_target_pairs={{0,128},{32,160},{64,192},{96,224},{128,0},{160,32},{192,64},{224,... | collective-permute-start | bytes 172040 | tf_op jit(solution)/shard_map/ppermute | solution.py:367
  80.1 13.8 %all-to-all-start.3 = ((f32[32,16,128]{2,1,0:T(8,128)}), f32[32,16,128]{2,1,0:T(8,128)S(1)}, u32[]{:S(2)}, u32[]{:S(2)}) async-start(f32[32,16,128]{2,1,0:T(8,128)} %bitcast.8), calls=%async_computation.3 | async-start | bytes 524288 | tf_op jit(solution)/shard_map/all_to_all | solution.py:364
  84.9 3.4 %collective-permute-start.11 = (f32[112,128]{1,0:T(8,128)S(1)}, f32[112,128]{1,0:T(8,128)S(1)}, u32[]{:S(2)}, u32[]{:S(2)}) collective-permute-start(f32[112,128]{1,0:T(8,128)S(1)} %add_add_fusion.own), channel_id=1, source_target_pairs={{0,32},{32,0},{64,96},{96,64},{128,160},{160,128},{192,224},{224,1... | collective-permute-start | bytes 172040 | tf_op jit(solution)/shard_map/ppermute | solution.py:369

commit v5 on v4

--- a/solution.py
+++ b/solution.py
@@ -251,6 +251,10 @@
             mixed[pl.ds(2 * core + j, 27, stride=4), :] = total[pl.ds(j, 27, stride=2), :]
 
 
+def add_kernel(own, other, total):
+    total[...] = own[...] + other[...]
+
+
 def final_kernel(own, other, into, onto):
     first = lax.axis_index("rows") % 2 == 0
     sums = (
@@ -294,8 +298,8 @@
     )
 
 
-def partner(n):
-    return [(i, i ^ 1) for i in range(n)]
+def partner(n, by=1):
+    return [(i, i ^ by) for i in range(n)]
 
 
 def beside(n):
@@ -306,8 +310,8 @@
     return [(i, i + 2) for i in range(1, n - 2, 2)] + [(i, i - 2) for i in range(2, n, 2)]
 
 
-def shifted(n, by):
-    return [(i, (i + by) % n) for i in range(n)]
+def mirrored(n):
+    return [(i, (n - 2 - i + 2 * (i % 2)) % n) for i in range(n)]
 
 
 def local(features, weight_in, weight_out, cotangent):
@@ -340,8 +344,8 @@
         cotangent, other_c, near, far
     )
     near_side = lax.ppermute(side, "chan", beside(32))
-    far_side = lax.ppermute(side, "chan", inward(32))
     other_tall = lax.ppermute(tall, "chan", partner(32))
+    far_side = lax.ppermute(near_side, "chan", partner(32))
     sent, own, given = call(
         main_kernel, (shape(32 * BACK, 128), shape(512, 128), shape(512, 128)), 7,
         [
@@ -361,11 +365,12 @@
     mixed = call(lambda *refs: weights_kernel(scale, *refs), shape(112, 128), 1, [pltpu.VMEM((56, 128), F32)])(
         back
     )
+    moved, mixed = lax.optimization_barrier((moved, mixed))
     image = lax.all_to_all(moved.reshape(32, 16, 128), "chan", 0, 0, tiled=True)
-    left = lax.ppermute(mixed, "rows", shifted(8, 2))
-    right = lax.ppermute(mixed, "rows", shifted(8, 6))
-    opposite = lax.ppermute(mixed, "rows", shifted(8, 4))
-    mixed = (mixed + opposite) + (left + right)
+    opposite = lax.ppermute(mixed, "rows", partner(8, 2))
+    mixed = call(add_kernel, shape(112, 128), 2, (), 10**10, 10**7)(mixed, opposite)
+    opposite = lax.ppermute(mixed, "rows", mirrored(8))
+    mixed = mixed + opposite
     counter = lax.ppermute(mixed, "rows", partner(8))
     into, onto = call(final_kernel, (shape(9, 8, 256), shape(9, 8, 128)), 2)(mixed, counter)
     rows = call(

time: 95.6 us -> 92.3 us (0.965)
  starting transfers between devices: 51.6 us -> 48 us
    ppermute x4 -> x3, starting transfers between devices: 14.2 us -> 8.26 us  [the longest x1 4.16 us: local(): opposite = lax.ppermute(mixed, 'rows', partner(8, 2))]
    all_to_all x1, waiting for transfers between devices: 4.87 us -> 0.01 us  [local(): image = lax.all_to_all(moved.reshape(32, 16, 128), 'chan', 0, 0, tiled=True)]
    ppermute x4 -> x3, waiting for transfers between devices: 0.42 us -> 3.67 us  [the longest x1 2.47 us: local(): opposite = lax.ppermute(mixed, 'rows', mirrored(8))]
    ppermute x1, waiting for transfers between devices: 2.76 us -> 4.79 us  [local(): near_side = lax.ppermute(side, 'chan', beside(32))]
    ppermute x1, starting transfers between devices: 1.57 us -> 3.6 us  [local(): counter = lax.ppermute(mixed, 'rows', partner(8))]
    ppermute x1, starting transfers between devices: 2.31 us -> 3.44 us  [local(): near_side = lax.ppermute(side, 'chan', beside(32))]
  transfers between devices with their start and end apart: 16 -> 15, of which waited for: 10 -> 10; matrix products, arithmetic and copies ran while one was open for 1% -> 1% of each run, Pallas kernels for 1% -> 1%
where the time goes in v5:
time: 92.3 us; the launch traced here: 90.9 us
  starting transfers between devices  48 us (52%)
  waiting for transfers between devices  30.4 us (33%)
  Pallas kernels  9.19 us (10%)
  local copies, waits for them, and re-layouts  1.8 us (2%)
    all_to_all x1, starting transfers between devices, local(): kernels = lax.all_to_all(packed, 'chan', 0, 0, tiled=True)  8.6 us
    ppermute x1, waiting for transfers between devices, local(): given = lax.ppermute(given, 'rows', partner(8))  6.53 us
    all_to_all x1, starting transfers between devices, local(): back = lax.all_to_all(sent.reshape(32, BACK, 128), 'chan', 0, 0, tiled=True)  5.85 us
    ppermute x1, waiting for transfers between devices, local(): near_side = lax.ppermute(side, 'chan', beside(32))  4.79 us
    ppermute x1, starting transfers between devices, local(): given = lax.ppermute(given, 'rows', partner(8))  4.71 us
    all_to_all x1, starting transfers between devices, local(): recv = lax.all_to_all(packed, 'chan', 0, 0, tiled=True)  4.71 us
    all_to_all x1, starting transfers between devices, local(): image = lax.all_to_all(moved.reshape(32, 16, 128), 'chan', 0, 0, tiled=True)  4.7 us
    ppermute x1, waiting for transfers between devices, local(): far = lax.ppermute(edge, 'rows', inward(8))  4.61 us
  transfers between devices with their start and end apart: 15, of which 10 were waited for; matrix products, arithmetic and copies ran while one was open for 1% of the time, Pallas kernels for 1%

profile of v5, /device:TPU:1, one launch (start us, length us, event | category | flops | bytes accessed | tf_op | source)
XLA Modules:
  0.0 90.9 jit_solution(2494849831963328358)
XLA Ops:
  0.7 1.9 %shard_map.67 = (f32[80,128]{1,0:T(8,128)}, f32[32,40,128]{2,1,0:T(8,128)}) custom-call(f32[12,8,256]{2,1,0:T(8,128)} %bitcast.20, f32[24,16,128]{2,1,0:T(8,128)} %own.1, f32[9,8,256]{2,1,0:T(8,128)} %bitcast.24), custom_call_target="tpu_custom_call" | custom-call | flops 1000000 | bytes 1000000 | tf_op jit(solution)/shard_map/pallas_call | solution.py:323
  2.5 8.6 %all-to-all-start = ((f32[32,40,128]{2,1,0:T(8,128)}), f32[32,40,128]{2,1,0:T(8,128)S(1)}, u32[]{:S(2)}, u32[]{:S(2)}) async-start(f32[32,40,128]{2,1,0:T(8,128)} %get-tuple-element.22), calls=%async_computation | async-start | bytes 1310720 | tf_op jit(solution)/shard_map/all_to_all | solution.py:336
  11.2 1.7 %collective-permute-start.3 = (f32[24,16,128]{2,1,0:T(8,128)S(1)}, f32[24,16,128]{2,1,0:T(8,128)S(1)}, u32[]{:S(2)}, u32[]{:S(2)}) collective-permute-start(f32[24,16,128]{2,1,0:T(8,128)S(1)} %copy-done), channel_id=1, source_target_pairs={{0,32},{32,0},{64,96},{96,64},{128,160},{160,128},{192,224},{224,1... | collective-permute-start | bytes 589832 | tf_op jit(solution)/shard_map/ppermute | solution.py:335
  12.9 0.1 collective-permute-start.2
  13.0 1.3 %collective-permute-start.1 = (f32[80,128]{1,0:T(8,128)S(1)}, f32[80,128]{1,0:T(8,128)S(1)}, u32[]{:S(2)}, u32[]{:S(2)}) collective-permute-start(f32[80,128]{1,0:T(8,128)S(1)} %copy-done.5), channel_id=1, source_target_pairs={{32,96},{96,160},{160,224},{64,0},{128,64},{192,128},{33,97},{97,1... | collective-permute-start | bytes 122888 | tf_op jit(solution)/shard_map/ppermute | solution.py:333
  14.3 0.7 collective-permute-start
  15.0 4.6 %collective-permute-done.1.far = f32[80,128]{1,0:T(8,128)S(1)} collective-permute-done((f32[80,128]{1,0:T(8,128)S(1)}, f32[80,128]{1,0:T(8,128)S(1)}, u32[]{:S(2)}, u32[]{:S(2)}) %collective-permute-start.1) | collective-permute-done | bytes 40992 | tf_op jit(solution)/shard_map/ppermute | solution.py:333
  19.6 1.3 %collective-permute-done.2.other = f32[12,8,256]{2,1,0:T(8,128)S(1)} collective-permute-done((f32[12,8,256]{2,1,0:T(8,128)S(1)}, f32[12,8,256]{2,1,0:T(8,128)S(1)}, u32[]{:S(2)}, u32[]{:S(2)}) %collective-permute-start.2) | collective-permute-done | bytes 98336 | tf_op jit(solution)/shard_map/ppermute | solution.py:334
  20.9 3.2 %all-to-all-done = f32[32,40,128]{2,1,0:T(8,128)S(1)} async-done(((f32[32,40,128]{2,1,0:T(8,128)}), f32[32,40,128]{2,1,0:T(8,128)S(1)}, u32[]{:S(2)}, u32[]{:S(2)}) %all-to-all-start) | async-done | bytes 655392 | tf_op jit(solution)/shard_map/all_to_all | solution.py:336
  24.1 1.6 %shard_map.68 = f32[32,32,128]{2,1,0:T(8,128)} custom-call(f32[12,8,256]{2,1,0:T(8,128)S(1)} %bitcast.22, f32[12,8,256]{2,1,0:T(8,128)S(1)} %collective-permute-done.2.other, f32[80,128]{1,0:T(8,128)S(1)} %collective-permute-done.near, f32[80,128]{1,0:T(8,128)S(1)} %collective-permute-done.1.far), custom_call_target="tpu_custom_call" | custom-call | flops 1000000 | bytes 1000000 | tf_op jit(solution)/shard_map/pallas_call | solution.py:338
  25.7 4.7 %all-to-all-start.1 = ((f32[32,32,128]{2,1,0:T(8,128)}), f32[32,32,128]{2,1,0:T(8,128)S(1)}, u32[]{:S(2)}, u32[]{:S(2)}) async-start(f32[32,32,128]{2,1,0:T(8,128)} %shard_map.68), calls=%async_computation.1 | async-start | bytes 1048576 | tf_op jit(solution)/shard_map/all_to_all | solution.py:341
  30.5 0.3 collective-permute-start.4
  30.8 3.4 %collective-permute-start.5 = (f32[56,128]{1,0:T(8,128)S(1)}, f32[56,128]{1,0:T(8,128)S(1)}, u32[]{:S(2)}, u32[]{:S(2)}) collective-permute-start(f32[56,128]{1,0:T(8,128)S(1)} %get-tuple-element.29), channel_id=1, source_target_pairs={{1,2},{3,4},{5,6},{7,8},{9,10},{11,12},{13,14},{15,16},{17,18},{19... | collective-permute-start | bytes 86024 | tf_op jit(solution)/shard_map/ppermute | solution.py:346
  34.2 4.8 %collective-permute-done.5.near = f32[56,128]{1,0:T(8,128)S(1)} collective-permute-done((f32[56,128]{1,0:T(8,128)S(1)}, f32[56,128]{1,0:T(8,128)S(1)}, u32[]{:S(2)}, u32[]{:S(2)}) %collective-permute-start.5) | collective-permute-done | bytes 28704 | tf_op jit(solution)/shard_map/ppermute | solution.py:346
  39.0 1.2 %collective-permute-done.6.far = f32[56,128]{1,0:T(8,128)S(1)} collective-permute-done((f32[56,128]{1,0:T(8,128)S(1)}, f32[56,128]{1,0:T(8,128)S(1)}, u32[]{:S(2)}, u32[]{:S(2)}) %collective-permute-start.6) | collective-permute-done | bytes 28704 | tf_op jit(solution)/shard_map/ppermute | solution.py:348
  40.2 0.8 copy-done.3
  41.0 0.9 %all-to-all-done.1 = f32[32,32,128]{2,1,0:T(8,128)S(1)} async-done(((f32[32,32,128]{2,1,0:T(8,128)}), f32[32,32,128]{2,1,0:T(8,128)S(1)}, u32[]{:S(2)}, u32[]{:S(2)}) %all-to-all-start.1) | async-done | bytes 524320 | tf_op jit(solution)/shard_map/all_to_all | solution.py:341
  41.9 1.0 %copy-done.4 = f32[54,16,128]{2,1,0:T(8,128)S(1)} copy-done((f32[54,16,128]{2,1,0:T(8,128)S(1)}, f32[54,16,128]{2,1,0:T(8,128)}, u32[]{:S(2)}) %copy-start.4) | copy-done | bytes 442392
  43.0 3.9 %shard_map.70 = (f32[1792,128]{1,0:T(8,128)}, f32[512,128]{1,0:T(8,128)S(1)}, f32[512,128]{1,0:T(8,128)S(1)}) custom-call(f32[1024,128]{1,0:T(8,128)S(1)} %bitcast.19, f32[1280,128]{1,0:T(8,128)S(1)} %bitcast.18, f32[54,16,128]{2,1,0:T(8,128)S(1)} %get-tuple-element.28.own, f32[54,16,128]{2,1,0:T(8,128)S(1)} %copy-done.4, ...), custom_call_target="tpu_custom_call" | custom-call | flops 1000000000 | bytes 5000000 | tf_op jit(solution)/shard_map/pallas_call | solution.py:349
  46.8 5.9 %all-to-all-start.2 = ((f32[32,56,128]{2,1,0:T(8,128)}), f32[32,56,128]{2,1,0:T(8,128)S(1)}, u32[]{:S(2)}, u32[]{:S(2)}) async-start(f32[32,56,128]{2,1,0:T(8,128)} %bitcast.7), calls=%async_computation.2 | async-start | bytes 1835008 | tf_op jit(solution)/shard_map/all_to_all | solution.py:363
  52.7 4.7 %collective-permute-start.7 = (f32[512,128]{1,0:T(8,128)S(1)}, f32[512,128]{1,0:T(8,128)S(1)}, u32[]{:S(2)}, u32[]{:S(2)}) collective-permute-start(f32[512,128]{1,0:T(8,128)S(1)} %get-tuple-element.31), channel_id=1, source_target_pairs={{0,32},{32,0},{64,96},{96,64},{128,160},{160,128},{192,224},{224,1... | collective-permute-start | bytes 786440 | tf_op jit(solution)/shard_map/ppermute | solution.py:362
  57.4 6.5 %collective-permute-done.7 = f32[512,128]{1,0:T(8,128)S(1)} collective-permute-done((f32[512,128]{1,0:T(8,128)S(1)}, f32[512,128]{1,0:T(8,128)S(1)}, u32[]{:S(2)}, u32[]{:S(2)}) %collective-permute-start.7) | collective-permute-done | bytes 262176 | tf_op jit(solution)/shard_map/ppermute | solution.py:362
  63.9 0.7 add.6
  64.7 3.8 %all-to-all-done.2.refs_0_ = f32[32,56,128]{2,1,0:T(8,128)S(1)} async-done(((f32[32,56,128]{2,1,0:T(8,128)}), f32[32,56,128]{2,1,0:T(8,128)S(1)}, u32[]{:S(2)}, u32[]{:S(2)}) %all-to-all-start.2) | async-done | bytes 917536 | tf_op jit(solution)/shard_map/all_to_all | solution.py:363
  68.5 4.2 %collective-permute-start.8 = (f32[112,128]{1,0:T(8,128)S(1)}, f32[112,128]{1,0:T(8,128)S(1)}, u32[]{:S(2)}, u32[]{:S(2)}) collective-permute-start(f32[112,128]{1,0:T(8,128)S(1)} %shard_map.71.own), channel_id=1, source_target_pairs={{0,64},{32,96},{64,0},{96,32},{128,192},{160,224},{192,128},{224,1... | collective-permute-start | bytes 172040 | tf_op jit(solution)/shard_map/ppermute | solution.py:370
  72.7 4.7 %all-to-all-start.3 = ((f32[32,16,128]{2,1,0:T(8,128)}), f32[32,16,128]{2,1,0:T(8,128)S(1)}, u32[]{:S(2)}, u32[]{:S(2)}) async-start(f32[32,16,128]{2,1,0:T(8,128)} %bitcast.8), calls=%async_computation.3 | async-start | bytes 524288 | tf_op jit(solution)/shard_map/all_to_all | solution.py:369
  77.4 4.1 %collective-permute-start.9 = (f32[112,128]{1,0:T(8,128)S(1)}, f32[112,128]{1,0:T(8,128)S(1)}, u32[]{:S(2)}, u32[]{:S(2)}) collective-permute-start(f32[112,128]{1,0:T(8,128)S(1)} %shard_map.73), channel_id=1, source_target_pairs={{0,192},{32,224},{64,128},{96,160},{128,64},{160,96},{192,0},{224,... | collective-permute-start | bytes 172040 | tf_op jit(solution)/shard_map/ppermute | solution.py:372
  81.5 2.5 %collective-permute-done.9 = f32[112,128]{1,0:T(8,128)S(1)} collective-permute-done((f32[112,128]{1,0:T(8,128)S(1)}, f32[112,128]{1,0:T(8,128)S(1)}, u32[]{:S(2)}, u32[]{:S(2)}) %collective-permute-start.9) | collective-permute-done | bytes 57376 | tf_op jit(solution)/shard_map/ppermute | solution.py:372
  84.0 3.6 %collective-permute-start.10 = (f32[112,128]{1,0:T(8,128)S(1)}, f32[112,128]{1,0:T(8,128)S(1)}, u32[]{:S(2)}, u32[]{:S(2)}) collective-permute-start(f32[112,128]{1,0:T(8,128)S(1)} %add.7.own), channel_id=1, source_target_pairs={{0,32},{32,0},{64,96},{96,64},{128,160},{160,128},{192,224},{224,1... | collective-permute-start | bytes 172040 | tf_op jit(solution)/shard_map/ppermute | solution.py:374
  87.6 1.6 %collective-permute-done.10.other = f32[112,128]{1,0:T(8,128)S(1)} collective-permute-done((f32[112,128]{1,0:T(8,128)S(1)}, f32[112,128]{1,0:T(8,128)S(1)}, u32[]{:S(2)}, u32[]{:S(2)}) %collective-permute-start.10) | collective-permute-done | bytes 57376 | tf_op jit(solution)/shard_map/ppermute | solution.py:374
  89.2 0.7 shard_map.74
  89.8 1.0 %shard_map.72 = f32[12,8,256]{2,1,0:T(8,128)} custom-call(f32[32,16,128]{2,1,0:T(8,128)S(1)} %all-to-all-done.3.recv), custom_call_target="tpu_custom_call" | custom-call | flops 99999997952 | bytes 100000000 | tf_op jit(solution)/shard_map/pallas_call | solution.py:376
  (20 shorter events, 0.2 us)
Async XLA Ops:
  0.6 10.5 %copy-start = (f32[24,16,128]{2,1,0:T(8,128)S(1)}, f32[24,16,128]{2,1,0:T(8,128)}, u32[]{:S(2)}) copy-start(f32[24,16,128]{2,1,0:T(8,128)} %own.1) | copy-start | bytes 589828
  0.6 12.3 %copy-start.1 = (f32[8,12,256]{2,0,1:T(8,128)S(1)}, f32[8,12,256]{2,0,1:T(8,128)}, u32[]{:S(2)}) copy-start(f32[8,12,256]{2,0,1:T(8,128)} %param.4) | copy-start | bytes 294916
  2.5 10.5 %copy-start.5 = (f32[80,128]{1,0:T(8,128)S(1)}, f32[80,128]{1,0:T(8,128)}, u32[]{:S(2)}) copy-start(f32[80,128]{1,0:T(8,128)} %get-tuple-element.21) | copy-start | bytes 122884
  2.5 21.5 %all-to-all-start = ((f32[32,40,128]{2,1,0:T(8,128)}), f32[32,40,128]{2,1,0:T(8,128)S(1)}, u32[]{:S(2)}, u32[]{:S(2)}) async-start(f32[32,40,128]{2,1,0:T(8,128)} %get-tuple-element.22), calls=%async_computation | async-start | bytes 1310720 | tf_op jit(solution)/shard_map/all_to_all | solution.py:336
  11.2 30.8 %copy-start.2 = (f32[256,3,3,128]{3,0,2,1:T(8,128)S(1)}, f32[256,3,3,128]{3,0,2,1:T(8,128)}, u32[]{:S(2)}) copy-start(f32[256,3,3,128]{3,0,2,1:T(8,128)} %param.6) | copy-start | bytes 3538948
  11.2 9.7 %collective-permute-start.3 = (f32[24,16,128]{2,1,0:T(8,128)S(1)}, f32[24,16,128]{2,1,0:T(8,128)S(1)}, u32[]{:S(2)}, u32[]{:S(2)}) collective-permute-start(f32[24,16,128]{2,1,0:T(8,128)S(1)} %copy-done), channel_id=1, source_target_pairs={{0,32},{32,0},{64,96},{96,64},{128,160},{160,128},{192,224},{224,1... | collective-permute-start | bytes 589832 | tf_op jit(solution)/shard_map/ppermute | solution.py:335
  12.9 8.0 %collective-permute-start.2 = (f32[12,8,256]{2,1,0:T(8,128)S(1)}, f32[12,8,256]{2,1,0:T(8,128)S(1)}, u32[]{:S(2)}, u32[]{:S(2)}) collective-permute-start(f32[12,8,256]{2,1,0:T(8,128)S(1)} %bitcast.21), channel_id=1, source_target_pairs={{0,32},{32,0},{64,96},{96,64},{128,160},{160,128},{192,224},{224,1... | collective-permute-start | bytes 294920 | tf_op jit(solution)/shard_map/ppermute | solution.py:334
  13.0 6.6 %collective-permute-start.1 = (f32[80,128]{1,0:T(8,128)S(1)}, f32[80,128]{1,0:T(8,128)S(1)}, u32[]{:S(2)}, u32[]{:S(2)}) collective-permute-start(f32[80,128]{1,0:T(8,128)S(1)} %copy-done.5), channel_id=1, source_target_pairs={{32,96},{96,160},{160,224},{64,0},{128,64},{192,128},{33,97},{97,1... | collective-permute-start | bytes 122888 | tf_op jit(solution)/shard_map/ppermute | solution.py:333
  14.3 5.3 %collective-permute-start = (f32[80,128]{1,0:T(8,128)S(1)}, f32[80,128]{1,0:T(8,128)S(1)}, u32[]{:S(2)}, u32[]{:S(2)}) collective-permute-start(f32[80,128]{1,0:T(8,128)S(1)} %copy-done.5), channel_id=1, source_target_pairs={{32,64},{96,128},{160,192},{64,32},{128,96},{192,160},{33,65},{97,... | collective-permute-start | bytes 122888 | tf_op jit(solution)/shard_map/ppermute | solution.py:332
  25.7 16.3 %all-to-all-start.1 = ((f32[32,32,128]{2,1,0:T(8,128)}), f32[32,32,128]{2,1,0:T(8,128)S(1)}, u32[]{:S(2)}, u32[]{:S(2)}) async-start(f32[32,32,128]{2,1,0:T(8,128)} %shard_map.68), calls=%async_computation.1 | async-start | bytes 1048576 | tf_op jit(solution)/shard_map/all_to_all | solution.py:341
  30.5 9.8 %collective-permute-start.4 = (f32[54,16,128]{2,1,0:T(8,128)S(1)}, f32[54,16,128]{2,1,0:T(8,128)S(1)}, u32[]{:S(2)}, u32[]{:S(2)}) collective-permute-start(f32[54,16,128]{2,1,0:T(8,128)S(1)} %get-tuple-element.28.own), channel_id=1, source_target_pairs={{0,1},{1,0},{2,3},{3,2},{4,5},{5,4},{6,7},{7,6},{8,9},{9,8},{10,11... | collective-permute-start | bytes 1327112 | tf_op jit(solution)/shard_map/ppermute | solution.py:347
  30.8 8.2 %collective-permute-start.5 = (f32[56,128]{1,0:T(8,128)S(1)}, f32[56,128]{1,0:T(8,128)S(1)}, u32[]{:S(2)}, u32[]{:S(2)}) collective-permute-start(f32[56,128]{1,0:T(8,128)S(1)} %get-tuple-element.29), channel_id=1, source_target_pairs={{1,2},{3,4},{5,6},{7,8},{9,10},{11,12},{13,14},{15,16},{17,18},{19... | collective-permute-start | bytes 86024 | tf_op jit(solution)/shard_map/ppermute | solution.py:346
  39.0 1.2 %collective-permute-start.6 = (f32[56,128]{1,0:T(8,128)S(1)}, f32[56,128]{1,0:T(8,128)S(1)}, u32[]{:S(2)}, u32[]{:S(2)}) collective-permute-start(f32[56,128]{1,0:T(8,128)S(1)} %collective-permute-done.5.near), channel_id=1, source_target_pairs={{0,1},{1,0},{2,3},{3,2},{4,5},{5,4},{6,7},{7,6},{8,9},{9,8},{10,11... | collective-permute-start | bytes 86024 | tf_op jit(solution)/shard_map/ppermute | solution.py:348
  40.2 0.8 copy-start.3
  41.9 1.0 %copy-start.4 = (f32[54,16,128]{2,1,0:T(8,128)S(1)}, f32[54,16,128]{2,1,0:T(8,128)}, u32[]{:S(2)}) copy-start(f32[54,16,128]{2,1,0:T(8,128)} %copy-done.3) | copy-start | bytes 1327108
  46.8 21.6 %all-to-all-start.2 = ((f32[32,56,128]{2,1,0:T(8,128)}), f32[32,56,128]{2,1,0:T(8,128)S(1)}, u32[]{:S(2)}, u32[]{:S(2)}) async-start(f32[32,56,128]{2,1,0:T(8,128)} %bitcast.7), calls=%async_computation.2 | async-start | bytes 1835008 | tf_op jit(solution)/shard_map/all_to_all | solution.py:363
  52.7 11.2 %collective-permute-start.7 = (f32[512,128]{1,0:T(8,128)S(1)}, f32[512,128]{1,0:T(8,128)S(1)}, u32[]{:S(2)}, u32[]{:S(2)}) collective-permute-start(f32[512,128]{1,0:T(8,128)S(1)} %get-tuple-element.31), channel_id=1, source_target_pairs={{0,32},{32,0},{64,96},{96,64},{128,160},{160,128},{192,224},{224,1... | collective-permute-start | bytes 786440 | tf_op jit(solution)/shard_map/ppermute | solution.py:362
  68.5 8.9 %collective-permute-start.8 = (f32[112,128]{1,0:T(8,128)S(1)}, f32[112,128]{1,0:T(8,128)S(1)}, u32[]{:S(2)}, u32[]{:S(2)}) collective-permute-start(f32[112,128]{1,0:T(8,128)S(1)} %shard_map.71.own), channel_id=1, source_target_pairs={{0,64},{32,96},{64,0},{96,32},{128,192},{160,224},{192,128},{224,1... | collective-permute-start | bytes 172040 | tf_op jit(solution)/shard_map/ppermute | solution.py:370
  72.7 17.1 %all-to-all-start.3 = ((f32[32,16,128]{2,1,0:T(8,128)}), f32[32,16,128]{2,1,0:T(8,128)S(1)}, u32[]{:S(2)}, u32[]{:S(2)}) async-start(f32[32,16,128]{2,1,0:T(8,128)} %bitcast.8), calls=%async_computation.3 | async-start | bytes 524288 | tf_op jit(solution)/shard_map/all_to_all | solution.py:369
  77.4 6.6 %collective-permute-start.9 = (f32[112,128]{1,0:T(8,128)S(1)}, f32[112,128]{1,0:T(8,128)S(1)}, u32[]{:S(2)}, u32[]{:S(2)}) collective-permute-start(f32[112,128]{1,0:T(8,128)S(1)} %shard_map.73), channel_id=1, source_target_pairs={{0,192},{32,224},{64,128},{96,160},{128,64},{160,96},{192,0},{224,... | collective-permute-start | bytes 172040 | tf_op jit(solution)/shard_map/ppermute | solution.py:372
  84.0 5.2 %collective-permute-start.10 = (f32[112,128]{1,0:T(8,128)S(1)}, f32[112,128]{1,0:T(8,128)S(1)}, u32[]{:S(2)}, u32[]{:S(2)}) collective-permute-start(f32[112,128]{1,0:T(8,128)S(1)} %add.7.own), channel_id=1, source_target_pairs={{0,32},{32,0},{64,96},{96,64},{128,160},{160,128},{192,224},{224,1... | collective-permute-start | bytes 172040 | tf_op jit(solution)/shard_map/ppermute | solution.py:374

commit v6 on v5

--- a/solution.py
+++ b/solution.py
@@ -372,11 +372,12 @@
     opposite = lax.ppermute(mixed, "rows", mirrored(8))
     mixed = mixed + opposite
     counter = lax.ppermute(mixed, "rows", partner(8))
-    into, onto = call(final_kernel, (shape(9, 8, 256), shape(9, 8, 128)), 2)(mixed, counter)
     rows = call(
         image_kernel, shape(12, 8, 256), 1,
-        [pltpu.VMEM((12, 8, 512), F32), pltpu.VMEM((8, 256), F32)], 10**11, 10**8,
+        [pltpu.VMEM((12, 8, 512), F32), pltpu.VMEM((8, 256), F32)],
     )(image)
+    rows, counter = lax.optimization_barrier((rows, counter))
+    into, onto = call(final_kernel, (shape(9, 8, 256), shape(9, 8, 128)), 2)(mixed, counter)
     grad_image = jnp.transpose(rows, (1, 0, 2))
     grad_in = jnp.transpose(into.reshape(3, 3, 8, 256), (2, 0, 1, 3))
     grad_out = jnp.transpose(onto.reshape(3, 3, 8, 128), (2, 0, 1, 3))

time: 92.3 us -> 91.3 us (0.989)
  waiting for transfers between devices: 30.4 us -> 29.3 us
    ppermute x1, waiting for transfers between devices: 1.57 us -> 0.52 us  [local(): counter = lax.ppermute(mixed, 'rows', partner(8))]
where the time goes in v6:
time: 91.3 us; the launch traced here: 89.8 us
  starting transfers between devices  48 us (53%)
  waiting for transfers between devices  29.3 us (32%)
  Pallas kernels  9.2 us (10%)
  local copies, waits for them, and re-layouts  1.8 us (2%)
    all_to_all x1, starting transfers between devices, local(): kernels = lax.all_to_all(packed, 'chan', 0, 0, tiled=True)  8.6 us
    ppermute x1, waiting for transfers between devices, local(): given = lax.ppermute(given, 'rows', partner(8))  6.53 us
    all_to_all x1, starting transfers between devices, local(): back = lax.all_to_all(sent.reshape(32, BACK, 128), 'chan', 0, 0, tiled=True)  5.85 us
    ppermute x1, waiting for transfers between devices, local(): near_side = lax.ppermute(side, 'chan', beside(32))  4.79 us
    ppermute x1, starting transfers between devices, local(): given = lax.ppermute(given, 'rows', partner(8))  4.71 us
    all_to_all x1, starting transfers between devices, local(): recv = lax.all_to_all(packed, 'chan', 0, 0, tiled=True)  4.71 us
    all_to_all x1, starting transfers between devices, local(): image = lax.all_to_all(moved.reshape(32, 16, 128), 'chan', 0, 0, tiled=True)  4.7 us
    ppermute x1, waiting for transfers between devices, local(): far = lax.ppermute(edge, 'rows', inward(8))  4.61 us
  transfers between devices with their start and end apart: 15, of which 10 were waited for; matrix products, arithmetic and copies ran while one was open for 1% of the time, Pallas kernels for 1%

profile of v6, /device:TPU:1, one launch (start us, length us, event | category | flops | bytes accessed | tf_op | source)
XLA Modules:
  0.0 89.8 jit_solution(16947871965288589827)
XLA Ops:
  0.7 1.9 %shard_map.67 = (f32[80,128]{1,0:T(8,128)}, f32[32,40,128]{2,1,0:T(8,128)}) custom-call(f32[12,8,256]{2,1,0:T(8,128)} %bitcast.20, f32[24,16,128]{2,1,0:T(8,128)} %own.1, f32[9,8,256]{2,1,0:T(8,128)} %bitcast.25), custom_call_target="tpu_custom_call" | custom-call | flops 1000000 | bytes 1000000 | tf_op jit(solution)/shard_map/pallas_call | solution.py:323
  2.5 8.6 %all-to-all-start = ((f32[32,40,128]{2,1,0:T(8,128)}), f32[32,40,128]{2,1,0:T(8,128)S(1)}, u32[]{:S(2)}, u32[]{:S(2)}) async-start(f32[32,40,128]{2,1,0:T(8,128)} %get-tuple-element.24), calls=%async_computation | async-start | bytes 1310720 | tf_op jit(solution)/shard_map/all_to_all | solution.py:336
  11.2 1.7 %collective-permute-start.3 = (f32[24,16,128]{2,1,0:T(8,128)S(1)}, f32[24,16,128]{2,1,0:T(8,128)S(1)}, u32[]{:S(2)}, u32[]{:S(2)}) collective-permute-start(f32[24,16,128]{2,1,0:T(8,128)S(1)} %copy-done), channel_id=1, source_target_pairs={{0,32},{32,0},{64,96},{96,64},{128,160},{160,128},{192,224},{224,1... | collective-permute-start | bytes 589832 | tf_op jit(solution)/shard_map/ppermute | solution.py:335
  12.9 0.1 collective-permute-start.2
  13.0 1.3 %collective-permute-start.1 = (f32[80,128]{1,0:T(8,128)S(1)}, f32[80,128]{1,0:T(8,128)S(1)}, u32[]{:S(2)}, u32[]{:S(2)}) collective-permute-start(f32[80,128]{1,0:T(8,128)S(1)} %copy-done.5), channel_id=1, source_target_pairs={{32,96},{96,160},{160,224},{64,0},{128,64},{192,128},{33,97},{97,1... | collective-permute-start | bytes 122888 | tf_op jit(solution)/shard_map/ppermute | solution.py:333
  14.3 0.7 collective-permute-start
  15.0 4.6 %collective-permute-done.1.far = f32[80,128]{1,0:T(8,128)S(1)} collective-permute-done((f32[80,128]{1,0:T(8,128)S(1)}, f32[80,128]{1,0:T(8,128)S(1)}, u32[]{:S(2)}, u32[]{:S(2)}) %collective-permute-start.1) | collective-permute-done | bytes 40992 | tf_op jit(solution)/shard_map/ppermute | solution.py:333
  19.6 1.3 %collective-permute-done.2.other = f32[12,8,256]{2,1,0:T(8,128)S(1)} collective-permute-done((f32[12,8,256]{2,1,0:T(8,128)S(1)}, f32[12,8,256]{2,1,0:T(8,128)S(1)}, u32[]{:S(2)}, u32[]{:S(2)}) %collective-permute-start.2) | collective-permute-done | bytes 98336 | tf_op jit(solution)/shard_map/ppermute | solution.py:334
  20.9 3.2 %all-to-all-done = f32[32,40,128]{2,1,0:T(8,128)S(1)} async-done(((f32[32,40,128]{2,1,0:T(8,128)}), f32[32,40,128]{2,1,0:T(8,128)S(1)}, u32[]{:S(2)}, u32[]{:S(2)}) %all-to-all-start) | async-done | bytes 655392 | tf_op jit(solution)/shard_map/all_to_all | solution.py:336
  24.1 1.6 %shard_map.68 = f32[32,32,128]{2,1,0:T(8,128)} custom-call(f32[12,8,256]{2,1,0:T(8,128)S(1)} %bitcast.22, f32[12,8,256]{2,1,0:T(8,128)S(1)} %collective-permute-done.2.other, f32[80,128]{1,0:T(8,128)S(1)} %collective-permute-done.near, f32[80,128]{1,0:T(8,128)S(1)} %collective-permute-done.1.far), custom_call_target="tpu_custom_call" | custom-call | flops 1000000 | bytes 1000000 | tf_op jit(solution)/shard_map/pallas_call | solution.py:338
  25.7 4.7 %all-to-all-start.1 = ((f32[32,32,128]{2,1,0:T(8,128)}), f32[32,32,128]{2,1,0:T(8,128)S(1)}, u32[]{:S(2)}, u32[]{:S(2)}) async-start(f32[32,32,128]{2,1,0:T(8,128)} %shard_map.68), calls=%async_computation.1 | async-start | bytes 1048576 | tf_op jit(solution)/shard_map/all_to_all | solution.py:341
  30.5 0.3 collective-permute-start.4
  30.8 3.4 %collective-permute-start.5 = (f32[56,128]{1,0:T(8,128)S(1)}, f32[56,128]{1,0:T(8,128)S(1)}, u32[]{:S(2)}, u32[]{:S(2)}) collective-permute-start(f32[56,128]{1,0:T(8,128)S(1)} %get-tuple-element.31), channel_id=1, source_target_pairs={{1,2},{3,4},{5,6},{7,8},{9,10},{11,12},{13,14},{15,16},{17,18},{19... | collective-permute-start | bytes 86024 | tf_op jit(solution)/shard_map/ppermute | solution.py:346
  34.2 4.8 %collective-permute-done.5.near = f32[56,128]{1,0:T(8,128)S(1)} collective-permute-done((f32[56,128]{1,0:T(8,128)S(1)}, f32[56,128]{1,0:T(8,128)S(1)}, u32[]{:S(2)}, u32[]{:S(2)}) %collective-permute-start.5) | collective-permute-done | bytes 28704 | tf_op jit(solution)/shard_map/ppermute | solution.py:346
  39.0 1.2 %collective-permute-done.6.far = f32[56,128]{1,0:T(8,128)S(1)} collective-permute-done((f32[56,128]{1,0:T(8,128)S(1)}, f32[56,128]{1,0:T(8,128)S(1)}, u32[]{:S(2)}, u32[]{:S(2)}) %collective-permute-start.6) | collective-permute-done | bytes 28704 | tf_op jit(solution)/shard_map/ppermute | solution.py:348
  40.2 0.8 copy-done.3
  41.0 0.9 %all-to-all-done.1 = f32[32,32,128]{2,1,0:T(8,128)S(1)} async-done(((f32[32,32,128]{2,1,0:T(8,128)}), f32[32,32,128]{2,1,0:T(8,128)S(1)}, u32[]{:S(2)}, u32[]{:S(2)}) %all-to-all-start.1) | async-done | bytes 524320 | tf_op jit(solution)/shard_map/all_to_all | solution.py:341
  41.9 1.0 %copy-done.4 = f32[54,16,128]{2,1,0:T(8,128)S(1)} copy-done((f32[54,16,128]{2,1,0:T(8,128)S(1)}, f32[54,16,128]{2,1,0:T(8,128)}, u32[]{:S(2)}) %copy-start.4) | copy-done | bytes 442392
  43.0 3.9 %shard_map.70 = (f32[1792,128]{1,0:T(8,128)}, f32[512,128]{1,0:T(8,128)S(1)}, f32[512,128]{1,0:T(8,128)S(1)}) custom-call(f32[1024,128]{1,0:T(8,128)S(1)} %bitcast.19, f32[1280,128]{1,0:T(8,128)S(1)} %bitcast.18, f32[54,16,128]{2,1,0:T(8,128)S(1)} %get-tuple-element.30.own, f32[54,16,128]{2,1,0:T(8,128)S(1)} %copy-done.4, ...), custom_call_target="tpu_custom_call" | custom-call | flops 1000000000 | bytes 5000000 | tf_op jit(solution)/shard_map/pallas_call | solution.py:349
  46.8 5.9 %all-to-all-start.2 = ((f32[32,56,128]{2,1,0:T(8,128)}), f32[32,56,128]{2,1,0:T(8,128)S(1)}, u32[]{:S(2)}, u32[]{:S(2)}) async-start(f32[32,56,128]{2,1,0:T(8,128)} %bitcast.7), calls=%async_computation.2 | async-start | bytes 1835008 | tf_op jit(solution)/shard_map/all_to_all | solution.py:363
  52.7 4.7 %collective-permute-start.7 = (f32[512,128]{1,0:T(8,128)S(1)}, f32[512,128]{1,0:T(8,128)S(1)}, u32[]{:S(2)}, u32[]{:S(2)}) collective-permute-start(f32[512,128]{1,0:T(8,128)S(1)} %get-tuple-element.33), channel_id=1, source_target_pairs={{0,32},{32,0},{64,96},{96,64},{128,160},{160,128},{192,224},{224,1... | collective-permute-start | bytes 786440 | tf_op jit(solution)/shard_map/ppermute | solution.py:362
  57.4 6.5 %collective-permute-done.7 = f32[512,128]{1,0:T(8,128)S(1)} collective-permute-done((f32[512,128]{1,0:T(8,128)S(1)}, f32[512,128]{1,0:T(8,128)S(1)}, u32[]{:S(2)}, u32[]{:S(2)}) %collective-permute-start.7) | collective-permute-done | bytes 262176 | tf_op jit(solution)/shard_map/ppermute | solution.py:362
  63.9 0.7 add.6
  64.7 3.8 %all-to-all-done.2.refs_0_ = f32[32,56,128]{2,1,0:T(8,128)S(1)} async-done(((f32[32,56,128]{2,1,0:T(8,128)}), f32[32,56,128]{2,1,0:T(8,128)S(1)}, u32[]{:S(2)}, u32[]{:S(2)}) %all-to-all-start.2) | async-done | bytes 917536 | tf_op jit(solution)/shard_map/all_to_all | solution.py:363
  68.5 4.2 %collective-permute-start.8 = (f32[112,128]{1,0:T(8,128)S(1)}, f32[112,128]{1,0:T(8,128)S(1)}, u32[]{:S(2)}, u32[]{:S(2)}) collective-permute-start(f32[112,128]{1,0:T(8,128)S(1)} %shard_map.71.own), channel_id=1, source_target_pairs={{0,64},{32,96},{64,0},{96,32},{128,192},{160,224},{192,128},{224,1... | collective-permute-start | bytes 172040 | tf_op jit(solution)/shard_map/ppermute | solution.py:370
  72.7 4.7 %all-to-all-start.3 = ((f32[32,16,128]{2,1,0:T(8,128)}), f32[32,16,128]{2,1,0:T(8,128)S(1)}, u32[]{:S(2)}, u32[]{:S(2)}) async-start(f32[32,16,128]{2,1,0:T(8,128)} %bitcast.8), calls=%async_computation.3 | async-start | bytes 524288 | tf_op jit(solution)/shard_map/all_to_all | solution.py:369
  77.4 4.1 %collective-permute-start.9 = (f32[112,128]{1,0:T(8,128)S(1)}, f32[112,128]{1,0:T(8,128)S(1)}, u32[]{:S(2)}, u32[]{:S(2)}) collective-permute-start(f32[112,128]{1,0:T(8,128)S(1)} %shard_map.73), channel_id=1, source_target_pairs={{0,192},{32,224},{64,128},{96,160},{128,64},{160,96},{192,0},{224,... | collective-permute-start | bytes 172040 | tf_op jit(solution)/shard_map/ppermute | solution.py:372
  81.5 2.5 %collective-permute-done.9 = f32[112,128]{1,0:T(8,128)S(1)} collective-permute-done((f32[112,128]{1,0:T(8,128)S(1)}, f32[112,128]{1,0:T(8,128)S(1)}, u32[]{:S(2)}, u32[]{:S(2)}) %collective-permute-start.9) | collective-permute-done | bytes 57376 | tf_op jit(solution)/shard_map/ppermute | solution.py:372
  84.0 3.6 %collective-permute-start.10 = (f32[112,128]{1,0:T(8,128)S(1)}, f32[112,128]{1,0:T(8,128)S(1)}, u32[]{:S(2)}, u32[]{:S(2)}) collective-permute-start(f32[112,128]{1,0:T(8,128)S(1)} %add.7.own), channel_id=1, source_target_pairs={{0,32},{32,0},{64,96},{96,64},{128,160},{160,128},{192,224},{224,1... | collective-permute-start | bytes 172040 | tf_op jit(solution)/shard_map/ppermute | solution.py:374
  87.6 1.0 %shard_map.72 = f32[12,8,256]{2,1,0:T(8,128)} custom-call(f32[32,16,128]{2,1,0:T(8,128)S(1)} %all-to-all-done.3.recv), custom_call_target="tpu_custom_call" | custom-call | flops 1000000 | bytes 1000000 | tf_op jit(solution)/shard_map/pallas_call | solution.py:375
  88.6 0.5 collective-permute-done.10.other
  89.2 0.7 shard_map.74
  (20 shorter events, 0.2 us)
Async XLA Ops:
  0.6 10.5 %copy-start = (f32[24,16,128]{2,1,0:T(8,128)S(1)}, f32[24,16,128]{2,1,0:T(8,128)}, u32[]{:S(2)}) copy-start(f32[24,16,128]{2,1,0:T(8,128)} %own.1) | copy-start | bytes 589828
  0.6 12.3 %copy-start.1 = (f32[8,12,256]{2,0,1:T(8,128)S(1)}, f32[8,12,256]{2,0,1:T(8,128)}, u32[]{:S(2)}) copy-start(f32[8,12,256]{2,0,1:T(8,128)} %param.4) | copy-start | bytes 294916
  2.5 10.5 %copy-start.5 = (f32[80,128]{1,0:T(8,128)S(1)}, f32[80,128]{1,0:T(8,128)}, u32[]{:S(2)}) copy-start(f32[80,128]{1,0:T(8,128)} %get-tuple-element.23) | copy-start | bytes 122884
  2.5 21.5 %all-to-all-start = ((f32[32,40,128]{2,1,0:T(8,128)}), f32[32,40,128]{2,1,0:T(8,128)S(1)}, u32[]{:S(2)}, u32[]{:S(2)}) async-start(f32[32,40,128]{2,1,0:T(8,128)} %get-tuple-element.24), calls=%async_computation | async-start | bytes 1310720 | tf_op jit(solution)/shard_map/all_to_all | solution.py:336
  11.2 30.8 %copy-start.2 = (f32[256,3,3,128]{3,0,2,1:T(8,128)S(1)}, f32[256,3,3,128]{3,0,2,1:T(8,128)}, u32[]{:S(2)}) copy-start(f32[256,3,3,128]{3,0,2,1:T(8,128)} %param.6) | copy-start | bytes 3538948
  11.2 9.7 %collective-permute-start.3 = (f32[24,16,128]{2,1,0:T(8,128)S(1)}, f32[24,16,128]{2,1,0:T(8,128)S(1)}, u32[]{:S(2)}, u32[]{:S(2)}) collective-permute-start(f32[24,16,128]{2,1,0:T(8,128)S(1)} %copy-done), channel_id=1, source_target_pairs={{0,32},{32,0},{64,96},{96,64},{128,160},{160,128},{192,224},{224,1... | collective-permute-start | bytes 589832 | tf_op jit(solution)/shard_map/ppermute | solution.py:335
  12.9 8.0 %collective-permute-start.2 = (f32[12,8,256]{2,1,0:T(8,128)S(1)}, f32[12,8,256]{2,1,0:T(8,128)S(1)}, u32[]{:S(2)}, u32[]{:S(2)}) collective-permute-start(f32[12,8,256]{2,1,0:T(8,128)S(1)} %bitcast.21), channel_id=1, source_target_pairs={{0,32},{32,0},{64,96},{96,64},{128,160},{160,128},{192,224},{224,1... | collective-permute-start | bytes 294920 | tf_op jit(solution)/shard_map/ppermute | solution.py:334
  13.0 6.6 %collective-permute-start.1 = (f32[80,128]{1,0:T(8,128)S(1)}, f32[80,128]{1,0:T(8,128)S(1)}, u32[]{:S(2)}, u32[]{:S(2)}) collective-permute-start(f32[80,128]{1,0:T(8,128)S(1)} %copy-done.5), channel_id=1, source_target_pairs={{32,96},{96,160},{160,224},{64,0},{128,64},{192,128},{33,97},{97,1... | collective-permute-start | bytes 122888 | tf_op jit(solution)/shard_map/ppermute | solution.py:333
  14.3 5.3 %collective-permute-start = (f32[80,128]{1,0:T(8,128)S(1)}, f32[80,128]{1,0:T(8,128)S(1)}, u32[]{:S(2)}, u32[]{:S(2)}) collective-permute-start(f32[80,128]{1,0:T(8,128)S(1)} %copy-done.5), channel_id=1, source_target_pairs={{32,64},{96,128},{160,192},{64,32},{128,96},{192,160},{33,65},{97,... | collective-permute-start | bytes 122888 | tf_op jit(solution)/shard_map/ppermute | solution.py:332
  25.7 16.3 %all-to-all-start.1 = ((f32[32,32,128]{2,1,0:T(8,128)}), f32[32,32,128]{2,1,0:T(8,128)S(1)}, u32[]{:S(2)}, u32[]{:S(2)}) async-start(f32[32,32,128]{2,1,0:T(8,128)} %shard_map.68), calls=%async_computation.1 | async-start | bytes 1048576 | tf_op jit(solution)/shard_map/all_to_all | solution.py:341
  30.5 9.8 %collective-permute-start.4 = (f32[54,16,128]{2,1,0:T(8,128)S(1)}, f32[54,16,128]{2,1,0:T(8,128)S(1)}, u32[]{:S(2)}, u32[]{:S(2)}) collective-permute-start(f32[54,16,128]{2,1,0:T(8,128)S(1)} %get-tuple-element.30.own), channel_id=1, source_target_pairs={{0,1},{1,0},{2,3},{3,2},{4,5},{5,4},{6,7},{7,6},{8,9},{9,8},{10,11... | collective-permute-start | bytes 1327112 | tf_op jit(solution)/shard_map/ppermute | solution.py:347
  30.8 8.2 %collective-permute-start.5 = (f32[56,128]{1,0:T(8,128)S(1)}, f32[56,128]{1,0:T(8,128)S(1)}, u32[]{:S(2)}, u32[]{:S(2)}) collective-permute-start(f32[56,128]{1,0:T(8,128)S(1)} %get-tuple-element.31), channel_id=1, source_target_pairs={{1,2},{3,4},{5,6},{7,8},{9,10},{11,12},{13,14},{15,16},{17,18},{19... | collective-permute-start | bytes 86024 | tf_op jit(solution)/shard_map/ppermute | solution.py:346
  39.0 1.2 %collective-permute-start.6 = (f32[56,128]{1,0:T(8,128)S(1)}, f32[56,128]{1,0:T(8,128)S(1)}, u32[]{:S(2)}, u32[]{:S(2)}) collective-permute-start(f32[56,128]{1,0:T(8,128)S(1)} %collective-permute-done.5.near), channel_id=1, source_target_pairs={{0,1},{1,0},{2,3},{3,2},{4,5},{5,4},{6,7},{7,6},{8,9},{9,8},{10,11... | collective-permute-start | bytes 86024 | tf_op jit(solution)/shard_map/ppermute | solution.py:348
  40.2 0.8 copy-start.3
  41.9 1.0 %copy-start.4 = (f32[54,16,128]{2,1,0:T(8,128)S(1)}, f32[54,16,128]{2,1,0:T(8,128)}, u32[]{:S(2)}) copy-start(f32[54,16,128]{2,1,0:T(8,128)} %copy-done.3) | copy-start | bytes 1327108
  46.8 21.6 %all-to-all-start.2 = ((f32[32,56,128]{2,1,0:T(8,128)}), f32[32,56,128]{2,1,0:T(8,128)S(1)}, u32[]{:S(2)}, u32[]{:S(2)}) async-start(f32[32,56,128]{2,1,0:T(8,128)} %bitcast.7), calls=%async_computation.2 | async-start | bytes 1835008 | tf_op jit(solution)/shard_map/all_to_all | solution.py:363
  52.7 11.2 %collective-permute-start.7 = (f32[512,128]{1,0:T(8,128)S(1)}, f32[512,128]{1,0:T(8,128)S(1)}, u32[]{:S(2)}, u32[]{:S(2)}) collective-permute-start(f32[512,128]{1,0:T(8,128)S(1)} %get-tuple-element.33), channel_id=1, source_target_pairs={{0,32},{32,0},{64,96},{96,64},{128,160},{160,128},{192,224},{224,1... | collective-permute-start | bytes 786440 | tf_op jit(solution)/shard_map/ppermute | solution.py:362
  68.5 8.9 %collective-permute-start.8 = (f32[112,128]{1,0:T(8,128)S(1)}, f32[112,128]{1,0:T(8,128)S(1)}, u32[]{:S(2)}, u32[]{:S(2)}) collective-permute-start(f32[112,128]{1,0:T(8,128)S(1)} %shard_map.71.own), channel_id=1, source_target_pairs={{0,64},{32,96},{64,0},{96,32},{128,192},{160,224},{192,128},{224,1... | collective-permute-start | bytes 172040 | tf_op jit(solution)/shard_map/ppermute | solution.py:370
  72.7 14.9 %all-to-all-start.3 = ((f32[32,16,128]{2,1,0:T(8,128)}), f32[32,16,128]{2,1,0:T(8,128)S(1)}, u32[]{:S(2)}, u32[]{:S(2)}) async-start(f32[32,16,128]{2,1,0:T(8,128)} %bitcast.8), calls=%async_computation.3 | async-start | bytes 524288 | tf_op jit(solution)/shard_map/all_to_all | solution.py:369
  77.4 6.6 %collective-permute-start.9 = (f32[112,128]{1,0:T(8,128)S(1)}, f32[112,128]{1,0:T(8,128)S(1)}, u32[]{:S(2)}, u32[]{:S(2)}) collective-permute-start(f32[112,128]{1,0:T(8,128)S(1)} %shard_map.73), channel_id=1, source_target_pairs={{0,192},{32,224},{64,128},{96,160},{128,64},{160,96},{192,0},{224,... | collective-permute-start | bytes 172040 | tf_op jit(solution)/shard_map/ppermute | solution.py:372
  84.0 5.2 %collective-permute-start.10 = (f32[112,128]{1,0:T(8,128)S(1)}, f32[112,128]{1,0:T(8,128)S(1)}, u32[]{:S(2)}, u32[]{:S(2)}) collective-permute-start(f32[112,128]{1,0:T(8,128)S(1)} %add.7.own), channel_id=1, source_target_pairs={{0,32},{32,0},{64,96},{96,64},{128,160},{160,128},{192,224},{224,1... | collective-permute-start | bytes 172040 | tf_op jit(solution)/shard_map/ppermute | solution.py:374

commit v7 on v6

--- a/solution.py
+++ b/solution.py
@@ -160,11 +160,7 @@
     return STEP * (t // 3 == 0) + (t % 3 == 0)
 
 
-def main_kernel(
-    recv, kernels, own, other, near, far, weight, out, mine, theirs,
-    cells, sums, x_high, x_low, w_high, w_low, g_high, g_low,
-):
-    parts, grad = windows(own, other, near, far, weight, sums, cells)
+def hidden_kernel(recv, kernels, result, x_high, x_low, w_high, w_low):
     for pair in range(16):
         for q in range(4):
             tile = jnp.concatenate(
@@ -187,6 +183,17 @@
     hidden = each[0:64]
     for t in range(1, 9):
         hidden = hidden + pltpu.roll(each[t * 64 : t * 64 + 64], FLAT - ((t // 3) * STEP + t % 3), 1)
+    result[...] = hidden
+
+
+def main_kernel(
+    forward, x_high, x_low, w_high, w_low, own, other, near, far, weight, out, mine, theirs,
+    cells, sums, g_high, g_low,
+):
+    parts, grad = windows(own, other, near, far, weight, sums, cells)
+    hidden = forward[...]
+    weights = (w_high[...], w_low[...])
+    image = (x_high[...], x_low[...])
     at = lax.broadcasted_iota(jnp.int32, (64, FLAT), 1)
     block = lax.axis_index("rows") // 2
     across = at % STEP < BLOCK
@@ -346,17 +353,23 @@
     near_side = lax.ppermute(side, "chan", beside(32))
     other_tall = lax.ppermute(tall, "chan", partner(32))
     far_side = lax.ppermute(near_side, "chan", partner(32))
+    forward = call(
+        hidden_kernel,
+        (
+            shape(64, FLAT), shape(256, FLAT, dtype=BF16), shape(256, FLAT, dtype=BF16),
+            shape(576, 256, dtype=BF16), shape(576, 256, dtype=BF16),
+        ),
+        2, (), 5 * 10**9, 5 * 10**6,
+    )(recv.reshape(1024, 128), kernels.reshape(32 * PACK, 128))
     sent, own, given = call(
-        main_kernel, (shape(32 * BACK, 128), shape(512, 128), shape(512, 128)), 7,
+        main_kernel, (shape(32 * BACK, 128), shape(512, 128), shape(512, 128)), 10,
         [
             pltpu.VMEM((FINE, 48, 128), F32), pltpu.VMEM((FLAT, 512), F32),
-            pltpu.VMEM((256, FLAT), BF16), pltpu.VMEM((256, FLAT), BF16),
-            pltpu.VMEM((576, 256), BF16), pltpu.VMEM((576, 256), BF16),
             pltpu.VMEM((576, FLAT), BF16), pltpu.VMEM((576, FLAT), BF16),
         ],
         10**9, 5 * 10**6,
     )(
-        recv.reshape(1024, 128), kernels.reshape(32 * PACK, 128), tall, other_tall, near_side, far_side,
+        *forward, tall, other_tall, near_side, far_side,
         jnp.transpose(weight_out, (1, 2, 0, 3)).reshape(2304, 128),
     )
     given = lax.ppermute(given, "rows", partner(8))

time: 91.3 us -> 89.1 us (0.976)
  starting transfers between devices: 48 us -> 46 us
  local copies, waits for them, and re-layouts: 1.8 us -> 0.34 us
  waiting for transfers between devices: 29.3 us -> 30.3 us
    all_to_all x1, waiting for transfers between devices: 0.93 us -> 2.9 us  [local(): recv = lax.all_to_all(packed, 'chan', 0, 0, tiled=True)]
    all_to_all x1, starting transfers between devices: 5.85 us -> 4.02 us  [local(): back = lax.all_to_all(sent.reshape(32, BACK, 128), 'chan', 0, 0, tiled=True)]
    unnamed x12 -> x8, local copies, waits for them, and re-layouts: 1.8 us -> 0.34 us
    ppermute x1, waiting for transfers between devices: 1.2 us -> 0.01 us  [local(): far_side = lax.ppermute(near_side, 'chan', partner(32))]
    pallas_call x0 -> x1, Pallas kernels: none -> 0.92 us  [local(): call(hidden_kernel, (shape(64, FLAT), shape(256, FLAT, dtype=BF16), shape...]
  transfers between devices with their start and end apart: 15 -> 15, of which waited for: 10 -> 9; matrix products, arithmetic and copies ran while one was open for 1% -> 1% of each run, Pallas kernels for 1% -> 2%
where the time goes in v7:
time: 89.1 us; the launch traced here: 87.6 us
  starting transfers between devices  46 us (52%)
  waiting for transfers between devices  30.3 us (34%)
  Pallas kernels  9.38 us (11%)
    all_to_all x1, starting transfers between devices, local(): kernels = lax.all_to_all(packed, 'chan', 0, 0, tiled=True)  8.6 us
    ppermute x1, waiting for transfers between devices, local(): given = lax.ppermute(given, 'rows', partner(8))  6.4 us
    ppermute x1, waiting for transfers between devices, local(): near_side = lax.ppermute(side, 'chan', beside(32))  4.92 us
    ppermute x1, starting transfers between devices, local(): given = lax.ppermute(given, 'rows', partner(8))  4.71 us
    all_to_all x1, starting transfers between devices, local(): image = lax.all_to_all(moved.reshape(32, 16, 128), 'chan', 0, 0, tiled=True)  4.71 us
    all_to_all x1, starting transfers between devices, local(): recv = lax.all_to_all(packed, 'chan', 0, 0, tiled=True)  4.69 us
    ppermute x1, waiting for transfers between devices, local(): far = lax.ppermute(edge, 'rows', inward(8))  4.61 us
    ppermute x1, starting transfers between devices, local(): opposite = lax.ppermute(mixed, 'rows', partner(8, 2))  4.16 us
  transfers between devices with their start and end apart: 15, of which 9 were waited for; matrix products, arithmetic and copies ran while one was open for 1% of the time, Pallas kernels for 2%

profile of v7, /device:TPU:1, one launch (start us, length us, event | category | flops | bytes accessed | tf_op | source)
XLA Modules:
  0.0 87.6 jit_solution(3626918424617244170)
XLA Ops:
  0.7 1.9 %shard_map.67 = (f32[80,128]{1,0:T(8,128)}, f32[32,40,128]{2,1,0:T(8,128)}) custom-call(f32[12,8,256]{2,1,0:T(8,128)} %bitcast.20, f32[24,16,128]{2,1,0:T(8,128)} %own.1, f32[9,8,256]{2,1,0:T(8,128)} %bitcast.25), custom_call_target="tpu_custom_call" | custom-call | flops 1000000 | bytes 1000000 | tf_op jit(solution)/shard_map/pallas_call | solution.py:330
  2.5 8.6 %all-to-all-start = ((f32[32,40,128]{2,1,0:T(8,128)}), f32[32,40,128]{2,1,0:T(8,128)S(1)}, u32[]{:S(2)}, u32[]{:S(2)}) async-start(f32[32,40,128]{2,1,0:T(8,128)} %get-tuple-element.29), calls=%async_computation | async-start | bytes 1310720 | tf_op jit(solution)/shard_map/all_to_all | solution.py:343
  11.2 1.7 %collective-permute-start.3 = (f32[24,16,128]{2,1,0:T(8,128)S(1)}, f32[24,16,128]{2,1,0:T(8,128)S(1)}, u32[]{:S(2)}, u32[]{:S(2)}) collective-permute-start(f32[24,16,128]{2,1,0:T(8,128)S(1)} %copy-done), channel_id=1, source_target_pairs={{0,32},{32,0},{64,96},{96,64},{128,160},{160,128},{192,224},{224,1... | collective-permute-start | bytes 589832 | tf_op jit(solution)/shard_map/ppermute | solution.py:342
  12.9 0.1 collective-permute-start.2
  13.0 1.3 %collective-permute-start.1 = (f32[80,128]{1,0:T(8,128)S(1)}, f32[80,128]{1,0:T(8,128)S(1)}, u32[]{:S(2)}, u32[]{:S(2)}) collective-permute-start(f32[80,128]{1,0:T(8,128)S(1)} %copy-done.3), channel_id=1, source_target_pairs={{32,96},{96,160},{160,224},{64,0},{128,64},{192,128},{33,97},{97,1... | collective-permute-start | bytes 122888 | tf_op jit(solution)/shard_map/ppermute | solution.py:340
  14.3 0.7 collective-permute-start
  15.0 4.6 %collective-permute-done.1.far = f32[80,128]{1,0:T(8,128)S(1)} collective-permute-done((f32[80,128]{1,0:T(8,128)S(1)}, f32[80,128]{1,0:T(8,128)S(1)}, u32[]{:S(2)}, u32[]{:S(2)}) %collective-permute-start.1) | collective-permute-done | bytes 40992 | tf_op jit(solution)/shard_map/ppermute | solution.py:340
  19.6 1.3 %collective-permute-done.2.other = f32[12,8,256]{2,1,0:T(8,128)S(1)} collective-permute-done((f32[12,8,256]{2,1,0:T(8,128)S(1)}, f32[12,8,256]{2,1,0:T(8,128)S(1)}, u32[]{:S(2)}, u32[]{:S(2)}) %collective-permute-start.2) | collective-permute-done | bytes 98336 | tf_op jit(solution)/shard_map/ppermute | solution.py:341
  20.9 3.2 %all-to-all-done = f32[32,40,128]{2,1,0:T(8,128)S(1)} async-done(((f32[32,40,128]{2,1,0:T(8,128)}), f32[32,40,128]{2,1,0:T(8,128)S(1)}, u32[]{:S(2)}, u32[]{:S(2)}) %all-to-all-start) | async-done | bytes 655392 | tf_op jit(solution)/shard_map/all_to_all | solution.py:343
  24.1 1.6 %shard_map.68 = f32[32,32,128]{2,1,0:T(8,128)} custom-call(f32[12,8,256]{2,1,0:T(8,128)S(1)} %bitcast.22, f32[12,8,256]{2,1,0:T(8,128)S(1)} %collective-permute-done.2.other, f32[80,128]{1,0:T(8,128)S(1)} %collective-permute-done.near, f32[80,128]{1,0:T(8,128)S(1)} %collective-permute-done.1.far), custom_call_target="tpu_custom_call" | custom-call | flops 1000000 | bytes 1000000 | tf_op jit(solution)/shard_map/pallas_call | solution.py:345
  25.7 4.7 %all-to-all-start.1 = ((f32[32,32,128]{2,1,0:T(8,128)}), f32[32,32,128]{2,1,0:T(8,128)S(1)}, u32[]{:S(2)}, u32[]{:S(2)}) async-start(f32[32,32,128]{2,1,0:T(8,128)} %shard_map.68), calls=%async_computation.1 | async-start | bytes 1048576 | tf_op jit(solution)/shard_map/all_to_all | solution.py:348
  30.4 0.1 shard_map.70
  30.5 3.5 %collective-permute-start.5 = (f32[56,128]{1,0:T(8,128)S(1)}, f32[56,128]{1,0:T(8,128)S(1)}, u32[]{:S(2)}, u32[]{:S(2)}) collective-permute-start(f32[56,128]{1,0:T(8,128)S(1)} %get-tuple-element.41), channel_id=1, source_target_pairs={{1,2},{3,4},{5,6},{7,8},{9,10},{11,12},{13,14},{15,16},{17,18},{19... | collective-permute-start | bytes 86024 | tf_op jit(solution)/shard_map/ppermute | solution.py:353
  34.0 0.1 collective-permute-start.4
  34.1 4.9 %collective-permute-done.5.near = f32[56,128]{1,0:T(8,128)S(1)} collective-permute-done((f32[56,128]{1,0:T(8,128)S(1)}, f32[56,128]{1,0:T(8,128)S(1)}, u32[]{:S(2)}, u32[]{:S(2)}) %collective-permute-start.5) | collective-permute-done | bytes 28704 | tf_op jit(solution)/shard_map/ppermute | solution.py:353
  39.0 2.9 %all-to-all-done.1 = f32[32,32,128]{2,1,0:T(8,128)S(1)} async-done(((f32[32,32,128]{2,1,0:T(8,128)}), f32[32,32,128]{2,1,0:T(8,128)S(1)}, u32[]{:S(2)}, u32[]{:S(2)}) %all-to-all-start.1) | async-done | bytes 524320 | tf_op jit(solution)/shard_map/all_to_all | solution.py:348
  41.9 0.9 %shard_map.69 = (f32[64,512]{1,0:T(8,128)S(1)}, bf16[256,512]{1,0:T(8,128)(2,1)S(1)}, bf16[256,512]{1,0:T(8,128)(2,1)S(1)}, bf16[576,256]{1,0:T(8,128)(2,1)S(1)}, bf16[576,256]{1,0:T(8,128)(2,1)S(1)}) custom-call(f32[1024,128]{1,0:T(8,128)S(1)} %bitcast.19, f32[1280,128]{1,0:T(8,128)S(1)} %bitcast.18), custom_call_target="tpu_custom_call" | custom-call | flops 5000000000 | bytes 5000000 | tf_op jit(solution)/shard_map/pallas_call | solution.py:356
  42.9 0.3 copy-done.2
  43.2 3.1 %shard_map.71 = (f32[1792,128]{1,0:T(8,128)}, f32[512,128]{1,0:T(8,128)S(1)}, f32[512,128]{1,0:T(8,128)S(1)}) custom-call(f32[64,512]{1,0:T(8,128)S(1)} %get-tuple-element.34.forward, bf16[256,512]{1,0:T(8,128)(2,1)S(1)} %get-tuple-element.35.x_high, bf16[256,512]{1,0:T(8,128)(2,1)S(1)} %get-tuple-element.36.x_low, ...), custom_call_target="tpu_custom_call" | custom-call | flops 1000000000 | bytes 5000000 | tf_op jit(solution)/shard_map/pallas_call | solution.py:364
  46.3 4.0 %all-to-all-start.2 = ((f32[32,56,128]{2,1,0:T(8,128)}), f32[32,56,128]{2,1,0:T(8,128)S(1)}, u32[]{:S(2)}, u32[]{:S(2)}) async-start(f32[32,56,128]{2,1,0:T(8,128)} %bitcast.7), calls=%async_computation.2 | async-start | bytes 1835008 | tf_op jit(solution)/shard_map/all_to_all | solution.py:376
  50.4 4.7 %collective-permute-start.7 = (f32[512,128]{1,0:T(8,128)S(1)}, f32[512,128]{1,0:T(8,128)S(1)}, u32[]{:S(2)}, u32[]{:S(2)}) collective-permute-start(f32[512,128]{1,0:T(8,128)S(1)} %get-tuple-element.43), channel_id=1, source_target_pairs={{0,32},{32,0},{64,96},{96,64},{128,160},{160,128},{192,224},{224,1... | collective-permute-start | bytes 786440 | tf_op jit(solution)/shard_map/ppermute | solution.py:375
  55.1 6.4 %collective-permute-done.7 = f32[512,128]{1,0:T(8,128)S(1)} collective-permute-done((f32[512,128]{1,0:T(8,128)S(1)}, f32[512,128]{1,0:T(8,128)S(1)}, u32[]{:S(2)}, u32[]{:S(2)}) %collective-permute-start.7) | collective-permute-done | bytes 262176 | tf_op jit(solution)/shard_map/ppermute | solution.py:375
  61.5 0.8 add.6
  62.2 4.0 %all-to-all-done.2.refs_0_ = f32[32,56,128]{2,1,0:T(8,128)S(1)} async-done(((f32[32,56,128]{2,1,0:T(8,128)}), f32[32,56,128]{2,1,0:T(8,128)S(1)}, u32[]{:S(2)}, u32[]{:S(2)}) %all-to-all-start.2) | async-done | bytes 917536 | tf_op jit(solution)/shard_map/all_to_all | solution.py:376
  66.3 4.2 %collective-permute-start.8 = (f32[112,128]{1,0:T(8,128)S(1)}, f32[112,128]{1,0:T(8,128)S(1)}, u32[]{:S(2)}, u32[]{:S(2)}) collective-permute-start(f32[112,128]{1,0:T(8,128)S(1)} %shard_map.72.own), channel_id=1, source_target_pairs={{0,64},{32,96},{64,0},{96,32},{128,192},{160,224},{192,128},{224,1... | collective-permute-start | bytes 172040 | tf_op jit(solution)/shard_map/ppermute | solution.py:383
  70.5 4.7 %all-to-all-start.3 = ((f32[32,16,128]{2,1,0:T(8,128)}), f32[32,16,128]{2,1,0:T(8,128)S(1)}, u32[]{:S(2)}, u32[]{:S(2)}) async-start(f32[32,16,128]{2,1,0:T(8,128)} %bitcast.8), calls=%async_computation.3 | async-start | bytes 524288 | tf_op jit(solution)/shard_map/all_to_all | solution.py:382
  75.2 4.1 %collective-permute-start.9 = (f32[112,128]{1,0:T(8,128)S(1)}, f32[112,128]{1,0:T(8,128)S(1)}, u32[]{:S(2)}, u32[]{:S(2)}) collective-permute-start(f32[112,128]{1,0:T(8,128)S(1)} %shard_map.74), channel_id=1, source_target_pairs={{0,192},{32,224},{64,128},{96,160},{128,64},{160,96},{192,0},{224,... | collective-permute-start | bytes 172040 | tf_op jit(solution)/shard_map/ppermute | solution.py:385
  79.3 2.5 %collective-permute-done.9 = f32[112,128]{1,0:T(8,128)S(1)} collective-permute-done((f32[112,128]{1,0:T(8,128)S(1)}, f32[112,128]{1,0:T(8,128)S(1)}, u32[]{:S(2)}, u32[]{:S(2)}) %collective-permute-start.9) | collective-permute-done | bytes 57376 | tf_op jit(solution)/shard_map/ppermute | solution.py:385
  81.8 3.6 %collective-permute-start.10 = (f32[112,128]{1,0:T(8,128)S(1)}, f32[112,128]{1,0:T(8,128)S(1)}, u32[]{:S(2)}, u32[]{:S(2)}) collective-permute-start(f32[112,128]{1,0:T(8,128)S(1)} %add.7.own), channel_id=1, source_target_pairs={{0,32},{32,0},{64,96},{96,64},{128,160},{160,128},{192,224},{224,1... | collective-permute-start | bytes 172040 | tf_op jit(solution)/shard_map/ppermute | solution.py:387
  85.4 1.0 %shard_map.73 = f32[12,8,256]{2,1,0:T(8,128)} custom-call(f32[32,16,128]{2,1,0:T(8,128)S(1)} %all-to-all-done.3.recv), custom_call_target="tpu_custom_call" | custom-call | flops 1000000 | bytes 1000000 | tf_op jit(solution)/shard_map/pallas_call | solution.py:388
  86.4 0.5 collective-permute-done.10.other
  86.9 0.7 shard_map.75
  (17 shorter events, 0.1 us)
Async XLA Ops:
  0.6 10.5 %copy-start = (f32[24,16,128]{2,1,0:T(8,128)S(1)}, f32[24,16,128]{2,1,0:T(8,128)}, u32[]{:S(2)}) copy-start(f32[24,16,128]{2,1,0:T(8,128)} %own.1) | copy-start | bytes 589828
  0.6 12.2 %copy-start.1 = (f32[8,12,256]{2,0,1:T(8,128)S(1)}, f32[8,12,256]{2,0,1:T(8,128)}, u32[]{:S(2)}) copy-start(f32[8,12,256]{2,0,1:T(8,128)} %param.4) | copy-start | bytes 294916
  2.5 10.5 %copy-start.3 = (f32[80,128]{1,0:T(8,128)S(1)}, f32[80,128]{1,0:T(8,128)}, u32[]{:S(2)}) copy-start(f32[80,128]{1,0:T(8,128)} %get-tuple-element.28) | copy-start | bytes 122884
  2.5 21.5 %all-to-all-start = ((f32[32,40,128]{2,1,0:T(8,128)}), f32[32,40,128]{2,1,0:T(8,128)S(1)}, u32[]{:S(2)}, u32[]{:S(2)}) async-start(f32[32,40,128]{2,1,0:T(8,128)} %get-tuple-element.29), calls=%async_computation | async-start | bytes 1310720 | tf_op jit(solution)/shard_map/all_to_all | solution.py:343
  11.2 9.7 %collective-permute-start.3 = (f32[24,16,128]{2,1,0:T(8,128)S(1)}, f32[24,16,128]{2,1,0:T(8,128)S(1)}, u32[]{:S(2)}, u32[]{:S(2)}) collective-permute-start(f32[24,16,128]{2,1,0:T(8,128)S(1)} %copy-done), channel_id=1, source_target_pairs={{0,32},{32,0},{64,96},{96,64},{128,160},{160,128},{192,224},{224,1... | collective-permute-start | bytes 589832 | tf_op jit(solution)/shard_map/ppermute | solution.py:342
  12.9 8.0 %collective-permute-start.2 = (f32[12,8,256]{2,1,0:T(8,128)S(1)}, f32[12,8,256]{2,1,0:T(8,128)S(1)}, u32[]{:S(2)}, u32[]{:S(2)}) collective-permute-start(f32[12,8,256]{2,1,0:T(8,128)S(1)} %bitcast.21), channel_id=1, source_target_pairs={{0,32},{32,0},{64,96},{96,64},{128,160},{160,128},{192,224},{224,1... | collective-permute-start | bytes 294920 | tf_op jit(solution)/shard_map/ppermute | solution.py:341
  13.0 6.6 %collective-permute-start.1 = (f32[80,128]{1,0:T(8,128)S(1)}, f32[80,128]{1,0:T(8,128)S(1)}, u32[]{:S(2)}, u32[]{:S(2)}) collective-permute-start(f32[80,128]{1,0:T(8,128)S(1)} %copy-done.3), channel_id=1, source_target_pairs={{32,96},{96,160},{160,224},{64,0},{128,64},{192,128},{33,97},{97,1... | collective-permute-start | bytes 122888 | tf_op jit(solution)/shard_map/ppermute | solution.py:340
  14.3 5.3 %collective-permute-start = (f32[80,128]{1,0:T(8,128)S(1)}, f32[80,128]{1,0:T(8,128)S(1)}, u32[]{:S(2)}, u32[]{:S(2)}) collective-permute-start(f32[80,128]{1,0:T(8,128)S(1)} %copy-done.3), channel_id=1, source_target_pairs={{32,64},{96,128},{160,192},{64,32},{128,96},{192,160},{33,65},{97,... | collective-permute-start | bytes 122888 | tf_op jit(solution)/shard_map/ppermute | solution.py:339
  25.7 16.3 %all-to-all-start.1 = ((f32[32,32,128]{2,1,0:T(8,128)}), f32[32,32,128]{2,1,0:T(8,128)S(1)}, u32[]{:S(2)}, u32[]{:S(2)}) async-start(f32[32,32,128]{2,1,0:T(8,128)} %shard_map.68), calls=%async_computation.1 | async-start | bytes 1048576 | tf_op jit(solution)/shard_map/all_to_all | solution.py:348
  30.5 8.6 %collective-permute-start.5 = (f32[56,128]{1,0:T(8,128)S(1)}, f32[56,128]{1,0:T(8,128)S(1)}, u32[]{:S(2)}, u32[]{:S(2)}) collective-permute-start(f32[56,128]{1,0:T(8,128)S(1)} %get-tuple-element.41), channel_id=1, source_target_pairs={{1,2},{3,4},{5,6},{7,8},{9,10},{11,12},{13,14},{15,16},{17,18},{19... | collective-permute-start | bytes 86024 | tf_op jit(solution)/shard_map/ppermute | solution.py:353
  34.0 8.9 %collective-permute-start.4 = (f32[54,16,128]{2,1,0:T(8,128)S(1)}, f32[54,16,128]{2,1,0:T(8,128)S(1)}, u32[]{:S(2)}, u32[]{:S(2)}) collective-permute-start(f32[54,16,128]{2,1,0:T(8,128)S(1)} %get-tuple-element.40.own), channel_id=1, source_target_pairs={{0,1},{1,0},{2,3},{3,2},{4,5},{5,4},{6,7},{7,6},{8,9},{9,8},{10,11... | collective-permute-start | bytes 1327112 | tf_op jit(solution)/shard_map/ppermute | solution.py:354
  39.0 3.8 %collective-permute-start.6 = (f32[56,128]{1,0:T(8,128)S(1)}, f32[56,128]{1,0:T(8,128)S(1)}, u32[]{:S(2)}, u32[]{:S(2)}) collective-permute-start(f32[56,128]{1,0:T(8,128)S(1)} %collective-permute-done.5.near), channel_id=1, source_target_pairs={{0,1},{1,0},{2,3},{3,2},{4,5},{5,4},{6,7},{7,6},{8,9},{9,8},{10,11... | collective-permute-start | bytes 86024 | tf_op jit(solution)/shard_map/ppermute | solution.py:355
  41.9 1.3 %copy-start.2 = (f32[256,3,3,128]{3,0,2,1:T(8,128)S(1)}, f32[256,3,3,128]{3,0,2,1:T(8,128)}, u32[]{:S(2)}) copy-start(f32[256,3,3,128]{3,0,2,1:T(8,128)} %param.6) | copy-start | bytes 3538948
  46.3 19.9 %all-to-all-start.2 = ((f32[32,56,128]{2,1,0:T(8,128)}), f32[32,56,128]{2,1,0:T(8,128)S(1)}, u32[]{:S(2)}, u32[]{:S(2)}) async-start(f32[32,56,128]{2,1,0:T(8,128)} %bitcast.7), calls=%async_computation.2 | async-start | bytes 1835008 | tf_op jit(solution)/shard_map/all_to_all | solution.py:376
  50.4 11.1 %collective-permute-start.7 = (f32[512,128]{1,0:T(8,128)S(1)}, f32[512,128]{1,0:T(8,128)S(1)}, u32[]{:S(2)}, u32[]{:S(2)}) collective-permute-start(f32[512,128]{1,0:T(8,128)S(1)} %get-tuple-element.43), channel_id=1, source_target_pairs={{0,32},{32,0},{64,96},{96,64},{128,160},{160,128},{192,224},{224,1... | collective-permute-start | bytes 786440 | tf_op jit(solution)/shard_map/ppermute | solution.py:375
  66.3 8.9 %collective-permute-start.8 = (f32[112,128]{1,0:T(8,128)S(1)}, f32[112,128]{1,0:T(8,128)S(1)}, u32[]{:S(2)}, u32[]{:S(2)}) collective-permute-start(f32[112,128]{1,0:T(8,128)S(1)} %shard_map.72.own), channel_id=1, source_target_pairs={{0,64},{32,96},{64,0},{96,32},{128,192},{160,224},{192,128},{224,1... | collective-permute-start | bytes 172040 | tf_op jit(solution)/shard_map/ppermute | solution.py:383
  70.5 14.9 %all-to-all-start.3 = ((f32[32,16,128]{2,1,0:T(8,128)}), f32[32,16,128]{2,1,0:T(8,128)S(1)}, u32[]{:S(2)}, u32[]{:S(2)}) async-start(f32[32,16,128]{2,1,0:T(8,128)} %bitcast.8), calls=%async_computation.3 | async-start | bytes 524288 | tf_op jit(solution)/shard_map/all_to_all | solution.py:382
  75.2 6.6 %collective-permute-start.9 = (f32[112,128]{1,0:T(8,128)S(1)}, f32[112,128]{1,0:T(8,128)S(1)}, u32[]{:S(2)}, u32[]{:S(2)}) collective-permute-start(f32[112,128]{1,0:T(8,128)S(1)} %shard_map.74), channel_id=1, source_target_pairs={{0,192},{32,224},{64,128},{96,160},{128,64},{160,96},{192,0},{224,... | collective-permute-start | bytes 172040 | tf_op jit(solution)/shard_map/ppermute | solution.py:385
  81.8 5.2 %collective-permute-start.10 = (f32[112,128]{1,0:T(8,128)S(1)}, f32[112,128]{1,0:T(8,128)S(1)}, u32[]{:S(2)}, u32[]{:S(2)}) collective-permute-start(f32[112,128]{1,0:T(8,128)S(1)} %add.7.own), channel_id=1, source_target_pairs={{0,32},{32,0},{64,96},{96,64},{128,160},{160,128},{192,224},{224,1... | collective-permute-start | bytes 172040 | tf_op jit(solution)/shard_map/ppermute | solution.py:387

commit v8 on v7

--- a/solution.py
+++ b/solution.py
@@ -186,13 +186,21 @@
     result[...] = hidden
 
 
+def stack(values, offset, g_high, g_low):
+    for t in range(9):
+        shift = ((t // 3) * STEP + t % 3 + offset) % FLAT
+        high, low = halves(pltpu.roll(values, shift, 1) if shift else values)
+        g_high[t * 64 : t * 64 + 64, :] = high
+        g_low[t * 64 : t * 64 + 64, :] = low
+    return g_high[...], g_low[...]
+
+
 def main_kernel(
-    forward, x_high, x_low, w_high, w_low, own, other, near, far, weight, out, mine, theirs,
+    forward, x_high, x_low, own, other, near, far, weight, out, gradient_out,
     cells, sums, g_high, g_low,
 ):
     parts, grad = windows(own, other, near, far, weight, sums, cells)
     hidden = forward[...]
-    weights = (w_high[...], w_low[...])
     image = (x_high[...], x_low[...])
     at = lax.broadcasted_iota(jnp.int32, (64, FLAT), 1)
     block = lax.axis_index("rows") // 2
@@ -206,15 +214,7 @@
     slope = sigma * (1.0 + hidden * (1.0 - sigma))
     gradient = grad * slope
 
-    def stack(values, offset):
-        for t in range(9):
-            shift = ((t // 3) * STEP + t % 3 + offset) % FLAT
-            high, low = halves(pltpu.roll(values, shift, 1) if shift else values)
-            g_high[t * 64 : t * 64 + 64, :] = high
-            g_low[t * 64 : t * 64 + 64, :] = low
-        return g_high[...], g_low[...]
-
-    moved = stack(jnp.where(inside, gradient, 0.0), 0)
+    moved = stack(jnp.where(inside, gradient, 0.0), 0, g_high, g_low)
     into = product(moved, image, NT)
     for t in range(9):
         for h in range(2):
@@ -231,7 +231,15 @@
             out[pl.ds(36 + t * 2 + j, 32, stride=BACK), :] = onto[
                 at + j * 32 : at + j * 32 + 32, kind * 128 : kind * 128 + 128
             ]
-    back = product(weights, stack(jnp.where(around, gradient, 0.0), -2 * STEP), TN)
+    gradient_out[...] = jnp.where(around, gradient, 0.0)
+    blank = jnp.zeros((2, 128), F32)
+    for d in range(32):
+        out[pl.ds(d * BACK + 54, 2), :] = blank
+
+
+def back_kernel(gradient, w_high, w_low, mine, theirs, g_high, g_low):
+    weights = (w_high[...], w_low[...])
+    back = product(weights, stack(gradient[...], -2 * STEP, g_high, g_low), TN)
     half = ROWS // 2 * STEP
     first = lax.axis_index("rows") % 2 == 0
     upper, lower = back[:, 0:256], pltpu.roll(back, FLAT - half, 1)[:, 0:256]
@@ -242,9 +250,6 @@
         for d in range(32):
             for q in range(2):
                 dst[pl.ds(d * 16 + q * 8, 8), :] = part[d * 8 : d * 8 + 8, q * 128 : q * 128 + 128]
-    blank = jnp.zeros((2, 128), F32)
-    for d in range(32):
-        out[pl.ds(d * BACK + 54, 2), :] = blank
 
 
 def weights_kernel(scale, recv, mixed, total):
@@ -361,16 +366,17 @@
         ),
         2, (), 5 * 10**9, 5 * 10**6,
     )(recv.reshape(1024, 128), kernels.reshape(32 * PACK, 128))
-    sent, own, given = call(
-        main_kernel, (shape(32 * BACK, 128), shape(512, 128), shape(512, 128)), 10,
-        [
-            pltpu.VMEM((FINE, 48, 128), F32), pltpu.VMEM((FLAT, 512), F32),
-            pltpu.VMEM((576, FLAT), BF16), pltpu.VMEM((576, FLAT), BF16),
-        ],
-        10**9, 5 * 10**6,
+    hidden, x_high, x_low, w_high, w_low = forward
+    stacks = [pltpu.VMEM((576, FLAT), BF16), pltpu.VMEM((576, FLAT), BF16)]
+    sent, gradient = call(
+        main_kernel, (shape(32 * BACK, 128), shape(64, FLAT)), 8,
+        [pltpu.VMEM((FINE, 48, 128), F32), pltpu.VMEM((FLAT, 512), F32)] + stacks, 10**9, 5 * 10**6,
     )(
-        *forward, tall, other_tall, near_side, far_side,
+        hidden, x_high, x_low, tall, other_tall, near_side, far_side,
         jnp.transpose(weight_out, (1, 2, 0, 3)).reshape(2304, 128),
+    )
+    own, given = call(back_kernel, (shape(512, 128), shape(512, 128)), 3, stacks, 5 * 10**9, 3 * 10**6)(
+        gradient, w_high, w_low
     )
     given = lax.ppermute(given, "rows", partner(8))
     back = lax.all_to_all(sent.reshape(32, BACK, 128), "chan", 0, 0, tiled=True)

time: 89.1 us -> 89.1 us (level)
  Pallas kernels: 9.38 us -> 10.6 us
  waiting for transfers between devices: 30.3 us -> 29.3 us
    all_to_all x1, waiting for transfers between devices: 4 us -> 2.81 us  [local(): back = lax.all_to_all(sent.reshape(32, BACK, 128), 'chan', 0, 0, tiled=True)]
    pallas_call x1 -> x2, Pallas kernels: 3.13 us -> 4.32 us  [the longest x1 3.14 us: local(): call(main_kernel, (shape(32 * BACK, 128), shape(64, FLAT)), 8, [pltpu.VME...]
    all_to_all x1, starting transfers between devices: 4.71 us -> 5.89 us  [local(): image = lax.all_to_all(moved.reshape(32, 16, 128), 'chan', 0, 0, tiled=True)]
    ppermute x1, starting transfers between devices: 4.08 us -> 2.91 us  [local(): opposite = lax.ppermute(mixed, 'rows', mirrored(8))]
  transfers between devices with their start and end apart: 15 -> 15, of which waited for: 9 -> 9; matrix products, arithmetic and copies ran while one was open for 1% -> 1% of each run, Pallas kernels for 2% -> 4%
where the time goes in v8:
time: 89.1 us; the launch traced here: 87.6 us
  starting transfers between devices  45.9 us (52%)
  waiting for transfers between devices  29.3 us (33%)
  Pallas kernels  10.6 us (12%)
    all_to_all x1, starting transfers between devices, local(): kernels = lax.all_to_all(packed, 'chan', 0, 0, tiled=True)  8.6 us
    ppermute x1, waiting for transfers between devices, local(): given = lax.ppermute(given, 'rows', partner(8))  6.41 us
    all_to_all x1, starting transfers between devices, local(): image = lax.all_to_all(moved.reshape(32, 16, 128), 'chan', 0, 0, tiled=True)  5.89 us
    ppermute x1, waiting for transfers between devices, local(): near_side = lax.ppermute(side, 'chan', beside(32))  4.92 us
    ppermute x1, starting transfers between devices, local(): given = lax.ppermute(given, 'rows', partner(8))  4.72 us
    all_to_all x1, starting transfers between devices, local(): recv = lax.all_to_all(packed, 'chan', 0, 0, tiled=True)  4.69 us
    ppermute x1, waiting for transfers between devices, local(): far = lax.ppermute(edge, 'rows', inward(8))  4.61 us
    ppermute x1, starting transfers between devices, local(): opposite = lax.ppermute(mixed, 'rows', partner(8, 2))  4.16 us
  transfers between devices with their start and end apart: 15, of which 9 were waited for; matrix products, arithmetic and copies ran while one was open for 1% of the time, Pallas kernels for 4%

profile of v8, /device:TPU:1, one launch (start us, length us, event | category | flops | bytes accessed | tf_op | source)
XLA Modules:
  0.0 87.6 jit_solution(5794784737856159865)
XLA Ops:
  0.7 1.9 %shard_map.67 = (f32[80,128]{1,0:T(8,128)}, f32[32,40,128]{2,1,0:T(8,128)}) custom-call(f32[12,8,256]{2,1,0:T(8,128)} %bitcast.20, f32[24,16,128]{2,1,0:T(8,128)} %own.1, f32[9,8,256]{2,1,0:T(8,128)} %bitcast.25), custom_call_target="tpu_custom_call" | custom-call | flops 1000000 | bytes 1000000 | tf_op jit(solution)/shard_map/pallas_call | solution.py:335
  2.5 8.6 %all-to-all-start = ((f32[32,40,128]{2,1,0:T(8,128)}), f32[32,40,128]{2,1,0:T(8,128)S(1)}, u32[]{:S(2)}, u32[]{:S(2)}) async-start(f32[32,40,128]{2,1,0:T(8,128)} %get-tuple-element.30), calls=%async_computation | async-start | bytes 1310720 | tf_op jit(solution)/shard_map/all_to_all | solution.py:348
  11.2 1.7 %collective-permute-start.3 = (f32[24,16,128]{2,1,0:T(8,128)S(1)}, f32[24,16,128]{2,1,0:T(8,128)S(1)}, u32[]{:S(2)}, u32[]{:S(2)}) collective-permute-start(f32[24,16,128]{2,1,0:T(8,128)S(1)} %copy-done), channel_id=1, source_target_pairs={{0,32},{32,0},{64,96},{96,64},{128,160},{160,128},{192,224},{224,1... | collective-permute-start | bytes 589832 | tf_op jit(solution)/shard_map/ppermute | solution.py:347
  12.9 0.1 collective-permute-start.2
  13.0 1.3 %collective-permute-start.1 = (f32[80,128]{1,0:T(8,128)S(1)}, f32[80,128]{1,0:T(8,128)S(1)}, u32[]{:S(2)}, u32[]{:S(2)}) collective-permute-start(f32[80,128]{1,0:T(8,128)S(1)} %copy-done.3), channel_id=1, source_target_pairs={{32,96},{96,160},{160,224},{64,0},{128,64},{192,128},{33,97},{97,1... | collective-permute-start | bytes 122888 | tf_op jit(solution)/shard_map/ppermute | solution.py:345
  14.3 0.7 collective-permute-start
  15.0 4.6 %collective-permute-done.1.far = f32[80,128]{1,0:T(8,128)S(1)} collective-permute-done((f32[80,128]{1,0:T(8,128)S(1)}, f32[80,128]{1,0:T(8,128)S(1)}, u32[]{:S(2)}, u32[]{:S(2)}) %collective-permute-start.1) | collective-permute-done | bytes 40992 | tf_op jit(solution)/shard_map/ppermute | solution.py:345
  19.6 1.3 %collective-permute-done.2.other = f32[12,8,256]{2,1,0:T(8,128)S(1)} collective-permute-done((f32[12,8,256]{2,1,0:T(8,128)S(1)}, f32[12,8,256]{2,1,0:T(8,128)S(1)}, u32[]{:S(2)}, u32[]{:S(2)}) %collective-permute-start.2) | collective-permute-done | bytes 98336 | tf_op jit(solution)/shard_map/ppermute | solution.py:346
  20.9 3.2 %all-to-all-done = f32[32,40,128]{2,1,0:T(8,128)S(1)} async-done(((f32[32,40,128]{2,1,0:T(8,128)}), f32[32,40,128]{2,1,0:T(8,128)S(1)}, u32[]{:S(2)}, u32[]{:S(2)}) %all-to-all-start) | async-done | bytes 655392 | tf_op jit(solution)/shard_map/all_to_all | solution.py:348
  24.1 1.6 %shard_map.68 = f32[32,32,128]{2,1,0:T(8,128)} custom-call(f32[12,8,256]{2,1,0:T(8,128)S(1)} %bitcast.22, f32[12,8,256]{2,1,0:T(8,128)S(1)} %collective-permute-done.2.other, f32[80,128]{1,0:T(8,128)S(1)} %collective-permute-done.near, f32[80,128]{1,0:T(8,128)S(1)} %collective-permute-done.1.far), custom_call_target="tpu_custom_call" | custom-call | flops 1000000 | bytes 1000000 | tf_op jit(solution)/shard_map/pallas_call | solution.py:350
  25.7 4.7 %all-to-all-start.1 = ((f32[32,32,128]{2,1,0:T(8,128)}), f32[32,32,128]{2,1,0:T(8,128)S(1)}, u32[]{:S(2)}, u32[]{:S(2)}) async-start(f32[32,32,128]{2,1,0:T(8,128)} %shard_map.68), calls=%async_computation.1 | async-start | bytes 1048576 | tf_op jit(solution)/shard_map/all_to_all | solution.py:353
  30.5 3.5 %collective-permute-start.5 = (f32[56,128]{1,0:T(8,128)S(1)}, f32[56,128]{1,0:T(8,128)S(1)}, u32[]{:S(2)}, u32[]{:S(2)}) collective-permute-start(f32[56,128]{1,0:T(8,128)S(1)} %get-tuple-element.40), channel_id=1, source_target_pairs={{1,2},{3,4},{5,6},{7,8},{9,10},{11,12},{13,14},{15,16},{17,18},{19... | collective-permute-start | bytes 86024 | tf_op jit(solution)/shard_map/ppermute | solution.py:358
  34.0 0.1 collective-permute-start.4
  34.1 4.9 %collective-permute-done.5.near = f32[56,128]{1,0:T(8,128)S(1)} collective-permute-done((f32[56,128]{1,0:T(8,128)S(1)}, f32[56,128]{1,0:T(8,128)S(1)}, u32[]{:S(2)}, u32[]{:S(2)}) %collective-permute-start.5) | collective-permute-done | bytes 28704 | tf_op jit(solution)/shard_map/ppermute | solution.py:358
  39.0 2.9 %all-to-all-done.1 = f32[32,32,128]{2,1,0:T(8,128)S(1)} async-done(((f32[32,32,128]{2,1,0:T(8,128)}), f32[32,32,128]{2,1,0:T(8,128)S(1)}, u32[]{:S(2)}, u32[]{:S(2)}) %all-to-all-start.1) | async-done | bytes 524320 | tf_op jit(solution)/shard_map/all_to_all | solution.py:353
  41.9 0.9 %shard_map.69 = (f32[64,512]{1,0:T(8,128)S(1)}, bf16[256,512]{1,0:T(8,128)(2,1)S(1)}, bf16[256,512]{1,0:T(8,128)(2,1)S(1)}, bf16[576,256]{1,0:T(8,128)(2,1)S(1)}, bf16[576,256]{1,0:T(8,128)(2,1)S(1)}) custom-call(f32[1024,128]{1,0:T(8,128)S(1)} %bitcast.19, f32[1280,128]{1,0:T(8,128)S(1)} %bitcast.18), custom_call_target="tpu_custom_call" | custom-call | flops 5000000000 | bytes 5000000 | tf_op jit(solution)/shard_map/pallas_call | solution.py:361
  42.9 0.3 copy-done.2
  43.2 3.1 %shard_map.71 = (f32[1792,128]{1,0:T(8,128)}, f32[64,512]{1,0:T(8,128)S(1)}) custom-call(f32[64,512]{1,0:T(8,128)S(1)} %get-tuple-element.35.forward, bf16[256,512]{1,0:T(8,128)(2,1)S(1)} %get-tuple-element.36.x_high, bf16[256,512]{1,0:T(8,128)(2,1)S(1)} %get-tuple-element.37.x_low, f32[54,16,128]{2,1,0:T(8,128)S(1)} %get-tuple-element.39.own, ...), custom_call_target="tpu_custom_call" | custom-call | flops 1000000000 | bytes 5000000 | tf_op jit(solution)/shard_map/pallas_call | solution.py:371
  46.3 4.0 %all-to-all-start.2 = ((f32[32,56,128]{2,1,0:T(8,128)}), f32[32,56,128]{2,1,0:T(8,128)S(1)}, u32[]{:S(2)}, u32[]{:S(2)}) async-start(f32[32,56,128]{2,1,0:T(8,128)} %bitcast.7), calls=%async_computation.2 | async-start | bytes 1835008 | tf_op jit(solution)/shard_map/all_to_all | solution.py:382
  50.4 1.2 %shard_map.72 = (f32[512,128]{1,0:T(8,128)S(1)}, f32[512,128]{1,0:T(8,128)S(1)}) custom-call(f32[64,512]{1,0:T(8,128)S(1)} %get-tuple-element.41.gradient, bf16[576,256]{1,0:T(8,128)(2,1)S(1)} %get-tuple-element.42.w_high, bf16[576,256]{1,0:T(8,128)(2,1)S(1)} %get-tuple-element.43.w_low), custom_call_target="tpu_custom_call" | custom-call | flops 5000000000 | bytes 3000000 | tf_op jit(solution)/shard_map/pallas_call | solution.py:378
  51.5 4.7 %collective-permute-start.7 = (f32[512,128]{1,0:T(8,128)S(1)}, f32[512,128]{1,0:T(8,128)S(1)}, u32[]{:S(2)}, u32[]{:S(2)}) collective-permute-start(f32[512,128]{1,0:T(8,128)S(1)} %get-tuple-element.45), channel_id=1, source_target_pairs={{0,32},{32,0},{64,96},{96,64},{128,160},{160,128},{192,224},{224,1... | collective-permute-start | bytes 786440 | tf_op jit(solution)/shard_map/ppermute | solution.py:381
  56.3 6.4 %collective-permute-done.7 = f32[512,128]{1,0:T(8,128)S(1)} collective-permute-done((f32[512,128]{1,0:T(8,128)S(1)}, f32[512,128]{1,0:T(8,128)S(1)}, u32[]{:S(2)}, u32[]{:S(2)}) %collective-permute-start.7) | collective-permute-done | bytes 262176 | tf_op jit(solution)/shard_map/ppermute | solution.py:381
  62.7 0.7 add.6
  63.4 2.8 %all-to-all-done.2.refs_0_ = f32[32,56,128]{2,1,0:T(8,128)S(1)} async-done(((f32[32,56,128]{2,1,0:T(8,128)}), f32[32,56,128]{2,1,0:T(8,128)S(1)}, u32[]{:S(2)}, u32[]{:S(2)}) %all-to-all-start.2) | async-done | bytes 917536 | tf_op jit(solution)/shard_map/all_to_all | solution.py:382
  66.3 4.2 %collective-permute-start.8 = (f32[112,128]{1,0:T(8,128)S(1)}, f32[112,128]{1,0:T(8,128)S(1)}, u32[]{:S(2)}, u32[]{:S(2)}) collective-permute-start(f32[112,128]{1,0:T(8,128)S(1)} %shard_map.73.own), channel_id=1, source_target_pairs={{0,64},{32,96},{64,0},{96,32},{128,192},{160,224},{192,128},{224,1... | collective-permute-start | bytes 172040 | tf_op jit(solution)/shard_map/ppermute | solution.py:389
  70.5 5.9 %all-to-all-start.3 = ((f32[32,16,128]{2,1,0:T(8,128)}), f32[32,16,128]{2,1,0:T(8,128)S(1)}, u32[]{:S(2)}, u32[]{:S(2)}) async-start(f32[32,16,128]{2,1,0:T(8,128)} %bitcast.8), calls=%async_computation.3 | async-start | bytes 524288 | tf_op jit(solution)/shard_map/all_to_all | solution.py:388
  76.4 2.9 %collective-permute-start.9 = (f32[112,128]{1,0:T(8,128)S(1)}, f32[112,128]{1,0:T(8,128)S(1)}, u32[]{:S(2)}, u32[]{:S(2)}) collective-permute-start(f32[112,128]{1,0:T(8,128)S(1)} %shard_map.75), channel_id=1, source_target_pairs={{0,192},{32,224},{64,128},{96,160},{128,64},{160,96},{192,0},{224,... | collective-permute-start | bytes 172040 | tf_op jit(solution)/shard_map/ppermute | solution.py:391
  79.3 2.6 %collective-permute-done.9 = f32[112,128]{1,0:T(8,128)S(1)} collective-permute-done((f32[112,128]{1,0:T(8,128)S(1)}, f32[112,128]{1,0:T(8,128)S(1)}, u32[]{:S(2)}, u32[]{:S(2)}) %collective-permute-start.9) | collective-permute-done | bytes 57376 | tf_op jit(solution)/shard_map/ppermute | solution.py:391
  81.9 3.5 %collective-permute-start.10 = (f32[112,128]{1,0:T(8,128)S(1)}, f32[112,128]{1,0:T(8,128)S(1)}, u32[]{:S(2)}, u32[]{:S(2)}) collective-permute-start(f32[112,128]{1,0:T(8,128)S(1)} %add.7.own), channel_id=1, source_target_pairs={{0,32},{32,0},{64,96},{96,64},{128,160},{160,128},{192,224},{224,1... | collective-permute-start | bytes 172040 | tf_op jit(solution)/shard_map/ppermute | solution.py:393
  85.4 1.0 %shard_map.74 = f32[12,8,256]{2,1,0:T(8,128)} custom-call(f32[32,16,128]{2,1,0:T(8,128)S(1)} %all-to-all-done.3.recv), custom_call_target="tpu_custom_call" | custom-call | flops 1000000 | bytes 1000000 | tf_op jit(solution)/shard_map/pallas_call | solution.py:394
  86.4 0.5 collective-permute-done.10.other
  86.9 0.7 shard_map.76
  (18 shorter events, 0.2 us)
Async XLA Ops:
  0.6 10.5 %copy-start = (f32[24,16,128]{2,1,0:T(8,128)S(1)}, f32[24,16,128]{2,1,0:T(8,128)}, u32[]{:S(2)}) copy-start(f32[24,16,128]{2,1,0:T(8,128)} %own.1) | copy-start | bytes 589828
  0.6 12.2 %copy-start.1 = (f32[8,12,256]{2,0,1:T(8,128)S(1)}, f32[8,12,256]{2,0,1:T(8,128)}, u32[]{:S(2)}) copy-start(f32[8,12,256]{2,0,1:T(8,128)} %param.4) | copy-start | bytes 294916
  2.5 10.5 %copy-start.3 = (f32[80,128]{1,0:T(8,128)S(1)}, f32[80,128]{1,0:T(8,128)}, u32[]{:S(2)}) copy-start(f32[80,128]{1,0:T(8,128)} %get-tuple-element.29) | copy-start | bytes 122884
  2.5 21.5 %all-to-all-start = ((f32[32,40,128]{2,1,0:T(8,128)}), f32[32,40,128]{2,1,0:T(8,128)S(1)}, u32[]{:S(2)}, u32[]{:S(2)}) async-start(f32[32,40,128]{2,1,0:T(8,128)} %get-tuple-element.30), calls=%async_computation | async-start | bytes 1310720 | tf_op jit(solution)/shard_map/all_to_all | solution.py:348
  11.2 9.7 %collective-permute-start.3 = (f32[24,16,128]{2,1,0:T(8,128)S(1)}, f32[24,16,128]{2,1,0:T(8,128)S(1)}, u32[]{:S(2)}, u32[]{:S(2)}) collective-permute-start(f32[24,16,128]{2,1,0:T(8,128)S(1)} %copy-done), channel_id=1, source_target_pairs={{0,32},{32,0},{64,96},{96,64},{128,160},{160,128},{192,224},{224,1... | collective-permute-start | bytes 589832 | tf_op jit(solution)/shard_map/ppermute | solution.py:347
  12.9 8.0 %collective-permute-start.2 = (f32[12,8,256]{2,1,0:T(8,128)S(1)}, f32[12,8,256]{2,1,0:T(8,128)S(1)}, u32[]{:S(2)}, u32[]{:S(2)}) collective-permute-start(f32[12,8,256]{2,1,0:T(8,128)S(1)} %bitcast.21), channel_id=1, source_target_pairs={{0,32},{32,0},{64,96},{96,64},{128,160},{160,128},{192,224},{224,1... | collective-permute-start | bytes 294920 | tf_op jit(solution)/shard_map/ppermute | solution.py:346
  13.0 6.6 %collective-permute-start.1 = (f32[80,128]{1,0:T(8,128)S(1)}, f32[80,128]{1,0:T(8,128)S(1)}, u32[]{:S(2)}, u32[]{:S(2)}) collective-permute-start(f32[80,128]{1,0:T(8,128)S(1)} %copy-done.3), channel_id=1, source_target_pairs={{32,96},{96,160},{160,224},{64,0},{128,64},{192,128},{33,97},{97,1... | collective-permute-start | bytes 122888 | tf_op jit(solution)/shard_map/ppermute | solution.py:345
  14.3 5.3 %collective-permute-start = (f32[80,128]{1,0:T(8,128)S(1)}, f32[80,128]{1,0:T(8,128)S(1)}, u32[]{:S(2)}, u32[]{:S(2)}) collective-permute-start(f32[80,128]{1,0:T(8,128)S(1)} %copy-done.3), channel_id=1, source_target_pairs={{32,64},{96,128},{160,192},{64,32},{128,96},{192,160},{33,65},{97,... | collective-permute-start | bytes 122888 | tf_op jit(solution)/shard_map/ppermute | solution.py:344
  25.7 16.3 %all-to-all-start.1 = ((f32[32,32,128]{2,1,0:T(8,128)}), f32[32,32,128]{2,1,0:T(8,128)S(1)}, u32[]{:S(2)}, u32[]{:S(2)}) async-start(f32[32,32,128]{2,1,0:T(8,128)} %shard_map.68), calls=%async_computation.1 | async-start | bytes 1048576 | tf_op jit(solution)/shard_map/all_to_all | solution.py:353
  30.5 8.6 %collective-permute-start.5 = (f32[56,128]{1,0:T(8,128)S(1)}, f32[56,128]{1,0:T(8,128)S(1)}, u32[]{:S(2)}, u32[]{:S(2)}) collective-permute-start(f32[56,128]{1,0:T(8,128)S(1)} %get-tuple-element.40), channel_id=1, source_target_pairs={{1,2},{3,4},{5,6},{7,8},{9,10},{11,12},{13,14},{15,16},{17,18},{19... | collective-permute-start | bytes 86024 | tf_op jit(solution)/shard_map/ppermute | solution.py:358
  34.0 8.9 %collective-permute-start.4 = (f32[54,16,128]{2,1,0:T(8,128)S(1)}, f32[54,16,128]{2,1,0:T(8,128)S(1)}, u32[]{:S(2)}, u32[]{:S(2)}) collective-permute-start(f32[54,16,128]{2,1,0:T(8,128)S(1)} %get-tuple-element.39.own), channel_id=1, source_target_pairs={{0,1},{1,0},{2,3},{3,2},{4,5},{5,4},{6,7},{7,6},{8,9},{9,8},{10,11... | collective-permute-start | bytes 1327112 | tf_op jit(solution)/shard_map/ppermute | solution.py:359
  39.0 3.8 %collective-permute-start.6 = (f32[56,128]{1,0:T(8,128)S(1)}, f32[56,128]{1,0:T(8,128)S(1)}, u32[]{:S(2)}, u32[]{:S(2)}) collective-permute-start(f32[56,128]{1,0:T(8,128)S(1)} %collective-permute-done.5.near), channel_id=1, source_target_pairs={{0,1},{1,0},{2,3},{3,2},{4,5},{5,4},{6,7},{7,6},{8,9},{9,8},{10,11... | collective-permute-start | bytes 86024 | tf_op jit(solution)/shard_map/ppermute | solution.py:360
  41.9 1.3 %copy-start.2 = (f32[256,3,3,128]{3,0,2,1:T(8,128)S(1)}, f32[256,3,3,128]{3,0,2,1:T(8,128)}, u32[]{:S(2)}) copy-start(f32[256,3,3,128]{3,0,2,1:T(8,128)} %param.6) | copy-start | bytes 3538948
  46.3 19.9 %all-to-all-start.2 = ((f32[32,56,128]{2,1,0:T(8,128)}), f32[32,56,128]{2,1,0:T(8,128)S(1)}, u32[]{:S(2)}, u32[]{:S(2)}) async-start(f32[32,56,128]{2,1,0:T(8,128)} %bitcast.7), calls=%async_computation.2 | async-start | bytes 1835008 | tf_op jit(solution)/shard_map/all_to_all | solution.py:382
  51.5 11.1 %collective-permute-start.7 = (f32[512,128]{1,0:T(8,128)S(1)}, f32[512,128]{1,0:T(8,128)S(1)}, u32[]{:S(2)}, u32[]{:S(2)}) collective-permute-start(f32[512,128]{1,0:T(8,128)S(1)} %get-tuple-element.45), channel_id=1, source_target_pairs={{0,32},{32,0},{64,96},{96,64},{128,160},{160,128},{192,224},{224,1... | collective-permute-start | bytes 786440 | tf_op jit(solution)/shard_map/ppermute | solution.py:381
  66.3 10.1 %collective-permute-start.8 = (f32[112,128]{1,0:T(8,128)S(1)}, f32[112,128]{1,0:T(8,128)S(1)}, u32[]{:S(2)}, u32[]{:S(2)}) collective-permute-start(f32[112,128]{1,0:T(8,128)S(1)} %shard_map.73.own), channel_id=1, source_target_pairs={{0,64},{32,96},{64,0},{96,32},{128,192},{160,224},{192,128},{224,1... | collective-permute-start | bytes 172040 | tf_op jit(solution)/shard_map/ppermute | solution.py:389
  70.5 14.9 %all-to-all-start.3 = ((f32[32,16,128]{2,1,0:T(8,128)}), f32[32,16,128]{2,1,0:T(8,128)S(1)}, u32[]{:S(2)}, u32[]{:S(2)}) async-start(f32[32,16,128]{2,1,0:T(8,128)} %bitcast.8), calls=%async_computation.3 | async-start | bytes 524288 | tf_op jit(solution)/shard_map/all_to_all | solution.py:388
  76.4 5.5 %collective-permute-start.9 = (f32[112,128]{1,0:T(8,128)S(1)}, f32[112,128]{1,0:T(8,128)S(1)}, u32[]{:S(2)}, u32[]{:S(2)}) collective-permute-start(f32[112,128]{1,0:T(8,128)S(1)} %shard_map.75), channel_id=1, source_target_pairs={{0,192},{32,224},{64,128},{96,160},{128,64},{160,96},{192,0},{224,... | collective-permute-start | bytes 172040 | tf_op jit(solution)/shard_map/ppermute | solution.py:391
  81.9 5.0 %collective-permute-start.10 = (f32[112,128]{1,0:T(8,128)S(1)}, f32[112,128]{1,0:T(8,128)S(1)}, u32[]{:S(2)}, u32[]{:S(2)}) collective-permute-start(f32[112,128]{1,0:T(8,128)S(1)} %add.7.own), channel_id=1, source_target_pairs={{0,32},{32,0},{64,96},{96,64},{128,160},{160,128},{192,224},{224,1... | collective-permute-start | bytes 172040 | tf_op jit(solution)/shard_map/ppermute | solution.py:393
